TPU v7x, 32 devices: a whole 2x2x4 slice. The times are simulated.
32 devices in a mesh: pipe: 4 (over x, core), dp: 8 (over z, y).
Axes of the slice: x: 2, y: 2, z: 4, core: 2. Of those that a mesh axis runs over, the one named last changes fastest.
Arguments:
- x_ckpt: bfloat16 [4, 2, 8, 512, 512], P('pipe', None, 'dp'), may hold values from -6 to 6
- top_cot: bfloat16 [2, 8, 512, 512], P(None, 'dp'), may hold values from -6 to 6
- skip_cot: bfloat16 [2, 8, 512, 512], P(None, 'dp'), may hold values from -6 to 6
- w_conv: bfloat16 [4, 512, 3, 1024], P('pipe', 'dp'), may hold values from -0.15625 to 0.15625
- w_mix: bfloat16 [4, 512, 1024], P('pipe', 'dp'), may hold values from -0.25 to 0.25
Outputs:
- cot_inputs: bfloat16 [4, 2, 8, 512, 512], P('pipe', None, 'dp')
- grad_conv: float32 [4, 512, 3, 1024], P('pipe', 'dp')
- grad_mix: float32 [4, 512, 1024], P('pipe', 'dp')
All inputs are finite; a program needn't handle non-finite values.
Results may differ from a plain program's by a relative error of at most 0.014.
Values may be sent and summed in bfloat16 or wider, within the bound.
No kernel may reach another device: no remote copies, remote signals or barrier semaphores. Data moves between devices by JAX's collectives and lax.ppermute only.
A program may use at most 128 MiB of HBM per device.

v0:
```python
import functools

import jax
import jax.numpy as jnp
from jax import lax
from jax.experimental import pallas as pl
from jax.experimental.pallas import tpu as pltpu
from jax.sharding import PartitionSpec as P

F32 = jnp.float32
BF16 = jnp.bfloat16
NT = (((1,), (1,)), ((), ()))
TN = (((0,), (0,)), ((), ()))
VMEM = pl.BlockSpec(memory_space=pltpu.VMEM)
PARAMS = pltpu.CompilerParams(vmem_limit_bytes=24 * 2**20)


def ring_pairs(count):
    order = list(range(0, count, 2)) + list(range(count - 1 - count % 2, 0, -2))
    right = [(order[i], order[(i + 1) % count]) for i in range(count)]
    return right, [(b, a) for a, b in right]


def in_vmem(*arrays):
    return [pltpu.with_memory_space_constraint(array, pltpu.VMEM) for array in arrays]


def cost(flops, moved):
    return pl.CostEstimate(flops=flops, bytes_accessed=moved, transcendentals=0)


def owner_row(replicas, part, offset):
    replica = lax.axis_index("dp")
    step = replica // 2
    place = jnp.where(lax.rem(replica, 2) == 0, step, replicas - 1 - step)
    at = lax.rem(place + (offset + replicas), replicas)
    owner = jnp.where(at < replicas // 2, 2 * at, 2 * (replicas - 1 - at) + 1)
    return pl.multiple_of(owner * part, part)


def split_kernel(conv, mix, low, high, sems):
    copies = [
        pltpu.make_async_copy(conv.at[0:2], low, sems.at[0]),
        pltpu.make_async_copy(conv.at[2], high.at[0], sems.at[1]),
        pltpu.make_async_copy(mix.at[0], high.at[1], sems.at[2]),
    ]
    for copy in copies:
        copy.start()
    for copy in copies:
        copy.wait()


def split_call(conv, mix):
    anywhere = pl.BlockSpec(memory_space=pl.ANY)
    return pl.pallas_call(
        split_kernel,
        out_shape=[pltpu.VMEM((2, *conv.shape[1:]), BF16)] * 2,
        in_specs=[anywhere] * 2,
        out_specs=[VMEM] * 2,
        scratch_shapes=[pltpu.SemaphoreType.DMA((3,))],
        compiler_params=PARAMS,
        cost_estimate=cost(0, 2**20),
    )(*[pltpu.with_memory_space_constraint(array, pltpu.HBM) for array in (conv, mix)])


def prepare_kernel(x, taps_t):
    seqs, samples, channels = x.shape
    dilation = jnp.left_shift(jnp.int32(1), lax.axis_index("pipe"))
    wide = 128
    for s in range(seqs):
        columns = slice(s * samples, (s + 1) * samples)
        for at in range(0, channels, wide):
            turned = x[s, :, at : at + wide].astype(F32).T
            position = lax.broadcasted_iota(jnp.int32, turned.shape, 1)
            taps_t[at : at + wide, columns] = turned.astype(BF16)
            for k in (1, 2):
                delayed = jnp.where(position >= k * dilation, pltpu.roll(turned, k * dilation, 1), 0.0)
                taps_t[k * channels + at : k * channels + at + wide, columns] = delayed.astype(BF16)


def prepare_call(x):
    seqs, samples, channels = x.shape
    return pl.pallas_call(
        prepare_kernel,
        out_shape=pltpu.VMEM((3 * channels, seqs * samples), BF16),
        in_specs=[VMEM],
        out_specs=VMEM,
        compiler_params=PARAMS,
        cost_estimate=cost(2**20, 2**22),
    )(x)


def tap_rows(taps_t, row, part, columns):
    channels = taps_t.shape[0] // 3
    return jnp.concatenate([taps_t[pl.ds(k * channels + row, part), columns] for k in range(3)], axis=0)


def place_rows(replicas, items, blocks):
    part = blocks[0].shape[1]
    return [(owner_row(replicas, part, offset), first, block) for (offset, first), block in zip(items, blocks)]


def shard_term(taps_t, columns, placed):
    channels = taps_t.shape[0] // 3
    part, wide = placed[0][2].shape[1:]
    rows, weights = [], []
    for row, first, block in placed:
        count = min(block.shape[0], 3 - first)
        if count == 0:
            continue
        rows += [taps_t[pl.ds((first + k) * channels + row, part), columns] for k in range(count)]
        weights.append(block[:count].reshape(count * part, wide))
    return lax.dot_general(
        jnp.concatenate(rows, axis=0), jnp.concatenate(weights, axis=0), TN, preferred_element_type=F32
    )


def store_shards(w, placed):
    channels = w.shape[0] // 4
    for row, first, block in placed:
        for k in range(block.shape[0]):
            w[pl.ds((first + k) * channels + row, block.shape[1]), :] = block[k]


def partial_kernel(replicas, items, first, quarters, tokens, taps_t, *refs):
    count = len(items)
    blocks = refs[:count]
    placed = place_rows(replicas, items, blocks)
    refs = refs[count:]
    acc, w, *passed = refs if first else refs[2 + tokens :]
    rows = taps_t.shape[1]
    chunk = min(256, rows)
    for at in range(0, rows, chunk):
        columns = slice(at, at + chunk)
        term = shard_term(taps_t, columns, placed)
        acc[columns, :] = term if first else refs[0][columns, :] + term
    store_shards(w, placed)
    if quarters:
        passed[0][...] = blocks[0][0:1]
        passed[1][...] = blocks[1][1:2]


def partial_call(replicas, items, taps_t, blocks, held, passing=None, tokens=()):
    part, wide = blocks[0].shape[1:]
    rows = taps_t.shape[1]
    count = len(items)
    inputs = in_vmem(taps_t, *blocks, *held, *tokens)
    aliases = {1 + count + i: i for i in range(len(held))}
    if passing == "whole":
        aliases |= {1 + i: 2 + i for i in range(count)}
    return pl.pallas_call(
        functools.partial(partial_kernel, replicas, items, not held, passing == "quarters", len(tokens)),
        out_shape=[pltpu.VMEM((rows, wide), F32), pltpu.VMEM((2 * wide, wide), BF16)]
        + [pltpu.VMEM((2 if passing == "whole" else 1, part, wide), BF16) for _ in blocks if passing],
        in_specs=[VMEM] * len(inputs),
        out_specs=[VMEM] * (2 + count if passing else 2),
        input_output_aliases=aliases,
        compiler_params=PARAMS,
        cost_estimate=cost(3 * rows * part * count * wide, 2**20),
    )(*inputs)


def forward_kernel(replicas, index, store, taps_t, acc, w_in, *refs):
    blocks, refs = refs[:2], refs[2:]
    a1, a2, hid_t = refs[:3]
    samples, channels = a1.shape
    placed = place_rows(replicas, [(replicas // 2, k) for k in (2, 3)], blocks)
    chunk = min(256, samples)
    for at in range(0, samples, chunk):
        columns = slice(index * samples + at, index * samples + at + chunk)
        pre = acc[columns, :] + shard_term(taps_t, columns, placed)
        filt = jnp.tanh(pre[:, :channels])
        gate = jax.nn.sigmoid(pre[:, channels:])
        a1[at : at + chunk, :] = (gate * (1.0 - filt * filt)).astype(BF16)
        a2[at : at + chunk, :] = (filt * gate * (1.0 - gate)).astype(BF16)
        hid_t[:, at : at + chunk] = (filt * gate).T.astype(BF16)
    if store:
        store_shards(refs[3], placed)


def forward_call(replicas, index, micro, store, taps_t, acc, w, blocks):
    rows, wide = acc.shape
    channels = wide // 2
    samples = rows // micro
    inputs = in_vmem(taps_t, acc, w, *blocks)
    return pl.pallas_call(
        functools.partial(forward_kernel, replicas, index, store),
        out_shape=[pltpu.VMEM((samples, channels), BF16)] * 2
        + [pltpu.VMEM((channels, samples), BF16)]
        + ([pltpu.VMEM(w.shape, BF16)] if store else []),
        in_specs=[VMEM] * len(inputs),
        out_specs=[VMEM] * (4 if store else 3),
        input_output_aliases={2: 3} if store else {},
        compiler_params=PARAMS,
        cost_estimate=cost(2**28, 2**22),
    )(*inputs)


def chain_kernel(stage, index, halves, padding, before, held, g, skip, a1, a2, w, *refs):
    bt = refs[-1]
    carried = refs[0] if halves == (0,) else None
    pg, ig, gk, *extra = refs[before + held : -1]
    samples, channels = gk.shape
    chunk = samples // 2
    base = min(halves) * chunk
    count = len(halves) * chunk
    dilation = 2**stage
    g_base = base if g.shape[0] == samples else 0

    @pl.when(lax.axis_index("pipe") == stage)
    def _():
        for k in (1, 2):
            bt[k, count:, :] = jnp.zeros((padding, channels), F32) if carried is None else carried[k - 1]
        for half in halves:
            at = half * chunk
            rows = slice(at, at + chunk)
            here = slice(at - base, at - base + chunk)
            g_rows = slice(at - base + g_base, at - base + g_base + chunk)
            hid = lax.dot_general(
                g[g_rows, :], w[3 * channels :, :channels], NT, preferred_element_type=F32
            ) + lax.dot_general(
                skip[index, rows, :], w[3 * channels :, channels:], NT, preferred_element_type=F32
            )
            pg[rows, :channels] = (hid * a1[rows, :].astype(F32)).astype(BF16)
            pg[rows, channels:] = (hid * a2[rows, :].astype(F32)).astype(BF16)
            for k in range(3):
                bt[k, here, :] = lax.dot_general(
                    pg[rows, :], w[k * channels : (k + 1) * channels, :], NT, preferred_element_type=F32
                )
            piece = 64
            for first in range(at - base + chunk - piece, at - base - 1, -piece):
                last = first + piece
                total = g[first + g_base : last + g_base, :].astype(F32) + bt[0, first:last, :]
                total = total + bt[1, first + dilation : last + dilation, :]
                total = total + bt[2, first + 2 * dilation : last + 2 * dilation, :]
                ig[first + base : last + base, :] = total.astype(BF16)
                if len(halves) == 1 and stage:
                    extra[0][first:last, :] = total.astype(BF16)
            gk[rows, :] = g[g_rows, :]
        if halves == (1,):
            for k in (1, 2):
                extra[-1][k - 1] = bt[k, :padding, :]


def chain_call(stage, index, halves, padding, g, skip, a1, a2, w, carried, held):
    samples, channels = a1.shape
    chunk = samples // 2
    tile = pltpu.VMEM((samples, channels), BF16)
    outs = [pltpu.VMEM((samples, 2 * channels), BF16), tile, tile]
    if len(halves) == 1 and stage:
        outs.append(pltpu.VMEM((chunk, channels), BF16))
    if halves == (1,):
        outs.append(pltpu.VMEM((2, padding, channels), F32))
    inputs = in_vmem(g, skip, a1, a2, w, *carried, *held)
    return pl.pallas_call(
        functools.partial(chain_kernel, stage, index, halves, padding, len(carried), len(held)),
        out_shape=outs,
        in_specs=[VMEM] * len(inputs),
        out_specs=[VMEM] * len(outs),
        scratch_shapes=[pltpu.VMEM((3, len(halves) * chunk + padding, channels), F32)],
        input_output_aliases={len(inputs) - len(held) + i: i for i in range(len(held))},
        compiler_params=PARAMS,
        cost_estimate=cost(8 * len(halves) * chunk * channels * channels, 2**22),
    )(*inputs)


def term_kernel(replicas, offsets, micro, taps_t, skip, *refs):
    hids, refs = refs[:micro], refs[micro:]
    pgs, refs = refs[:micro], refs[micro:]
    gs, refs = refs[:micro], refs[micro:]
    outs = refs[-2 * len(offsets) :]
    samples, wide = pgs[0].shape
    channels = wide // 2
    part = channels // replicas
    places = [owner_row(replicas, part, offset) for offset in offsets]
    step = min(256, channels)

    def product(rows_of, right, columns):
        total = None
        for m in range(micro):
            new = jnp.dot(rows_of(m), right(m, columns), preferred_element_type=F32)
            total = new if total is None else total + new
        return total

    def conv_rows(m):
        here = slice(m * samples, (m + 1) * samples)
        return jnp.concatenate([tap_rows(taps_t, row, part, here) for row in places], axis=0)

    def mix_rows(m):
        return jnp.concatenate([hids[m][pl.ds(row, part), :] for row in places], axis=0)

    @pl.loop(0, wide // step)
    def _(j):
        columns = pl.ds(pl.multiple_of(j * step, step), step)
        conv = product(conv_rows, lambda m, at: pgs[m][:, at], columns)
        for slot in range(len(offsets)):
            low, high = outs[2 * slot : 2 * slot + 2]
            for k, (target, index) in enumerate(((low, 0), (low, 1), (high, 0))):
                at = (slot * 3 + k) * part
                target[index, :, columns] = conv[at : at + part, :].astype(low.dtype)

    @pl.loop(0, channels // step)
    def _(j):
        columns = pl.ds(pl.multiple_of(j * step, step), step)
        after = pl.ds(pl.multiple_of(channels + j * step, step), step)
        mix_g = product(mix_rows, lambda m, at: gs[m][:, at], columns)
        mix_s = product(mix_rows, lambda m, at: skip[m, :, at], columns)
        for slot in range(len(offsets)):
            high = outs[2 * slot + 1]
            here = slice(slot * part, (slot + 1) * part)
            high[1, :, columns] = mix_g[here, :].astype(high.dtype)
            high[1, :, after] = mix_s[here, :].astype(high.dtype)


def term_call(replicas, offsets, kind, taps_t, skip, hid_t, pre_grads, gs, tokens):
    micro, samples, channels = skip.shape
    part = channels // replicas
    inputs = in_vmem(taps_t, skip, *hid_t, *pre_grads, *gs, *tokens)
    outs = 2 * len(offsets)
    return pl.pallas_call(
        functools.partial(term_kernel, replicas, offsets, micro),
        out_shape=[pltpu.VMEM((2, part, 2 * channels), kind)] * outs,
        in_specs=[VMEM] * len(inputs),
        out_specs=[VMEM] * outs,
        compiler_params=PARAMS,
        cost_estimate=cost(2**29 * len(offsets), 2**20),
    )(*inputs)


def add_kernel(mine_r, mine_l, got_r, got_l, *refs):
    out_r, out_l = refs[-2:]
    out_r[...] = (mine_r[...].astype(F32) + got_r[...].astype(F32)).astype(BF16)
    out_l[...] = (mine_l[...].astype(F32) + got_l[...].astype(F32)).astype(BF16)


def add_call(mine, got, tokens):
    inputs = in_vmem(*mine, *got, *tokens)
    return pl.pallas_call(
        add_kernel,
        out_shape=[pltpu.VMEM(got[0].shape, BF16)] * 2,
        in_specs=[VMEM] * len(inputs),
        out_specs=[VMEM] * 2,
        compiler_params=PARAMS,
        cost_estimate=cost(2**18, 2**19),
    )(*inputs)


def final_kernel(low, high, low_r, low_l, high_r, high_l, conv, mix):
    conv[0:2] = low[...] + (low_r[...].astype(F32) + low_l[...].astype(F32))
    total = high[...] + (high_r[...].astype(F32) + high_l[...].astype(F32))
    conv[2] = total[0]
    mix[...] = total[1]


def final_call(*blocks):
    part, wide = blocks[0].shape[1:]
    return pl.pallas_call(
        final_kernel,
        out_shape=[jax.ShapeDtypeStruct((3, part, wide), F32), jax.ShapeDtypeStruct((part, wide), F32)],
        in_specs=[VMEM] * 6,
        out_specs=[VMEM] * 2,
        compiler_params=PARAMS,
        cost_estimate=cost(2**19, 2**20),
    )(*in_vmem(*blocks))


def local(x_ckpt, top_cot, skip_cot, w_conv, w_mix):
    sections = lax.axis_size("pipe")
    replicas = lax.axis_size("dp")
    micro, seqs, samples, channels = x_ckpt.shape[1:]
    block = seqs * samples
    half = replicas // 2
    right, left = ring_pairs(replicas)

    def send(to_right, to_left):
        return lax.ppermute(to_right, "dp", right), lax.ppermute(to_left, "dp", left)

    taps_t = prepare_call(x_ckpt[0].reshape(micro * seqs, samples, channels))
    low, high = split_call(w_conv[0].transpose(1, 0, 2), w_mix)
    streams = {0: (low, low), 2: (high, high)}
    held = partial_call(replicas, ((0, 0), (0, 2)), taps_t, [low, high], [])
    skip = skip_cot.reshape(micro, block, channels)
    for step in range(1, half):
        last = step == half - 1
        for first, (to_right, to_left) in streams.items():
            got = send(to_right, to_left)
            items = ((-step, first), (step, first))
            if last and first:
                blocks = send(got[0][:1], got[1][1:])
                items += ((half, 0), (half, 1))
                held = partial_call(replicas, items, taps_t, [*got, *ahead], held, None, (skip,))
                continue
            passing = "quarters" if last else "whole"
            *held, to_right, to_left = partial_call(replicas, items, taps_t, got, held, passing)
            streams[first] = (to_right, to_left)
            if last:
                ahead = send(to_right, to_left)
    acc, w_full = held

    g = list(top_cot.reshape(micro, block, channels))
    padding = max(16, 2 * 2 ** (sections - 1))
    hid_t, held, ready = [], [()] * micro, []
    for m in range(micro):
        a1, a2, hid, *stored = forward_call(
            replicas, m, micro, m == 0, taps_t, acc, w_full, blocks
        )
        if stored:
            w_full = stored[0]
        hid_t.append(hid)
        ready.append((a1, a2))
    last = sections - 1
    g = [[piece, piece] for piece in g]
    for m in range(micro):
        held[m] = chain_call(last, m, (1, 0), padding, g[m][0], skip, *ready[m], w_full, (), ())
        g[m] = [lax.ppermute(held[m][1], "pipe", [(last, last - 1)])] * 2
    for stage in range(last - 1, -1, -1):
        piece = None
        for m in range(micro):
            carried = () if piece is None else (piece,)
            for half_at in (1, 0):
                out = chain_call(
                    stage, m, (half_at,), padding, g[m][half_at], skip, *ready[m], w_full, carried, held[m]
                )
                held[m], carried = out[:3], out[-1:]
                piece = out[3] if stage else out[1]
                if stage:
                    g[m][half_at] = lax.ppermute(piece, "pipe", [(stage, stage - 1)])
    pre_grads, cots, gs = zip(*held)
    cot = jnp.stack(cots, axis=0)

    def terms(dist, tokens, kind=BF16):
        offsets = (dist,) if dist in (0, half) else (dist, -dist)
        return term_call(replicas, offsets, kind, taps_t, skip, hid_t, pre_grads, gs, tokens)

    low, high = terms(half, ())
    got_one = send(low, high)
    mine = terms(half - 1, (low,))
    got_two = send(mine[1], mine[2])
    token = ()
    for dist in range(half - 1, 0, -1):
        if dist < half - 1:
            out = add_call((mine[1], mine[2]), got_two, token)
            token = out[:1]
            got_two = send(*out)
        out = add_call((mine[0], mine[3]), got_one, token)
        token = out[:1]
        got_one = send(*out)
        if dist > 1:
            mine = terms(dist - 1, token)
    low, high = terms(0, token, F32)
    share_conv, share_mix = final_call(low, high, got_one[0], got_two[1], got_two[0], got_one[1])
    return (
        cot.reshape(1, micro, seqs, samples, channels),
        share_conv.transpose(1, 0, 2)[None],
        share_mix[None],
    )


def solution(mesh):
    placed = (
        P("pipe", None, "dp", None, None),
        P(None, "dp", None, None),
        P(None, "dp", None, None),
        P("pipe", "dp", None, None),
        P("pipe", "dp", None),
    )
    return jax.shard_map(
        local,
        mesh=mesh,
        in_specs=placed,
        out_specs=(
            P("pipe", None, "dp", None, None),
            P("pipe", "dp", None, None),
            P("pipe", "dp", None),
        ),
        check_vma=False,
    )
```

profile of v0, /device:TPU:0, one launch (start us, length us, event | category | flops | bytes accessed | tf_op | source)
XLA Modules:
  0.0 120.4 jit_solution(14173967703658653625)
XLA Ops:
  1.7 3.1 %collective-permute-start.2 = (bf16[2,64,1024]{2,1,0:T(8,128)(2,1)S(1)}, bf16[2,64,1024]{2,1,0:T(8,128)(2,1)S(1)}, u32[]{:S(2)}, u32[]{:S(2)}) collective-permute-start(bf16[2,64,1024]{2,1,0:T(8,128)(2,1)S(1)} %get-tuple-element.121.refs_0_), channel_id=1, source_target_pairs={{0,2},{2,4},{4,6},{6,7},{7,5},{5,3},{3,1},{1,0},{8,10},{10,12},{12... | collective-permute-start | bytes 786440 | tf_op jit(solution)/shard_map/ppermute | solution.py:376
  4.8 2.0 %collective-permute-start = (bf16[2,64,1024]{2,1,0:T(8,128)(2,1)S(1)}, bf16[2,64,1024]{2,1,0:T(8,128)(2,1)S(1)}, u32[]{:S(2)}, u32[]{:S(2)}) collective-permute-start(bf16[2,64,1024]{2,1,0:T(8,128)(2,1)S(1)} %get-tuple-element.120.refs_1_), channel_id=1, source_target_pairs={{0,2},{2,4},{4,6},{6,7},{7,5},{5,3},{3,1},{1,0},{8,10},{10,12},{12... | collective-permute-start | bytes 786440 | tf_op jit(solution)/shard_map/ppermute | solution.py:376
  10.2 1.7 %collective-permute-done.2.refs_0_ = bf16[2,64,1024]{2,1,0:T(8,128)(2,1)S(1)} collective-permute-done((bf16[2,64,1024]{2,1,0:T(8,128)(2,1)S(1)}, bf16[2,64,1024]{2,1,0:T(8,128)(2,1)S(1)}, u32[]{:S(2)}, u32[]{:S(2)}) %collective-permute-start.2) | collective-permute-done | bytes 262176 | tf_op jit(solution)/shard_map/ppermute | solution.py:376
  11.9 2.2 %collective-permute-done.3.refs_1_ = bf16[2,64,1024]{2,1,0:T(8,128)(2,1)S(1)} collective-permute-done((bf16[2,64,1024]{2,1,0:T(8,128)(2,1)S(1)}, bf16[2,64,1024]{2,1,0:T(8,128)(2,1)S(1)}, u32[]{:S(2)}, u32[]{:S(2)}) %collective-permute-start.3) | collective-permute-done | bytes 262176 | tf_op jit(solution)/shard_map/ppermute | solution.py:376
  15.0 1.6 %collective-permute-start.6 = (bf16[2,64,1024]{2,1,0:T(8,128)(2,1)S(1)}, bf16[2,64,1024]{2,1,0:T(8,128)(2,1)S(1)}, u32[]{:S(2)}, u32[]{:S(2)}) collective-permute-start(bf16[2,64,1024]{2,1,0:T(8,128)(2,1)S(1)} %get-tuple-element.128), channel_id=1, source_target_pairs={{0,2},{2,4},{4,6},{6,7},{7,5},{5,3},{3,1},{1,0},{8,10},{10,12},{12... | collective-permute-start | bytes 786440 | tf_op jit(solution)/shard_map/ppermute | solution.py:376
  17.5 2.2 %collective-permute-done.1.refs_1_ = bf16[2,64,1024]{2,1,0:T(8,128)(2,1)S(1)} collective-permute-done((bf16[2,64,1024]{2,1,0:T(8,128)(2,1)S(1)}, bf16[2,64,1024]{2,1,0:T(8,128)(2,1)S(1)}, u32[]{:S(2)}, u32[]{:S(2)}) %collective-permute-start.1) | collective-permute-done | bytes 262176 | tf_op jit(solution)/shard_map/ppermute | solution.py:376
  20.6 1.6 %collective-permute-start.4 = (bf16[2,64,1024]{2,1,0:T(8,128)(2,1)S(1)}, bf16[2,64,1024]{2,1,0:T(8,128)(2,1)S(1)}, u32[]{:S(2)}, u32[]{:S(2)}) collective-permute-start(bf16[2,64,1024]{2,1,0:T(8,128)(2,1)S(1)} %get-tuple-element.126), channel_id=1, source_target_pairs={{0,2},{2,4},{4,6},{6,7},{7,5},{5,3},{3,1},{1,0},{8,10},{10,12},{12... | collective-permute-start | bytes 786440 | tf_op jit(solution)/shard_map/ppermute | solution.py:376
  24.1 1.7 %collective-permute-done.7.refs_1_ = bf16[2,64,1024]{2,1,0:T(8,128)(2,1)S(1)} collective-permute-done((bf16[2,64,1024]{2,1,0:T(8,128)(2,1)S(1)}, bf16[2,64,1024]{2,1,0:T(8,128)(2,1)S(1)}, u32[]{:S(2)}, u32[]{:S(2)}) %collective-permute-start.7) | collective-permute-done | bytes 262176 | tf_op jit(solution)/shard_map/ppermute | solution.py:376
  26.8 1.6 %collective-permute-start.10 = (bf16[2,64,1024]{2,1,0:T(8,128)(2,1)S(1)}, bf16[2,64,1024]{2,1,0:T(8,128)(2,1)S(1)}, u32[]{:S(2)}, u32[]{:S(2)}) collective-permute-start(bf16[2,64,1024]{2,1,0:T(8,128)(2,1)S(1)} %get-tuple-element.136), channel_id=1, source_target_pairs={{0,2},{2,4},{4,6},{6,7},{7,5},{5,3},{3,1},{1,0},{8,10},{10,12},{12... | collective-permute-start | bytes 786440 | tf_op jit(solution)/shard_map/ppermute | solution.py:376
  29.9 1.5 %collective-permute-done.5.refs_1_ = bf16[2,64,1024]{2,1,0:T(8,128)(2,1)S(1)} collective-permute-done((bf16[2,64,1024]{2,1,0:T(8,128)(2,1)S(1)}, bf16[2,64,1024]{2,1,0:T(8,128)(2,1)S(1)}, u32[]{:S(2)}, u32[]{:S(2)}) %collective-permute-start.5) | collective-permute-done | bytes 262176 | tf_op jit(solution)/shard_map/ppermute | solution.py:376
  32.4 1.6 %collective-permute-start.8 = (bf16[2,64,1024]{2,1,0:T(8,128)(2,1)S(1)}, bf16[2,64,1024]{2,1,0:T(8,128)(2,1)S(1)}, u32[]{:S(2)}, u32[]{:S(2)}) collective-permute-start(bf16[2,64,1024]{2,1,0:T(8,128)(2,1)S(1)} %get-tuple-element.134), channel_id=1, source_target_pairs={{0,2},{2,4},{4,6},{6,7},{7,5},{5,3},{3,1},{1,0},{8,10},{10,12},{12... | collective-permute-start | bytes 786440 | tf_op jit(solution)/shard_map/ppermute | solution.py:376
  35.9 1.7 %collective-permute-done.11.refs_1_ = bf16[2,64,1024]{2,1,0:T(8,128)(2,1)S(1)} collective-permute-done((bf16[2,64,1024]{2,1,0:T(8,128)(2,1)S(1)}, bf16[2,64,1024]{2,1,0:T(8,128)(2,1)S(1)}, u32[]{:S(2)}, u32[]{:S(2)}) %collective-permute-start.11) | collective-permute-done | bytes 262176 | tf_op jit(solution)/shard_map/ppermute | solution.py:376
  40.8 2.5 %collective-permute-start.14 = (bf16[1,64,1024]{2,1,0:T(8,128)(2,1)S(1)}, bf16[1,64,1024]{2,1,0:T(8,128)(2,1)S(1)}, u32[]{:S(2)}, u32[]{:S(2)}) collective-permute-start(bf16[1,64,1024]{2,1,0:T(8,128)(2,1)S(1)} %slice.10), channel_id=1, source_target_pairs={{0,2},{2,4},{4,6},{6,7},{7,5},{5,3},{3,1},{1,0},{8,10},{10,12},{12... | collective-permute-start | bytes 393224 | tf_op jit(solution)/shard_map/ppermute | solution.py:376
  46.0 2.4 %collective-permute-done.15.refs_1_ = bf16[1,64,1024]{2,1,0:T(8,128)(2,1)S(1)} collective-permute-done((bf16[1,64,1024]{2,1,0:T(8,128)(2,1)S(1)}, bf16[1,64,1024]{2,1,0:T(8,128)(2,1)S(1)}, u32[]{:S(2)}, u32[]{:S(2)}) %collective-permute-start.15) | collective-permute-done | bytes 131104 | tf_op jit(solution)/shard_map/ppermute | solution.py:376
  57.3 1.5 %collective-permute-start.25 = (bf16[256,512]{1,0:T(8,128)(2,1)S(1)}, bf16[256,512]{1,0:T(8,128)(2,1)S(1)}, u32[]{:S(2)}, u32[]{:S(2)}) collective-permute-start(bf16[256,512]{1,0:T(8,128)(2,1)S(1)} %get-tuple-element.194), channel_id=1, source_target_pairs={{8,0},{9,1},{10,2},{11,3},{12,4},{13,5},{14,6},{15,7}} | collective-permute-start | bytes 786440 | tf_op jit(solution)/shard_map/ppermute | solution.py:427
  60.2 5.1 %collective-permute-done.20.g = bf16[256,512]{1,0:T(8,128)(2,1)S(1)} collective-permute-done((bf16[256,512]{1,0:T(8,128)(2,1)S(1)}, bf16[256,512]{1,0:T(8,128)(2,1)S(1)}, u32[]{:S(2)}, u32[]{:S(2)}) %collective-permute-start.20) | collective-permute-done | bytes 262176 | tf_op jit(solution)/shard_map/ppermute | solution.py:427
  65.3 1.5 %shard_map.91 = (bf16[512,1024]{1,0:T(8,128)(2,1)S(1)}, bf16[512,512]{1,0:T(8,128)(2,1)S(1)}, bf16[512,512]{1,0:T(8,128)(2,1)S(1)}, f32[2,16,512]{2,1,0:T(8,128)S(1)}) custom-call(bf16[256,512]{1,0:T(8,128)(2,1)S(1)} %collective-permute-done.20.g, bf16[2,512,512]{2,1,0:T(8,128)(2,1)S(1)} %bitcast.30, ...), custom_call_target="tpu_custom_call", output_to_operand_aliasing={{0}: (5, {}), {1}: (6, {}), {2}: (7, {})} | custom-call | flops 536870912 | bytes 4194304 | tf_op jit(solution)/shard_map/pallas_call | solution.py:255
  68.2 1.5 %shard_map.92 = (bf16[512,1024]{1,0:T(8,128)(2,1)S(1)}, bf16[512,512]{1,0:T(8,128)(2,1)S(1)}, bf16[512,512]{1,0:T(8,128)(2,1)S(1)}) custom-call(bf16[256,512]{1,0:T(8,128)(2,1)S(1)} %collective-permute-done.19.g, bf16[2,512,512]{2,1,0:T(8,128)(2,1)S(1)} %bitcast.31, ...), custom_call_target="tpu_custom_call", output_to_operand_aliasing={{0}: (6, {}), {1}: (7, {}), {2}: (8, {})} | custom-call | flops 536870912 | bytes 4194304 | tf_op jit(solution)/shard_map/pallas_call | solution.py:255
  72.5 1.6 %collective-permute-done.24.g = bf16[256,512]{1,0:T(8,128)(2,1)S(1)} collective-permute-done((bf16[256,512]{1,0:T(8,128)(2,1)S(1)}, bf16[256,512]{1,0:T(8,128)(2,1)S(1)}, u32[]{:S(2)}, u32[]{:S(2)}) %collective-permute-start.24) | collective-permute-done | bytes 262176 | tf_op jit(solution)/shard_map/ppermute | solution.py:427
  74.1 1.5 %shard_map.100 = (bf16[512,1024]{1,0:T(8,128)(2,1)S(1)}, bf16[512,512]{1,0:T(8,128)(2,1)S(1)}, bf16[512,512]{1,0:T(8,128)(2,1)S(1)}) custom-call(bf16[256,512]{1,0:T(8,128)(2,1)S(1)} %collective-permute-done.24.g, bf16[2,512,512]{2,1,0:T(8,128)(2,1)S(1)} %bitcast.33, ...), custom_call_target="tpu_custom_call", output_to_operand_aliasing={{0}: (6, {}), {1}: (7, {}), {2}: (8, {})} | custom-call | flops 536870912 | bytes 4194304 | tf_op jit(solution)/shard_map/pallas_call | solution.py:255
  75.6 1.8 %shard_map.101 = (bf16[2,64,1024]{2,1,0:T(8,128)(2,1)S(1)}, bf16[2,64,1024]{2,1,0:T(8,128)(2,1)S(1)}) custom-call(bf16[1536,1024]{1,0:T(8,128)(2,1)S(1)} %shard_map.76.taps_t, bf16[2,512,512]{2,1,0:T(8,128)(2,1)S(1)} %bitcast.34, bf16[512,512]{1,0:T(8,128)(2,1)S(1)} %get-tuple-element.203.refs_0_, bf16[512,512]{1,0:T(8,128)(2,1)S(1)} %get-tuple-element.204.refs_1_, ...), custom_call_target="tpu_custom_call" | custom-call | flops 536870912 | bytes 1048576 | tf_op jit(solution)/shard_map/pallas_call | solution.py:320
  77.4 1.7 %collective-permute-start.26 = (bf16[2,64,1024]{2,1,0:T(8,128)(2,1)S(1)}, bf16[2,64,1024]{2,1,0:T(8,128)(2,1)S(1)}, u32[]{:S(2)}, u32[]{:S(2)}) collective-permute-start(bf16[2,64,1024]{2,1,0:T(8,128)(2,1)S(1)} %get-tuple-element.209.refs_6_), channel_id=1, source_target_pairs={{0,2},{2,4},{4,6},{6,7},{7,5},{5,3},{3,1},{1,0},{8,10},{10,12},{12... | collective-permute-start | bytes 786440 | tf_op jit(solution)/shard_map/ppermute | solution.py:376
  79.5 2.2 %shard_map.102 = (bf16[2,64,1024]{2,1,0:T(8,128)(2,1)S(1)}, bf16[2,64,1024]{2,1,0:T(8,128)(2,1)S(1)}, bf16[2,64,1024]{2,1,0:T(8,128)(2,1)S(1)}, bf16[2,64,1024]{2,1,0:T(8,128)(2,1)S(1)}) custom-call(bf16[1536,1024]{1,0:T(8,128)(2,1)S(1)} %shard_map.76.taps_t, bf16[2,512,512]{2,1,0:T(8,128)(2,1)S(1)} %bitcast.35, ...), custom_call_target="tpu_custom_call" | custom-call | flops 1073741824 | bytes 1048576 | tf_op jit(solution)/shard_map/pallas_call | solution.py:320
  81.6 1.7 %collective-permute-start.30 = (bf16[2,64,1024]{2,1,0:T(8,128)(2,1)S(1)}, bf16[2,64,1024]{2,1,0:T(8,128)(2,1)S(1)}, u32[]{:S(2)}, u32[]{:S(2)}) collective-permute-start(bf16[2,64,1024]{2,1,0:T(8,128)(2,1)S(1)} %get-tuple-element.219), channel_id=1, source_target_pairs={{0,2},{2,4},{4,6},{6,7},{7,5},{5,3},{3,1},{1,0},{8,10},{10,12},{12... | collective-permute-start | bytes 786440 | tf_op jit(solution)/shard_map/ppermute | solution.py:376
  83.7 2.4 %collective-permute-done.26.got_r = bf16[2,64,1024]{2,1,0:T(8,128)(2,1)S(1)} collective-permute-done((bf16[2,64,1024]{2,1,0:T(8,128)(2,1)S(1)}, bf16[2,64,1024]{2,1,0:T(8,128)(2,1)S(1)}, u32[]{:S(2)}, u32[]{:S(2)}) %collective-permute-start.26) | collective-permute-done | bytes 262176 | tf_op jit(solution)/shard_map/ppermute | solution.py:376
  89.7 2.2 %shard_map.104 = (bf16[2,64,1024]{2,1,0:T(8,128)(2,1)S(1)}, bf16[2,64,1024]{2,1,0:T(8,128)(2,1)S(1)}, bf16[2,64,1024]{2,1,0:T(8,128)(2,1)S(1)}, bf16[2,64,1024]{2,1,0:T(8,128)(2,1)S(1)}) custom-call(bf16[1536,1024]{1,0:T(8,128)(2,1)S(1)} %shard_map.76.taps_t, bf16[2,512,512]{2,1,0:T(8,128)(2,1)S(1)} %bitcast.36, ...), custom_call_target="tpu_custom_call" | custom-call | flops 1073741824 | bytes 1048576 | tf_op jit(solution)/shard_map/pallas_call | solution.py:320
  95.4 2.0 %collective-permute-done.28.got_r = bf16[2,64,1024]{2,1,0:T(8,128)(2,1)S(1)} collective-permute-done((bf16[2,64,1024]{2,1,0:T(8,128)(2,1)S(1)}, bf16[2,64,1024]{2,1,0:T(8,128)(2,1)S(1)}, u32[]{:S(2)}, u32[]{:S(2)}) %collective-permute-start.28) | collective-permute-done | bytes 262176 | tf_op jit(solution)/shard_map/ppermute | solution.py:376
  101.0 2.2 %shard_map.107 = (bf16[2,64,1024]{2,1,0:T(8,128)(2,1)S(1)}, bf16[2,64,1024]{2,1,0:T(8,128)(2,1)S(1)}, bf16[2,64,1024]{2,1,0:T(8,128)(2,1)S(1)}, bf16[2,64,1024]{2,1,0:T(8,128)(2,1)S(1)}) custom-call(bf16[1536,1024]{1,0:T(8,128)(2,1)S(1)} %shard_map.76.taps_t, bf16[2,512,512]{2,1,0:T(8,128)(2,1)S(1)} %bitcast.37, ...), custom_call_target="tpu_custom_call" | custom-call | flops 1073741824 | bytes 1048576 | tf_op jit(solution)/shard_map/pallas_call | solution.py:320
  105.0 1.6 %collective-permute-start.38 = (bf16[2,64,1024]{2,1,0:T(8,128)(2,1)S(1)}, bf16[2,64,1024]{2,1,0:T(8,128)(2,1)S(1)}, u32[]{:S(2)}, u32[]{:S(2)}) collective-permute-start(bf16[2,64,1024]{2,1,0:T(8,128)(2,1)S(1)} %get-tuple-element.229.refs_0_), channel_id=1, source_target_pairs={{0,2},{2,4},{4,6},{6,7},{7,5},{5,3},{3,1},{1,0},{8,10},{10,12},{12... | collective-permute-start | bytes 786440 | tf_op jit(solution)/shard_map/ppermute | solution.py:376
  106.6 2.0 %collective-permute-done.32.got_r = bf16[2,64,1024]{2,1,0:T(8,128)(2,1)S(1)} collective-permute-done((bf16[2,64,1024]{2,1,0:T(8,128)(2,1)S(1)}, bf16[2,64,1024]{2,1,0:T(8,128)(2,1)S(1)}, u32[]{:S(2)}, u32[]{:S(2)}) %collective-permute-start.32) | collective-permute-done | bytes 262176 | tf_op jit(solution)/shard_map/ppermute | solution.py:376
  113.3 1.7 %shard_map.110 = (f32[2,64,1024]{2,1,0:T(8,128)S(1)}, f32[2,64,1024]{2,1,0:T(8,128)S(1)}) custom-call(bf16[1536,1024]{1,0:T(8,128)(2,1)S(1)} %shard_map.76.taps_t, bf16[2,512,512]{2,1,0:T(8,128)(2,1)S(1)} %bitcast.38, bf16[512,512]{1,0:T(8,128)(2,1)S(1)} %get-tuple-element.203.refs_0_, bf16[512,512]{1,0:T(8,128)(2,1)S(1)} %get-tuple-element.204.refs_1_, ...), custom_call_target="tpu_custom_call" | custom-call | flops 536870912 | bytes 1048576 | tf_op jit(solution)/shard_map/pallas_call | solution.py:320
  115.6 2.3 %collective-permute-done.36.low_r = bf16[2,64,1024]{2,1,0:T(8,128)(2,1)S(1)} collective-permute-done((bf16[2,64,1024]{2,1,0:T(8,128)(2,1)S(1)}, bf16[2,64,1024]{2,1,0:T(8,128)(2,1)S(1)}, u32[]{:S(2)}, u32[]{:S(2)}) %collective-permute-start.36) | collective-permute-done | bytes 262176 | tf_op jit(solution)/shard_map/ppermute | solution.py:376
  (94 shorter events, 55.3 us)
Async XLA Ops:
  1.7 10.2 %collective-permute-start.2 = (bf16[2,64,1024]{2,1,0:T(8,128)(2,1)S(1)}, bf16[2,64,1024]{2,1,0:T(8,128)(2,1)S(1)}, u32[]{:S(2)}, u32[]{:S(2)}) collective-permute-start(bf16[2,64,1024]{2,1,0:T(8,128)(2,1)S(1)} %get-tuple-element.121.refs_0_), channel_id=1, source_target_pairs={{0,2},{2,4},{4,6},{6,7},{7,5},{5,3},{3,1},{1,0},{8,10},{10,12},{12... | collective-permute-start | bytes 786440 | tf_op jit(solution)/shard_map/ppermute | solution.py:376
  4.8 9.2 %collective-permute-start.3 = (bf16[2,64,1024]{2,1,0:T(8,128)(2,1)S(1)}, bf16[2,64,1024]{2,1,0:T(8,128)(2,1)S(1)}, u32[]{:S(2)}, u32[]{:S(2)}) collective-permute-start(bf16[2,64,1024]{2,1,0:T(8,128)(2,1)S(1)} %get-tuple-element.121.refs_0_), channel_id=1, source_target_pairs={{2,0},{4,2},{6,4},{7,6},{5,7},{3,5},{1,3},{0,1},{10,8},{12,10},{14... | collective-permute-start | bytes 786440 | tf_op jit(solution)/shard_map/ppermute | solution.py:376
  4.8 12.7 %collective-permute-start = (bf16[2,64,1024]{2,1,0:T(8,128)(2,1)S(1)}, bf16[2,64,1024]{2,1,0:T(8,128)(2,1)S(1)}, u32[]{:S(2)}, u32[]{:S(2)}) collective-permute-start(bf16[2,64,1024]{2,1,0:T(8,128)(2,1)S(1)} %get-tuple-element.120.refs_1_), channel_id=1, source_target_pairs={{0,2},{2,4},{4,6},{6,7},{7,5},{5,3},{3,1},{1,0},{8,10},{10,12},{12... | collective-permute-start | bytes 786440 | tf_op jit(solution)/shard_map/ppermute | solution.py:376
  6.8 12.8 %collective-permute-start.1 = (bf16[2,64,1024]{2,1,0:T(8,128)(2,1)S(1)}, bf16[2,64,1024]{2,1,0:T(8,128)(2,1)S(1)}, u32[]{:S(2)}, u32[]{:S(2)}) collective-permute-start(bf16[2,64,1024]{2,1,0:T(8,128)(2,1)S(1)} %get-tuple-element.120.refs_1_), channel_id=1, source_target_pairs={{2,0},{4,2},{6,4},{7,6},{5,7},{3,5},{1,3},{0,1},{10,8},{12,10},{14... | collective-permute-start | bytes 786440 | tf_op jit(solution)/shard_map/ppermute | solution.py:376
  15.0 9.0 %collective-permute-start.6 = (bf16[2,64,1024]{2,1,0:T(8,128)(2,1)S(1)}, bf16[2,64,1024]{2,1,0:T(8,128)(2,1)S(1)}, u32[]{:S(2)}, u32[]{:S(2)}) collective-permute-start(bf16[2,64,1024]{2,1,0:T(8,128)(2,1)S(1)} %get-tuple-element.128), channel_id=1, source_target_pairs={{0,2},{2,4},{4,6},{6,7},{7,5},{5,3},{3,1},{1,0},{8,10},{10,12},{12... | collective-permute-start | bytes 786440 | tf_op jit(solution)/shard_map/ppermute | solution.py:376
  16.6 9.2 %collective-permute-start.7 = (bf16[2,64,1024]{2,1,0:T(8,128)(2,1)S(1)}, bf16[2,64,1024]{2,1,0:T(8,128)(2,1)S(1)}, u32[]{:S(2)}, u32[]{:S(2)}) collective-permute-start(bf16[2,64,1024]{2,1,0:T(8,128)(2,1)S(1)} %get-tuple-element.129), channel_id=1, source_target_pairs={{2,0},{4,2},{6,4},{7,6},{5,7},{3,5},{1,3},{0,1},{10,8},{12,10},{14... | collective-permute-start | bytes 786440 | tf_op jit(solution)/shard_map/ppermute | solution.py:376
  20.6 9.3 %collective-permute-start.4 = (bf16[2,64,1024]{2,1,0:T(8,128)(2,1)S(1)}, bf16[2,64,1024]{2,1,0:T(8,128)(2,1)S(1)}, u32[]{:S(2)}, u32[]{:S(2)}) collective-permute-start(bf16[2,64,1024]{2,1,0:T(8,128)(2,1)S(1)} %get-tuple-element.126), channel_id=1, source_target_pairs={{0,2},{2,4},{4,6},{6,7},{7,5},{5,3},{3,1},{1,0},{8,10},{10,12},{12... | collective-permute-start | bytes 786440 | tf_op jit(solution)/shard_map/ppermute | solution.py:376
  22.2 9.2 %collective-permute-start.5 = (bf16[2,64,1024]{2,1,0:T(8,128)(2,1)S(1)}, bf16[2,64,1024]{2,1,0:T(8,128)(2,1)S(1)}, u32[]{:S(2)}, u32[]{:S(2)}) collective-permute-start(bf16[2,64,1024]{2,1,0:T(8,128)(2,1)S(1)} %get-tuple-element.127), channel_id=1, source_target_pairs={{2,0},{4,2},{6,4},{7,6},{5,7},{3,5},{1,3},{0,1},{10,8},{12,10},{14... | collective-permute-start | bytes 786440 | tf_op jit(solution)/shard_map/ppermute | solution.py:376
  26.8 9.1 %collective-permute-start.10 = (bf16[2,64,1024]{2,1,0:T(8,128)(2,1)S(1)}, bf16[2,64,1024]{2,1,0:T(8,128)(2,1)S(1)}, u32[]{:S(2)}, u32[]{:S(2)}) collective-permute-start(bf16[2,64,1024]{2,1,0:T(8,128)(2,1)S(1)} %get-tuple-element.136), channel_id=1, source_target_pairs={{0,2},{2,4},{4,6},{6,7},{7,5},{5,3},{3,1},{1,0},{8,10},{10,12},{12... | collective-permute-start | bytes 786440 | tf_op jit(solution)/shard_map/ppermute | solution.py:376
  28.4 9.2 %collective-permute-start.11 = (bf16[2,64,1024]{2,1,0:T(8,128)(2,1)S(1)}, bf16[2,64,1024]{2,1,0:T(8,128)(2,1)S(1)}, u32[]{:S(2)}, u32[]{:S(2)}) collective-permute-start(bf16[2,64,1024]{2,1,0:T(8,128)(2,1)S(1)} %get-tuple-element.137), channel_id=1, source_target_pairs={{2,0},{4,2},{6,4},{7,6},{5,7},{3,5},{1,3},{0,1},{10,8},{12,10},{14... | collective-permute-start | bytes 786440 | tf_op jit(solution)/shard_map/ppermute | solution.py:376
  32.4 8.4 %collective-permute-start.8 = (bf16[2,64,1024]{2,1,0:T(8,128)(2,1)S(1)}, bf16[2,64,1024]{2,1,0:T(8,128)(2,1)S(1)}, u32[]{:S(2)}, u32[]{:S(2)}) collective-permute-start(bf16[2,64,1024]{2,1,0:T(8,128)(2,1)S(1)} %get-tuple-element.134), channel_id=1, source_target_pairs={{0,2},{2,4},{4,6},{6,7},{7,5},{5,3},{3,1},{1,0},{8,10},{10,12},{12... | collective-permute-start | bytes 786440 | tf_op jit(solution)/shard_map/ppermute | solution.py:376
  34.0 9.4 %collective-permute-start.9 = (bf16[2,64,1024]{2,1,0:T(8,128)(2,1)S(1)}, bf16[2,64,1024]{2,1,0:T(8,128)(2,1)S(1)}, u32[]{:S(2)}, u32[]{:S(2)}) collective-permute-start(bf16[2,64,1024]{2,1,0:T(8,128)(2,1)S(1)} %get-tuple-element.135), channel_id=1, source_target_pairs={{2,0},{4,2},{6,4},{7,6},{5,7},{3,5},{1,3},{0,1},{10,8},{12,10},{14... | collective-permute-start | bytes 786440 | tf_op jit(solution)/shard_map/ppermute | solution.py:376
  38.6 5.0 %collective-permute-start.12 = (bf16[1,64,1024]{2,1,0:T(8,128)(2,1)S(1)}, bf16[1,64,1024]{2,1,0:T(8,128)(2,1)S(1)}, u32[]{:S(2)}, u32[]{:S(2)}) collective-permute-start(bf16[1,64,1024]{2,1,0:T(8,128)(2,1)S(1)} %get-tuple-element.140), channel_id=1, source_target_pairs={{0,2},{2,4},{4,6},{6,7},{7,5},{5,3},{3,1},{1,0},{8,10},{10,12},{12... | collective-permute-start | bytes 393224 | tf_op jit(solution)/shard_map/ppermute | solution.py:376
  40.8 5.2 %collective-permute-start.14 = (bf16[1,64,1024]{2,1,0:T(8,128)(2,1)S(1)}, bf16[1,64,1024]{2,1,0:T(8,128)(2,1)S(1)}, u32[]{:S(2)}, u32[]{:S(2)}) collective-permute-start(bf16[1,64,1024]{2,1,0:T(8,128)(2,1)S(1)} %slice.10), channel_id=1, source_target_pairs={{0,2},{2,4},{4,6},{6,7},{7,5},{5,3},{3,1},{1,0},{8,10},{10,12},{12... | collective-permute-start | bytes 393224 | tf_op jit(solution)/shard_map/ppermute | solution.py:376
  54.6 10.7 %collective-permute-start.20 = (bf16[256,512]{1,0:T(8,128)(2,1)S(1)}, bf16[256,512]{1,0:T(8,128)(2,1)S(1)}, u32[]{:S(2)}, u32[]{:S(2)}) collective-permute-start(bf16[256,512]{1,0:T(8,128)(2,1)S(1)} %get-tuple-element.166), channel_id=1, source_target_pairs={{8,0},{9,1},{10,2},{11,3},{12,4},{13,5},{14,6},{15,7}} | collective-permute-start | bytes 786440 | tf_op jit(solution)/shard_map/ppermute | solution.py:427
  56.0 12.2 %collective-permute-start.19 = (bf16[256,512]{1,0:T(8,128)(2,1)S(1)}, bf16[256,512]{1,0:T(8,128)(2,1)S(1)}, u32[]{:S(2)}, u32[]{:S(2)}) collective-permute-start(bf16[256,512]{1,0:T(8,128)(2,1)S(1)} %get-tuple-element.165.refs_0_), channel_id=1, source_target_pairs={{8,0},{9,1},{10,2},{11,3},{12,4},{13,5},{14,6},{15,7}} | collective-permute-start | bytes 786440 | tf_op jit(solution)/shard_map/ppermute | solution.py:427
  57.3 13.7 %collective-permute-start.25 = (bf16[256,512]{1,0:T(8,128)(2,1)S(1)}, bf16[256,512]{1,0:T(8,128)(2,1)S(1)}, u32[]{:S(2)}, u32[]{:S(2)}) collective-permute-start(bf16[256,512]{1,0:T(8,128)(2,1)S(1)} %get-tuple-element.194), channel_id=1, source_target_pairs={{8,0},{9,1},{10,2},{11,3},{12,4},{13,5},{14,6},{15,7}} | collective-permute-start | bytes 786440 | tf_op jit(solution)/shard_map/ppermute | solution.py:427
  58.9 15.2 %collective-permute-start.24 = (bf16[256,512]{1,0:T(8,128)(2,1)S(1)}, bf16[256,512]{1,0:T(8,128)(2,1)S(1)}, u32[]{:S(2)}, u32[]{:S(2)}) collective-permute-start(bf16[256,512]{1,0:T(8,128)(2,1)S(1)} %get-tuple-element.193), channel_id=1, source_target_pairs={{8,0},{9,1},{10,2},{11,3},{12,4},{13,5},{14,6},{15,7}} | collective-permute-start | bytes 786440 | tf_op jit(solution)/shard_map/ppermute | solution.py:427
  77.4 8.7 %collective-permute-start.26 = (bf16[2,64,1024]{2,1,0:T(8,128)(2,1)S(1)}, bf16[2,64,1024]{2,1,0:T(8,128)(2,1)S(1)}, u32[]{:S(2)}, u32[]{:S(2)}) collective-permute-start(bf16[2,64,1024]{2,1,0:T(8,128)(2,1)S(1)} %get-tuple-element.209.refs_6_), channel_id=1, source_target_pairs={{0,2},{2,4},{4,6},{6,7},{7,5},{5,3},{3,1},{1,0},{8,10},{10,12},{12... | collective-permute-start | bytes 786440 | tf_op jit(solution)/shard_map/ppermute | solution.py:376
  79.1 8.5 %collective-permute-start.27 = (bf16[2,64,1024]{2,1,0:T(8,128)(2,1)S(1)}, bf16[2,64,1024]{2,1,0:T(8,128)(2,1)S(1)}, u32[]{:S(2)}, u32[]{:S(2)}) collective-permute-start(bf16[2,64,1024]{2,1,0:T(8,128)(2,1)S(1)} %get-tuple-element.212), channel_id=1, source_target_pairs={{2,0},{4,2},{6,4},{7,6},{5,7},{3,5},{1,3},{0,1},{10,8},{12,10},{14... | collective-permute-start | bytes 786440 | tf_op jit(solution)/shard_map/ppermute | solution.py:376
  81.6 10.3 %collective-permute-start.30 = (bf16[2,64,1024]{2,1,0:T(8,128)(2,1)S(1)}, bf16[2,64,1024]{2,1,0:T(8,128)(2,1)S(1)}, u32[]{:S(2)}, u32[]{:S(2)}) collective-permute-start(bf16[2,64,1024]{2,1,0:T(8,128)(2,1)S(1)} %get-tuple-element.219), channel_id=1, source_target_pairs={{0,2},{2,4},{4,6},{6,7},{7,5},{5,3},{3,1},{1,0},{8,10},{10,12},{12... | collective-permute-start | bytes 786440 | tf_op jit(solution)/shard_map/ppermute | solution.py:376
  83.3 9.8 %collective-permute-start.31 = (bf16[2,64,1024]{2,1,0:T(8,128)(2,1)S(1)}, bf16[2,64,1024]{2,1,0:T(8,128)(2,1)S(1)}, u32[]{:S(2)}, u32[]{:S(2)}) collective-permute-start(bf16[2,64,1024]{2,1,0:T(8,128)(2,1)S(1)} %get-tuple-element.220), channel_id=1, source_target_pairs={{2,0},{4,2},{6,4},{7,6},{5,7},{3,5},{1,3},{0,1},{10,8},{12,10},{14... | collective-permute-start | bytes 786440 | tf_op jit(solution)/shard_map/ppermute | solution.py:376
  87.7 9.7 %collective-permute-start.28 = (bf16[2,64,1024]{2,1,0:T(8,128)(2,1)S(1)}, bf16[2,64,1024]{2,1,0:T(8,128)(2,1)S(1)}, u32[]{:S(2)}, u32[]{:S(2)}) collective-permute-start(bf16[2,64,1024]{2,1,0:T(8,128)(2,1)S(1)} %get-tuple-element.213.refs_6_.refs_0_), channel_id=1, source_target_pairs={{0,2},{2,4},{4,6},{6,7},{7,5},{5,3},{3,1},{1,0},{8,10},{10,12},{12... | collective-permute-start | bytes 786440 | tf_op jit(solution)/shard_map/ppermute | solution.py:376
  88.6 10.1 %collective-permute-start.29 = (bf16[2,64,1024]{2,1,0:T(8,128)(2,1)S(1)}, bf16[2,64,1024]{2,1,0:T(8,128)(2,1)S(1)}, u32[]{:S(2)}, u32[]{:S(2)}) collective-permute-start(bf16[2,64,1024]{2,1,0:T(8,128)(2,1)S(1)} %get-tuple-element.216), channel_id=1, source_target_pairs={{2,0},{4,2},{6,4},{7,6},{5,7},{3,5},{1,3},{0,1},{10,8},{12,10},{14... | collective-permute-start | bytes 786440 | tf_op jit(solution)/shard_map/ppermute | solution.py:376
  93.3 9.9 %collective-permute-start.34 = (bf16[2,64,1024]{2,1,0:T(8,128)(2,1)S(1)}, bf16[2,64,1024]{2,1,0:T(8,128)(2,1)S(1)}, u32[]{:S(2)}, u32[]{:S(2)}) collective-permute-start(bf16[2,64,1024]{2,1,0:T(8,128)(2,1)S(1)} %get-tuple-element.221.refs_0_), channel_id=1, source_target_pairs={{0,2},{2,4},{4,6},{6,7},{7,5},{5,3},{3,1},{1,0},{8,10},{10,12},{12... | collective-permute-start | bytes 786440 | tf_op jit(solution)/shard_map/ppermute | solution.py:376
  94.3 10.1 %collective-permute-start.35 = (bf16[2,64,1024]{2,1,0:T(8,128)(2,1)S(1)}, bf16[2,64,1024]{2,1,0:T(8,128)(2,1)S(1)}, u32[]{:S(2)}, u32[]{:S(2)}) collective-permute-start(bf16[2,64,1024]{2,1,0:T(8,128)(2,1)S(1)} %get-tuple-element.228), channel_id=1, source_target_pairs={{2,0},{4,2},{6,4},{7,6},{5,7},{3,5},{1,3},{0,1},{10,8},{12,10},{14... | collective-permute-start | bytes 786440 | tf_op jit(solution)/shard_map/ppermute | solution.py:376
  98.9 9.7 %collective-permute-start.32 = (bf16[2,64,1024]{2,1,0:T(8,128)(2,1)S(1)}, bf16[2,64,1024]{2,1,0:T(8,128)(2,1)S(1)}, u32[]{:S(2)}, u32[]{:S(2)}) collective-permute-start(bf16[2,64,1024]{2,1,0:T(8,128)(2,1)S(1)} %get-tuple-element.222.refs_6_.refs_0_), channel_id=1, source_target_pairs={{0,2},{2,4},{4,6},{6,7},{7,5},{5,3},{3,1},{1,0},{8,10},{10,12},{12... | collective-permute-start | bytes 786440 | tf_op jit(solution)/shard_map/ppermute | solution.py:376
  99.9 10.1 %collective-permute-start.33 = (bf16[2,64,1024]{2,1,0:T(8,128)(2,1)S(1)}, bf16[2,64,1024]{2,1,0:T(8,128)(2,1)S(1)}, u32[]{:S(2)}, u32[]{:S(2)}) collective-permute-start(bf16[2,64,1024]{2,1,0:T(8,128)(2,1)S(1)} %get-tuple-element.225), channel_id=1, source_target_pairs={{2,0},{4,2},{6,4},{7,6},{5,7},{3,5},{1,3},{0,1},{10,8},{12,10},{14... | collective-permute-start | bytes 786440 | tf_op jit(solution)/shard_map/ppermute | solution.py:376
  104.5 11.1 %collective-permute-start.37 = (bf16[2,64,1024]{2,1,0:T(8,128)(2,1)S(1)}, bf16[2,64,1024]{2,1,0:T(8,128)(2,1)S(1)}, u32[]{:S(2)}, u32[]{:S(2)}) collective-permute-start(bf16[2,64,1024]{2,1,0:T(8,128)(2,1)S(1)} %get-tuple-element.233), channel_id=1, source_target_pairs={{2,0},{4,2},{6,4},{7,6},{5,7},{3,5},{1,3},{0,1},{10,8},{12,10},{14... | collective-permute-start | bytes 786440 | tf_op jit(solution)/shard_map/ppermute | solution.py:376
  105.0 10.7 %collective-permute-start.38 = (bf16[2,64,1024]{2,1,0:T(8,128)(2,1)S(1)}, bf16[2,64,1024]{2,1,0:T(8,128)(2,1)S(1)}, u32[]{:S(2)}, u32[]{:S(2)}) collective-permute-start(bf16[2,64,1024]{2,1,0:T(8,128)(2,1)S(1)} %get-tuple-element.229.refs_0_), channel_id=1, source_target_pairs={{0,2},{2,4},{4,6},{6,7},{7,5},{5,3},{3,1},{1,0},{8,10},{10,12},{12... | collective-permute-start | bytes 786440 | tf_op jit(solution)/shard_map/ppermute | solution.py:376
  110.1 7.8 %collective-permute-start.36 = (bf16[2,64,1024]{2,1,0:T(8,128)(2,1)S(1)}, bf16[2,64,1024]{2,1,0:T(8,128)(2,1)S(1)}, u32[]{:S(2)}, u32[]{:S(2)}) collective-permute-start(bf16[2,64,1024]{2,1,0:T(8,128)(2,1)S(1)} %get-tuple-element.230.refs_6_), channel_id=1, source_target_pairs={{0,2},{2,4},{4,6},{6,7},{7,5},{5,3},{3,1},{1,0},{8,10},{10,12},{12... | collective-permute-start | bytes 786440 | tf_op jit(solution)/shard_map/ppermute | solution.py:376
  111.1 8.2 %collective-permute-start.39 = (bf16[2,64,1024]{2,1,0:T(8,128)(2,1)S(1)}, bf16[2,64,1024]{2,1,0:T(8,128)(2,1)S(1)}, u32[]{:S(2)}, u32[]{:S(2)}) collective-permute-start(bf16[2,64,1024]{2,1,0:T(8,128)(2,1)S(1)} %get-tuple-element.234), channel_id=1, source_target_pairs={{2,0},{4,2},{6,4},{7,6},{5,7},{3,5},{1,3},{0,1},{10,8},{12,10},{14... | collective-permute-start | bytes 786440 | tf_op jit(solution)/shard_map/ppermute | solution.py:376
  (11 other events, 44.3 us)
where the time goes:
time: 121 us; the launch traced here: 120 us
  waiting for transfers between devices  45.9 us (38%)
  starting transfers between devices  42.3 us (35%)
  Pallas kernels  28.7 us (24%)
  local copies, waits for them, and re-layouts  1.32 us (1%)
    ppermute x15, starting transfers between devices, send(): lax.ppermute(to_right, 'dp', right)  24.4 us
    ppermute x15, waiting for transfers between devices, send(): lax.ppermute(to_left, 'dp', left)  21.6 us
    ppermute x15, waiting for transfers between devices, send(): lax.ppermute(to_right, 'dp', right)  15 us
    pallas_call x5, Pallas kernels, term_call(): pl.pallas_call(functools.partial(term_kernel, replicas, offsets, micro),...  9.98 us
    ppermute x8, waiting for transfers between devices, local(): g[m][half_at] = lax.ppermute(piece, 'pipe', [(stage, stage - 1)])  9.4 us
    ppermute x15, starting transfers between devices, send(): lax.ppermute(to_left, 'dp', left)  8.22 us
    ppermute x8, starting transfers between devices, local(): g[m][half_at] = lax.ppermute(piece, 'pipe', [(stage, stage - 1)])  8.1 us
    pallas_call x7, Pallas kernels, partial_call(): pl.pallas_call(functools.partial(partial_kernel, replicas, items, not hel...  6.69 us
  transfers between devices with their start and end apart: 40, of which 29 were waited for; matrix products, arithmetic and copies ran while one was open for 1% of the time, Pallas kernels for 19%

commit v1 on v0

--- a/solution.py
+++ b/solution.py
@@ -36,31 +36,6 @@
     at = lax.rem(place + (offset + replicas), replicas)
     owner = jnp.where(at < replicas // 2, 2 * at, 2 * (replicas - 1 - at) + 1)
     return pl.multiple_of(owner * part, part)
-
-
-def split_kernel(conv, mix, low, high, sems):
-    copies = [
-        pltpu.make_async_copy(conv.at[0:2], low, sems.at[0]),
-        pltpu.make_async_copy(conv.at[2], high.at[0], sems.at[1]),
-        pltpu.make_async_copy(mix.at[0], high.at[1], sems.at[2]),
-    ]
-    for copy in copies:
-        copy.start()
-    for copy in copies:
-        copy.wait()
-
-
-def split_call(conv, mix):
-    anywhere = pl.BlockSpec(memory_space=pl.ANY)
-    return pl.pallas_call(
-        split_kernel,
-        out_shape=[pltpu.VMEM((2, *conv.shape[1:]), BF16)] * 2,
-        in_specs=[anywhere] * 2,
-        out_specs=[VMEM] * 2,
-        scratch_shapes=[pltpu.SemaphoreType.DMA((3,))],
-        compiler_params=PARAMS,
-        cost_estimate=cost(0, 2**20),
-    )(*[pltpu.with_memory_space_constraint(array, pltpu.HBM) for array in (conv, mix)])
 
 
 def prepare_kernel(x, taps_t):
@@ -110,6 +85,8 @@
             continue
         rows += [taps_t[pl.ds((first + k) * channels + row, part), columns] for k in range(count)]
         weights.append(block[:count].reshape(count * part, wide))
+    if not rows:
+        return None
     return lax.dot_general(
         jnp.concatenate(rows, axis=0), jnp.concatenate(weights, axis=0), TN, preferred_element_type=F32
     )
@@ -122,7 +99,7 @@
             w[pl.ds((first + k) * channels + row, block.shape[1]), :] = block[k]
 
 
-def partial_kernel(replicas, items, first, quarters, tokens, taps_t, *refs):
+def partial_kernel(replicas, items, first, passing, tokens, taps_t, *refs):
     count = len(items)
     blocks = refs[:count]
     placed = place_rows(replicas, items, blocks)
@@ -133,11 +110,19 @@
     for at in range(0, rows, chunk):
         columns = slice(at, at + chunk)
         term = shard_term(taps_t, columns, placed)
-        acc[columns, :] = term if first else refs[0][columns, :] + term
+        if term is not None:
+            acc[columns, :] = term if first else refs[0][columns, :] + term
     store_shards(w, placed)
-    if quarters:
+    if passing == "quarters":
         passed[0][...] = blocks[0][0:1]
         passed[1][...] = blocks[1][1:2]
+    if passing == "low":
+        for out, block in zip(passed, blocks):
+            out[...] = block[0:2]
+    if passing == "high":
+        for out, conv, block in zip(passed, refs[2 : 2 + tokens], blocks):
+            out[0] = conv[2]
+            out[1] = block[0]
 
 
 def partial_call(replicas, items, taps_t, blocks, held, passing=None, tokens=()):
@@ -149,9 +134,9 @@
     if passing == "whole":
         aliases |= {1 + i: 2 + i for i in range(count)}
     return pl.pallas_call(
-        functools.partial(partial_kernel, replicas, items, not held, passing == "quarters", len(tokens)),
+        functools.partial(partial_kernel, replicas, items, not held, passing, len(tokens)),
         out_shape=[pltpu.VMEM((rows, wide), F32), pltpu.VMEM((2 * wide, wide), BF16)]
-        + [pltpu.VMEM((2 if passing == "whole" else 1, part, wide), BF16) for _ in blocks if passing],
+        + [pltpu.VMEM((1 if passing == "quarters" else 2, part, wide), BF16) for _ in blocks if passing],
         in_specs=[VMEM] * len(inputs),
         out_specs=[VMEM] * (2 + count if passing else 2),
         input_output_aliases=aliases,
@@ -289,7 +274,9 @@
     def mix_rows(m):
         return jnp.concatenate([hids[m][pl.ds(row, part), :] for row in places], axis=0)
 
-    @pl.loop(0, wide // step)
+    unroll = offsets == (replicas // 2,)
+
+    @pl.loop(0, wide // step, unroll=unroll)
     def _(j):
         columns = pl.ds(pl.multiple_of(j * step, step), step)
         conv = product(conv_rows, lambda m, at: pgs[m][:, at], columns)
@@ -299,7 +286,7 @@
                 at = (slot * 3 + k) * part
                 target[index, :, columns] = conv[at : at + part, :].astype(low.dtype)
 
-    @pl.loop(0, channels // step)
+    @pl.loop(0, channels // step, unroll=unroll)
     def _(j):
         columns = pl.ds(pl.multiple_of(j * step, step), step)
         after = pl.ds(pl.multiple_of(channels + j * step, step), step)
@@ -376,11 +363,14 @@
         return lax.ppermute(to_right, "dp", right), lax.ppermute(to_left, "dp", left)
 
     taps_t = prepare_call(x_ckpt[0].reshape(micro * seqs, samples, channels))
-    low, high = split_call(w_conv[0].transpose(1, 0, 2), w_mix)
-    streams = {0: (low, low), 2: (high, high)}
-    held = partial_call(replicas, ((0, 0), (0, 2)), taps_t, [low, high], [])
+    conv = w_conv[0].transpose(1, 0, 2)
+    held = partial_call(replicas, ((0, 0), (0, 3)), taps_t, [conv, w_mix], [])
+    convs, mixes = send(conv, conv), send(w_mix, w_mix)
+    *held, low_r, low_l = partial_call(replicas, ((-1, 0), (1, 0)), taps_t, convs, held, "low")
+    *held, high_r, high_l = partial_call(replicas, ((-1, 3), (1, 3)), taps_t, mixes, held, "high", convs)
+    streams = {0: (low_r, low_l), 2: (high_r, high_l)}
     skip = skip_cot.reshape(micro, block, channels)
-    for step in range(1, half):
+    for step in range(2, half):
         last = step == half - 1
         for first, (to_right, to_left) in streams.items():
             got = send(to_right, to_left)

time: 121 us -> 121 us (level)
  waiting for transfers between devices: 45.9 us -> 48.7 us
  Pallas kernels: 28.7 us -> 26.5 us
    ppermute x15, waiting for transfers between devices: 15 us -> 22.6 us  [send(): lax.ppermute(to_right, 'dp', right)]
    ppermute x15, waiting for transfers between devices: 21.6 us -> 16.7 us  [send(): lax.ppermute(to_left, 'dp', left)]
    ppermute x15, starting transfers between devices: 8.22 us -> 6.09 us  [send(): lax.ppermute(to_left, 'dp', left)]
    ppermute x15, starting transfers between devices: 24.4 us -> 26.1 us  [send(): lax.ppermute(to_right, 'dp', right)]
  transfers between devices with their start and end apart: 40 -> 40, of which waited for: 29 -> 29; matrix products, arithmetic and copies ran while one was open for 1% -> 1% of each run, Pallas kernels for 19% -> 18%
where the time goes in v1:
time: 121 us; the launch traced here: 120 us
  waiting for transfers between devices  48.7 us (40%)
  starting transfers between devices  41.6 us (34%)
  Pallas kernels  26.5 us (22%)
  local copies, waits for them, and re-layouts  1.33 us (1%)
    ppermute x15, starting transfers between devices, send(): lax.ppermute(to_right, 'dp', right)  26.1 us
    ppermute x15, waiting for transfers between devices, send(): lax.ppermute(to_right, 'dp', right)  22.6 us
    ppermute x15, waiting for transfers between devices, send(): lax.ppermute(to_left, 'dp', left)  16.7 us
    ppermute x8, waiting for transfers between devices, local(): g[m][half_at] = lax.ppermute(piece, 'pipe', [(stage, stage - 1)])  9.42 us
    pallas_call x5, Pallas kernels, term_call(): pl.pallas_call(functools.partial(term_kernel, replicas, offsets, micro),...  9.11 us
    ppermute x8, starting transfers between devices, local(): g[m][half_at] = lax.ppermute(piece, 'pipe', [(stage, stage - 1)])  7.88 us
    pallas_call x14, Pallas kernels, chain_call(): pl.pallas_call(functools.partial(chain_kernel, stage, index, halves, padd...  6.43 us
    pallas_call x7, Pallas kernels, partial_call(): pl.pallas_call(functools.partial(partial_kernel, replicas, items, not hel...  6.29 us
  transfers between devices with their start and end apart: 40, of which 29 were waited for; matrix products, arithmetic and copies ran while one was open for 1% of the time, Pallas kernels for 18%

profile of v1, /device:TPU:0, one launch (start us, length us, event | category | flops | bytes accessed | tf_op | source)
XLA Modules:
  0.0 120.4 jit_solution(14420138911700553073)
XLA Ops:
  0.6 3.1 %collective-permute-start.2 = (bf16[3,64,1024]{2,1,0:T(8,128)(2,1)}, bf16[3,64,1024]{2,1,0:T(8,128)(2,1)S(1)}, u32[]{:S(2)}, u32[]{:S(2)}) collective-permute-start(bf16[3,64,1024]{2,1,0:T(8,128)(2,1)} %bitcast.42), channel_id=1, source_target_pairs={{0,2},{2,4},{4,6},{6,7},{7,5},{5,3},{3,1},{1,0},{8,10},{10,12},{12... | collective-permute-start | bytes 1179656 | tf_op jit(solution)/shard_map/ppermute | solution.py:363
  3.7 2.0 %collective-permute-start = (bf16[1,64,1024]{2,1,0:T(8,128)(2,1)}, bf16[1,64,1024]{2,1,0:T(8,128)(2,1)S(1)}, u32[]{:S(2)}, u32[]{:S(2)}) collective-permute-start(bf16[1,64,1024]{2,1,0:T(8,128)(2,1)} %refs_1_.1), channel_id=1, source_target_pairs={{0,2},{2,4},{4,6},{6,7},{7,5},{5,3},{3,1},{1,0},{8,10},{10,12},{12... | collective-permute-start | bytes 393224 | tf_op jit(solution)/shard_map/ppermute | solution.py:363
  9.1 4.7 %collective-permute-done.2.refs_0_.refs_4_ = bf16[3,64,1024]{2,1,0:T(8,128)(2,1)S(1)} collective-permute-done((bf16[3,64,1024]{2,1,0:T(8,128)(2,1)}, bf16[3,64,1024]{2,1,0:T(8,128)(2,1)S(1)}, u32[]{:S(2)}, u32[]{:S(2)}) %collective-permute-start.2) | collective-permute-done | bytes 393248 | tf_op jit(solution)/shard_map/ppermute | solution.py:363
  13.8 2.1 %collective-permute-done.3.refs_1_.refs_5_ = bf16[3,64,1024]{2,1,0:T(8,128)(2,1)S(1)} collective-permute-done((bf16[3,64,1024]{2,1,0:T(8,128)(2,1)}, bf16[3,64,1024]{2,1,0:T(8,128)(2,1)S(1)}, u32[]{:S(2)}, u32[]{:S(2)}) %collective-permute-start.3) | collective-permute-done | bytes 393248 | tf_op jit(solution)/shard_map/ppermute | solution.py:363
  15.9 1.5 %shard_map.78 = (f32[1024,1024]{1,0:T(8,128)S(1)}, bf16[2048,1024]{1,0:T(8,128)(2,1)S(1)}, bf16[2,64,1024]{2,1,0:T(8,128)(2,1)S(1)}, bf16[2,64,1024]{2,1,0:T(8,128)(2,1)S(1)}) custom-call(bf16[1536,1024]{1,0:T(8,128)(2,1)S(1)} %shard_map.76.taps_t, ...), custom_call_target="tpu_custom_call", output_to_operand_aliasing={{0}: (3, {}), {1}: (4, {})} | custom-call | flops 402653184 | bytes 1048576 | tf_op jit(solution)/shard_map/pallas_call | solution.py:136
  17.4 1.6 %collective-permute-start.6 = (bf16[2,64,1024]{2,1,0:T(8,128)(2,1)S(1)}, bf16[2,64,1024]{2,1,0:T(8,128)(2,1)S(1)}, u32[]{:S(2)}, u32[]{:S(2)}) collective-permute-start(bf16[2,64,1024]{2,1,0:T(8,128)(2,1)S(1)} %get-tuple-element.124), channel_id=1, source_target_pairs={{0,2},{2,4},{4,6},{6,7},{7,5},{5,3},{3,1},{1,0},{8,10},{10,12},{12... | collective-permute-start | bytes 786440 | tf_op jit(solution)/shard_map/ppermute | solution.py:363
  19.5 1.6 %collective-permute-start.4 = (bf16[2,64,1024]{2,1,0:T(8,128)(2,1)S(1)}, bf16[2,64,1024]{2,1,0:T(8,128)(2,1)S(1)}, u32[]{:S(2)}, u32[]{:S(2)}) collective-permute-start(bf16[2,64,1024]{2,1,0:T(8,128)(2,1)S(1)} %get-tuple-element.122), channel_id=1, source_target_pairs={{0,2},{2,4},{4,6},{6,7},{7,5},{5,3},{3,1},{1,0},{8,10},{10,12},{12... | collective-permute-start | bytes 786440 | tf_op jit(solution)/shard_map/ppermute | solution.py:363
  21.6 4.6 %collective-permute-done.6.refs_0_ = bf16[2,64,1024]{2,1,0:T(8,128)(2,1)S(1)} collective-permute-done((bf16[2,64,1024]{2,1,0:T(8,128)(2,1)S(1)}, bf16[2,64,1024]{2,1,0:T(8,128)(2,1)S(1)}, u32[]{:S(2)}, u32[]{:S(2)}) %collective-permute-start.6) | collective-permute-done | bytes 262176 | tf_op jit(solution)/shard_map/ppermute | solution.py:363
  28.5 1.7 %collective-permute-start.10 = (bf16[2,64,1024]{2,1,0:T(8,128)(2,1)S(1)}, bf16[2,64,1024]{2,1,0:T(8,128)(2,1)S(1)}, u32[]{:S(2)}, u32[]{:S(2)}) collective-permute-start(bf16[2,64,1024]{2,1,0:T(8,128)(2,1)S(1)} %get-tuple-element.132), channel_id=1, source_target_pairs={{0,2},{2,4},{4,6},{6,7},{7,5},{5,3},{3,1},{1,0},{8,10},{10,12},{12... | collective-permute-start | bytes 786440 | tf_op jit(solution)/shard_map/ppermute | solution.py:363
  34.1 1.7 %collective-permute-start.8 = (bf16[2,64,1024]{2,1,0:T(8,128)(2,1)S(1)}, bf16[2,64,1024]{2,1,0:T(8,128)(2,1)S(1)}, u32[]{:S(2)}, u32[]{:S(2)}) collective-permute-start(bf16[2,64,1024]{2,1,0:T(8,128)(2,1)S(1)} %get-tuple-element.130), channel_id=1, source_target_pairs={{0,2},{2,4},{4,6},{6,7},{7,5},{5,3},{3,1},{1,0},{8,10},{10,12},{12... | collective-permute-start | bytes 786440 | tf_op jit(solution)/shard_map/ppermute | solution.py:363
  36.1 1.6 %collective-permute-done.10.refs_0_ = bf16[2,64,1024]{2,1,0:T(8,128)(2,1)S(1)} collective-permute-done((bf16[2,64,1024]{2,1,0:T(8,128)(2,1)S(1)}, bf16[2,64,1024]{2,1,0:T(8,128)(2,1)S(1)}, u32[]{:S(2)}, u32[]{:S(2)}) %collective-permute-start.10) | collective-permute-done | bytes 262176 | tf_op jit(solution)/shard_map/ppermute | solution.py:363
  40.3 2.0 %collective-permute-start.12 = (bf16[1,64,1024]{2,1,0:T(8,128)(2,1)S(1)}, bf16[1,64,1024]{2,1,0:T(8,128)(2,1)S(1)}, u32[]{:S(2)}, u32[]{:S(2)}) collective-permute-start(bf16[1,64,1024]{2,1,0:T(8,128)(2,1)S(1)} %get-tuple-element.136), channel_id=1, source_target_pairs={{0,2},{2,4},{4,6},{6,7},{7,5},{5,3},{3,1},{1,0},{8,10},{10,12},{12... | collective-permute-start | bytes 393224 | tf_op jit(solution)/shard_map/ppermute | solution.py:363
  42.6 1.8 %collective-permute-start.14 = (bf16[1,64,1024]{2,1,0:T(8,128)(2,1)S(1)}, bf16[1,64,1024]{2,1,0:T(8,128)(2,1)S(1)}, u32[]{:S(2)}, u32[]{:S(2)}) collective-permute-start(bf16[1,64,1024]{2,1,0:T(8,128)(2,1)S(1)} %slice.10), channel_id=1, source_target_pairs={{0,2},{2,4},{4,6},{6,7},{7,5},{5,3},{3,1},{1,0},{8,10},{10,12},{12... | collective-permute-start | bytes 393224 | tf_op jit(solution)/shard_map/ppermute | solution.py:363
  45.3 2.0 %collective-permute-done.13.refs_3_ = bf16[1,64,1024]{2,1,0:T(8,128)(2,1)S(1)} collective-permute-done((bf16[1,64,1024]{2,1,0:T(8,128)(2,1)S(1)}, bf16[1,64,1024]{2,1,0:T(8,128)(2,1)S(1)}, u32[]{:S(2)}, u32[]{:S(2)}) %collective-permute-start.13) | collective-permute-done | bytes 131104 | tf_op jit(solution)/shard_map/ppermute | solution.py:363
  61.2 5.1 %collective-permute-done.20.g = bf16[256,512]{1,0:T(8,128)(2,1)S(1)} collective-permute-done((bf16[256,512]{1,0:T(8,128)(2,1)S(1)}, bf16[256,512]{1,0:T(8,128)(2,1)S(1)}, u32[]{:S(2)}, u32[]{:S(2)}) %collective-permute-start.20) | collective-permute-done | bytes 262176 | tf_op jit(solution)/shard_map/ppermute | solution.py:417
  66.4 1.5 %shard_map.90 = (bf16[512,1024]{1,0:T(8,128)(2,1)S(1)}, bf16[512,512]{1,0:T(8,128)(2,1)S(1)}, bf16[512,512]{1,0:T(8,128)(2,1)S(1)}, f32[2,16,512]{2,1,0:T(8,128)S(1)}) custom-call(bf16[256,512]{1,0:T(8,128)(2,1)S(1)} %collective-permute-done.20.g, bf16[2,512,512]{2,1,0:T(8,128)(2,1)S(1)} %bitcast.30, ...), custom_call_target="tpu_custom_call", output_to_operand_aliasing={{0}: (5, {}), {1}: (6, {}), {2}: (7, {})} | custom-call | flops 536870912 | bytes 4194304 | tf_op jit(solution)/shard_map/pallas_call | solution.py:240
  69.2 1.5 %shard_map.91 = (bf16[512,1024]{1,0:T(8,128)(2,1)S(1)}, bf16[512,512]{1,0:T(8,128)(2,1)S(1)}, bf16[512,512]{1,0:T(8,128)(2,1)S(1)}) custom-call(bf16[256,512]{1,0:T(8,128)(2,1)S(1)} %collective-permute-done.19.g, bf16[2,512,512]{2,1,0:T(8,128)(2,1)S(1)} %bitcast.31, ...), custom_call_target="tpu_custom_call", output_to_operand_aliasing={{0}: (6, {}), {1}: (7, {}), {2}: (8, {})} | custom-call | flops 536870912 | bytes 4194304 | tf_op jit(solution)/shard_map/pallas_call | solution.py:240
  72.1 1.5 %shard_map.98 = (bf16[512,1024]{1,0:T(8,128)(2,1)S(1)}, bf16[512,512]{1,0:T(8,128)(2,1)S(1)}, bf16[512,512]{1,0:T(8,128)(2,1)S(1)}, f32[2,16,512]{2,1,0:T(8,128)S(1)}) custom-call(bf16[256,512]{1,0:T(8,128)(2,1)S(1)} %collective-permute-done.25.g, bf16[2,512,512]{2,1,0:T(8,128)(2,1)S(1)} %bitcast.32, ...), custom_call_target="tpu_custom_call", output_to_operand_aliasing={{0}: (6, {}), {1}: (7, {}), {2}: (8, {})} | custom-call | flops 536870912 | bytes 4194304 | tf_op jit(solution)/shard_map/pallas_call | solution.py:240
  73.6 1.6 %collective-permute-done.24.g = bf16[256,512]{1,0:T(8,128)(2,1)S(1)} collective-permute-done((bf16[256,512]{1,0:T(8,128)(2,1)S(1)}, bf16[256,512]{1,0:T(8,128)(2,1)S(1)}, u32[]{:S(2)}, u32[]{:S(2)}) %collective-permute-start.24) | collective-permute-done | bytes 262176 | tf_op jit(solution)/shard_map/ppermute | solution.py:417
  75.2 1.5 %shard_map.99 = (bf16[512,1024]{1,0:T(8,128)(2,1)S(1)}, bf16[512,512]{1,0:T(8,128)(2,1)S(1)}, bf16[512,512]{1,0:T(8,128)(2,1)S(1)}) custom-call(bf16[256,512]{1,0:T(8,128)(2,1)S(1)} %collective-permute-done.24.g, bf16[2,512,512]{2,1,0:T(8,128)(2,1)S(1)} %bitcast.33, ...), custom_call_target="tpu_custom_call", output_to_operand_aliasing={{0}: (6, {}), {1}: (7, {}), {2}: (8, {})} | custom-call | flops 536870912 | bytes 4194304 | tf_op jit(solution)/shard_map/pallas_call | solution.py:240
  79.7 2.2 %shard_map.101 = (bf16[2,64,1024]{2,1,0:T(8,128)(2,1)S(1)}, bf16[2,64,1024]{2,1,0:T(8,128)(2,1)S(1)}, bf16[2,64,1024]{2,1,0:T(8,128)(2,1)S(1)}, bf16[2,64,1024]{2,1,0:T(8,128)(2,1)S(1)}) custom-call(bf16[1536,1024]{1,0:T(8,128)(2,1)S(1)} %shard_map.76.taps_t, bf16[2,512,512]{2,1,0:T(8,128)(2,1)S(1)} %bitcast.35, ...), custom_call_target="tpu_custom_call" | custom-call | flops 1073741824 | bytes 1048576 | tf_op jit(solution)/shard_map/pallas_call | solution.py:307
  83.9 2.4 %collective-permute-done.26.got_r = bf16[2,64,1024]{2,1,0:T(8,128)(2,1)S(1)} collective-permute-done((bf16[2,64,1024]{2,1,0:T(8,128)(2,1)S(1)}, bf16[2,64,1024]{2,1,0:T(8,128)(2,1)S(1)}, u32[]{:S(2)}, u32[]{:S(2)}) %collective-permute-start.26) | collective-permute-done | bytes 262176 | tf_op jit(solution)/shard_map/ppermute | solution.py:363
  87.6 1.6 %collective-permute-start.28 = (bf16[2,64,1024]{2,1,0:T(8,128)(2,1)S(1)}, bf16[2,64,1024]{2,1,0:T(8,128)(2,1)S(1)}, u32[]{:S(2)}, u32[]{:S(2)}) collective-permute-start(bf16[2,64,1024]{2,1,0:T(8,128)(2,1)S(1)} %get-tuple-element.209.refs_6_.refs_0_), channel_id=1, source_target_pairs={{0,2},{2,4},{4,6},{6,7},{7,5},{5,3},{3,1},{1,0},{8,10},{10,12},{12... | collective-permute-start | bytes 786440 | tf_op jit(solution)/shard_map/ppermute | solution.py:363
  89.7 2.2 %shard_map.103 = (bf16[2,64,1024]{2,1,0:T(8,128)(2,1)S(1)}, bf16[2,64,1024]{2,1,0:T(8,128)(2,1)S(1)}, bf16[2,64,1024]{2,1,0:T(8,128)(2,1)S(1)}, bf16[2,64,1024]{2,1,0:T(8,128)(2,1)S(1)}) custom-call(bf16[1536,1024]{1,0:T(8,128)(2,1)S(1)} %shard_map.76.taps_t, bf16[2,512,512]{2,1,0:T(8,128)(2,1)S(1)} %bitcast.36, ...), custom_call_target="tpu_custom_call" | custom-call | flops 1073741824 | bytes 1048576 | tf_op jit(solution)/shard_map/pallas_call | solution.py:307
  93.3 1.6 %collective-permute-start.34 = (bf16[2,64,1024]{2,1,0:T(8,128)(2,1)S(1)}, bf16[2,64,1024]{2,1,0:T(8,128)(2,1)S(1)}, u32[]{:S(2)}, u32[]{:S(2)}) collective-permute-start(bf16[2,64,1024]{2,1,0:T(8,128)(2,1)S(1)} %get-tuple-element.217.refs_0_), channel_id=1, source_target_pairs={{0,2},{2,4},{4,6},{6,7},{7,5},{5,3},{3,1},{1,0},{8,10},{10,12},{12... | collective-permute-start | bytes 786440 | tf_op jit(solution)/shard_map/ppermute | solution.py:363
  95.3 2.3 %collective-permute-done.28.got_r = bf16[2,64,1024]{2,1,0:T(8,128)(2,1)S(1)} collective-permute-done((bf16[2,64,1024]{2,1,0:T(8,128)(2,1)S(1)}, bf16[2,64,1024]{2,1,0:T(8,128)(2,1)S(1)}, u32[]{:S(2)}, u32[]{:S(2)}) %collective-permute-start.28) | collective-permute-done | bytes 262176 | tf_op jit(solution)/shard_map/ppermute | solution.py:363
  98.9 1.6 %collective-permute-start.32 = (bf16[2,64,1024]{2,1,0:T(8,128)(2,1)S(1)}, bf16[2,64,1024]{2,1,0:T(8,128)(2,1)S(1)}, u32[]{:S(2)}, u32[]{:S(2)}) collective-permute-start(bf16[2,64,1024]{2,1,0:T(8,128)(2,1)S(1)} %get-tuple-element.218.refs_6_.refs_0_), channel_id=1, source_target_pairs={{0,2},{2,4},{4,6},{6,7},{7,5},{5,3},{3,1},{1,0},{8,10},{10,12},{12... | collective-permute-start | bytes 786440 | tf_op jit(solution)/shard_map/ppermute | solution.py:363
  101.0 2.2 %shard_map.106 = (bf16[2,64,1024]{2,1,0:T(8,128)(2,1)S(1)}, bf16[2,64,1024]{2,1,0:T(8,128)(2,1)S(1)}, bf16[2,64,1024]{2,1,0:T(8,128)(2,1)S(1)}, bf16[2,64,1024]{2,1,0:T(8,128)(2,1)S(1)}) custom-call(bf16[1536,1024]{1,0:T(8,128)(2,1)S(1)} %shard_map.76.taps_t, bf16[2,512,512]{2,1,0:T(8,128)(2,1)S(1)} %bitcast.37, ...), custom_call_target="tpu_custom_call" | custom-call | flops 1073741824 | bytes 1048576 | tf_op jit(solution)/shard_map/pallas_call | solution.py:307
  106.6 2.3 %collective-permute-done.32.got_r = bf16[2,64,1024]{2,1,0:T(8,128)(2,1)S(1)} collective-permute-done((bf16[2,64,1024]{2,1,0:T(8,128)(2,1)S(1)}, bf16[2,64,1024]{2,1,0:T(8,128)(2,1)S(1)}, u32[]{:S(2)}, u32[]{:S(2)}) %collective-permute-start.32) | collective-permute-done | bytes 262176 | tf_op jit(solution)/shard_map/ppermute | solution.py:363
  110.1 1.6 %collective-permute-start.36 = (bf16[2,64,1024]{2,1,0:T(8,128)(2,1)S(1)}, bf16[2,64,1024]{2,1,0:T(8,128)(2,1)S(1)}, u32[]{:S(2)}, u32[]{:S(2)}) collective-permute-start(bf16[2,64,1024]{2,1,0:T(8,128)(2,1)S(1)} %get-tuple-element.226.refs_6_), channel_id=1, source_target_pairs={{0,2},{2,4},{4,6},{6,7},{7,5},{5,3},{3,1},{1,0},{8,10},{10,12},{12... | collective-permute-start | bytes 786440 | tf_op jit(solution)/shard_map/ppermute | solution.py:363
  113.2 1.7 %shard_map.109 = (f32[2,64,1024]{2,1,0:T(8,128)S(1)}, f32[2,64,1024]{2,1,0:T(8,128)S(1)}) custom-call(bf16[1536,1024]{1,0:T(8,128)(2,1)S(1)} %shard_map.76.taps_t, bf16[2,512,512]{2,1,0:T(8,128)(2,1)S(1)} %bitcast.38, bf16[512,512]{1,0:T(8,128)(2,1)S(1)} %get-tuple-element.199.refs_0_, bf16[512,512]{1,0:T(8,128)(2,1)S(1)} %get-tuple-element.200.refs_1_, ...), custom_call_target="tpu_custom_call" | custom-call | flops 536870912 | bytes 1048576 | tf_op jit(solution)/shard_map/pallas_call | solution.py:307
  115.6 2.6 %collective-permute-done.36.low_r = bf16[2,64,1024]{2,1,0:T(8,128)(2,1)S(1)} collective-permute-done((bf16[2,64,1024]{2,1,0:T(8,128)(2,1)S(1)}, bf16[2,64,1024]{2,1,0:T(8,128)(2,1)S(1)}, u32[]{:S(2)}, u32[]{:S(2)}) %collective-permute-start.36) | collective-permute-done | bytes 262176 | tf_op jit(solution)/shard_map/ppermute | solution.py:363
  (97 shorter events, 50.5 us)
Async XLA Ops:
  0.6 13.2 %collective-permute-start.2 = (bf16[3,64,1024]{2,1,0:T(8,128)(2,1)}, bf16[3,64,1024]{2,1,0:T(8,128)(2,1)S(1)}, u32[]{:S(2)}, u32[]{:S(2)}) collective-permute-start(bf16[3,64,1024]{2,1,0:T(8,128)(2,1)} %bitcast.42), channel_id=1, source_target_pairs={{0,2},{2,4},{4,6},{6,7},{7,5},{5,3},{3,1},{1,0},{8,10},{10,12},{12... | collective-permute-start | bytes 1179656 | tf_op jit(solution)/shard_map/ppermute | solution.py:363
  3.7 12.2 %collective-permute-start.3 = (bf16[3,64,1024]{2,1,0:T(8,128)(2,1)}, bf16[3,64,1024]{2,1,0:T(8,128)(2,1)S(1)}, u32[]{:S(2)}, u32[]{:S(2)}) collective-permute-start(bf16[3,64,1024]{2,1,0:T(8,128)(2,1)} %bitcast.43), channel_id=1, source_target_pairs={{2,0},{4,2},{6,4},{7,6},{5,7},{3,5},{1,3},{0,1},{10,8},{12,10},{14... | collective-permute-start | bytes 1179656 | tf_op jit(solution)/shard_map/ppermute | solution.py:363
  3.7 15.8 %collective-permute-start = (bf16[1,64,1024]{2,1,0:T(8,128)(2,1)}, bf16[1,64,1024]{2,1,0:T(8,128)(2,1)S(1)}, u32[]{:S(2)}, u32[]{:S(2)}) collective-permute-start(bf16[1,64,1024]{2,1,0:T(8,128)(2,1)} %refs_1_.1), channel_id=1, source_target_pairs={{0,2},{2,4},{4,6},{6,7},{7,5},{5,3},{3,1},{1,0},{8,10},{10,12},{12... | collective-permute-start | bytes 393224 | tf_op jit(solution)/shard_map/ppermute | solution.py:363
  5.7 13.8 %collective-permute-start.1 = (bf16[1,64,1024]{2,1,0:T(8,128)(2,1)}, bf16[1,64,1024]{2,1,0:T(8,128)(2,1)S(1)}, u32[]{:S(2)}, u32[]{:S(2)}) collective-permute-start(bf16[1,64,1024]{2,1,0:T(8,128)(2,1)} %refs_1_.1), channel_id=1, source_target_pairs={{2,0},{4,2},{6,4},{7,6},{5,7},{3,5},{1,3},{0,1},{10,8},{12,10},{14... | collective-permute-start | bytes 393224 | tf_op jit(solution)/shard_map/ppermute | solution.py:363
  17.4 8.8 %collective-permute-start.6 = (bf16[2,64,1024]{2,1,0:T(8,128)(2,1)S(1)}, bf16[2,64,1024]{2,1,0:T(8,128)(2,1)S(1)}, u32[]{:S(2)}, u32[]{:S(2)}) collective-permute-start(bf16[2,64,1024]{2,1,0:T(8,128)(2,1)S(1)} %get-tuple-element.124), channel_id=1, source_target_pairs={{0,2},{2,4},{4,6},{6,7},{7,5},{5,3},{3,1},{1,0},{8,10},{10,12},{12... | collective-permute-start | bytes 786440 | tf_op jit(solution)/shard_map/ppermute | solution.py:363
  19.0 8.5 %collective-permute-start.7 = (bf16[2,64,1024]{2,1,0:T(8,128)(2,1)S(1)}, bf16[2,64,1024]{2,1,0:T(8,128)(2,1)S(1)}, u32[]{:S(2)}, u32[]{:S(2)}) collective-permute-start(bf16[2,64,1024]{2,1,0:T(8,128)(2,1)S(1)} %get-tuple-element.125), channel_id=1, source_target_pairs={{2,0},{4,2},{6,4},{7,6},{5,7},{3,5},{1,3},{0,1},{10,8},{12,10},{14... | collective-permute-start | bytes 786440 | tf_op jit(solution)/shard_map/ppermute | solution.py:363
  19.5 12.3 %collective-permute-start.4 = (bf16[2,64,1024]{2,1,0:T(8,128)(2,1)S(1)}, bf16[2,64,1024]{2,1,0:T(8,128)(2,1)S(1)}, u32[]{:S(2)}, u32[]{:S(2)}) collective-permute-start(bf16[2,64,1024]{2,1,0:T(8,128)(2,1)S(1)} %get-tuple-element.122), channel_id=1, source_target_pairs={{0,2},{2,4},{4,6},{6,7},{7,5},{5,3},{3,1},{1,0},{8,10},{10,12},{12... | collective-permute-start | bytes 786440 | tf_op jit(solution)/shard_map/ppermute | solution.py:363
  21.2 11.9 %collective-permute-start.5 = (bf16[2,64,1024]{2,1,0:T(8,128)(2,1)S(1)}, bf16[2,64,1024]{2,1,0:T(8,128)(2,1)S(1)}, u32[]{:S(2)}, u32[]{:S(2)}) collective-permute-start(bf16[2,64,1024]{2,1,0:T(8,128)(2,1)S(1)} %get-tuple-element.123), channel_id=1, source_target_pairs={{2,0},{4,2},{6,4},{7,6},{5,7},{3,5},{1,3},{0,1},{10,8},{12,10},{14... | collective-permute-start | bytes 786440 | tf_op jit(solution)/shard_map/ppermute | solution.py:363
  28.5 9.3 %collective-permute-start.10 = (bf16[2,64,1024]{2,1,0:T(8,128)(2,1)S(1)}, bf16[2,64,1024]{2,1,0:T(8,128)(2,1)S(1)}, u32[]{:S(2)}, u32[]{:S(2)}) collective-permute-start(bf16[2,64,1024]{2,1,0:T(8,128)(2,1)S(1)} %get-tuple-element.132), channel_id=1, source_target_pairs={{0,2},{2,4},{4,6},{6,7},{7,5},{5,3},{3,1},{1,0},{8,10},{10,12},{12... | collective-permute-start | bytes 786440 | tf_op jit(solution)/shard_map/ppermute | solution.py:363
  30.2 9.1 %collective-permute-start.11 = (bf16[2,64,1024]{2,1,0:T(8,128)(2,1)S(1)}, bf16[2,64,1024]{2,1,0:T(8,128)(2,1)S(1)}, u32[]{:S(2)}, u32[]{:S(2)}) collective-permute-start(bf16[2,64,1024]{2,1,0:T(8,128)(2,1)S(1)} %get-tuple-element.133), channel_id=1, source_target_pairs={{2,0},{4,2},{6,4},{7,6},{5,7},{3,5},{1,3},{0,1},{10,8},{12,10},{14... | collective-permute-start | bytes 786440 | tf_op jit(solution)/shard_map/ppermute | solution.py:363
  34.1 8.5 %collective-permute-start.8 = (bf16[2,64,1024]{2,1,0:T(8,128)(2,1)S(1)}, bf16[2,64,1024]{2,1,0:T(8,128)(2,1)S(1)}, u32[]{:S(2)}, u32[]{:S(2)}) collective-permute-start(bf16[2,64,1024]{2,1,0:T(8,128)(2,1)S(1)} %get-tuple-element.130), channel_id=1, source_target_pairs={{0,2},{2,4},{4,6},{6,7},{7,5},{5,3},{3,1},{1,0},{8,10},{10,12},{12... | collective-permute-start | bytes 786440 | tf_op jit(solution)/shard_map/ppermute | solution.py:363
  35.8 8.6 %collective-permute-start.9 = (bf16[2,64,1024]{2,1,0:T(8,128)(2,1)S(1)}, bf16[2,64,1024]{2,1,0:T(8,128)(2,1)S(1)}, u32[]{:S(2)}, u32[]{:S(2)}) collective-permute-start(bf16[2,64,1024]{2,1,0:T(8,128)(2,1)S(1)} %get-tuple-element.131), channel_id=1, source_target_pairs={{2,0},{4,2},{6,4},{7,6},{5,7},{3,5},{1,3},{0,1},{10,8},{12,10},{14... | collective-permute-start | bytes 786440 | tf_op jit(solution)/shard_map/ppermute | solution.py:363
  40.3 5.0 %collective-permute-start.12 = (bf16[1,64,1024]{2,1,0:T(8,128)(2,1)S(1)}, bf16[1,64,1024]{2,1,0:T(8,128)(2,1)S(1)}, u32[]{:S(2)}, u32[]{:S(2)}) collective-permute-start(bf16[1,64,1024]{2,1,0:T(8,128)(2,1)S(1)} %get-tuple-element.136), channel_id=1, source_target_pairs={{0,2},{2,4},{4,6},{6,7},{7,5},{5,3},{3,1},{1,0},{8,10},{10,12},{12... | collective-permute-start | bytes 393224 | tf_op jit(solution)/shard_map/ppermute | solution.py:363
  42.6 5.7 %collective-permute-start.14 = (bf16[1,64,1024]{2,1,0:T(8,128)(2,1)S(1)}, bf16[1,64,1024]{2,1,0:T(8,128)(2,1)S(1)}, u32[]{:S(2)}, u32[]{:S(2)}) collective-permute-start(bf16[1,64,1024]{2,1,0:T(8,128)(2,1)S(1)} %slice.10), channel_id=1, source_target_pairs={{0,2},{2,4},{4,6},{6,7},{7,5},{5,3},{3,1},{1,0},{8,10},{10,12},{12... | collective-permute-start | bytes 393224 | tf_op jit(solution)/shard_map/ppermute | solution.py:363
  55.7 10.7 %collective-permute-start.20 = (bf16[256,512]{1,0:T(8,128)(2,1)S(1)}, bf16[256,512]{1,0:T(8,128)(2,1)S(1)}, u32[]{:S(2)}, u32[]{:S(2)}) collective-permute-start(bf16[256,512]{1,0:T(8,128)(2,1)S(1)} %get-tuple-element.162), channel_id=1, source_target_pairs={{8,0},{9,1},{10,2},{11,3},{12,4},{13,5},{14,6},{15,7}} | collective-permute-start | bytes 786440 | tf_op jit(solution)/shard_map/ppermute | solution.py:417
  57.0 12.2 %collective-permute-start.19 = (bf16[256,512]{1,0:T(8,128)(2,1)S(1)}, bf16[256,512]{1,0:T(8,128)(2,1)S(1)}, u32[]{:S(2)}, u32[]{:S(2)}) collective-permute-start(bf16[256,512]{1,0:T(8,128)(2,1)S(1)} %get-tuple-element.161.refs_0_), channel_id=1, source_target_pairs={{8,0},{9,1},{10,2},{11,3},{12,4},{13,5},{14,6},{15,7}} | collective-permute-start | bytes 786440 | tf_op jit(solution)/shard_map/ppermute | solution.py:417
  58.4 13.7 %collective-permute-start.25 = (bf16[256,512]{1,0:T(8,128)(2,1)S(1)}, bf16[256,512]{1,0:T(8,128)(2,1)S(1)}, u32[]{:S(2)}, u32[]{:S(2)}) collective-permute-start(bf16[256,512]{1,0:T(8,128)(2,1)S(1)} %get-tuple-element.190), channel_id=1, source_target_pairs={{8,0},{9,1},{10,2},{11,3},{12,4},{13,5},{14,6},{15,7}} | collective-permute-start | bytes 786440 | tf_op jit(solution)/shard_map/ppermute | solution.py:417
  59.9 15.3 %collective-permute-start.24 = (bf16[256,512]{1,0:T(8,128)(2,1)S(1)}, bf16[256,512]{1,0:T(8,128)(2,1)S(1)}, u32[]{:S(2)}, u32[]{:S(2)}) collective-permute-start(bf16[256,512]{1,0:T(8,128)(2,1)S(1)} %get-tuple-element.189), channel_id=1, source_target_pairs={{8,0},{9,1},{10,2},{11,3},{12,4},{13,5},{14,6},{15,7}} | collective-permute-start | bytes 786440 | tf_op jit(solution)/shard_map/ppermute | solution.py:417
  77.6 8.8 %collective-permute-start.26 = (bf16[2,64,1024]{2,1,0:T(8,128)(2,1)S(1)}, bf16[2,64,1024]{2,1,0:T(8,128)(2,1)S(1)}, u32[]{:S(2)}, u32[]{:S(2)}) collective-permute-start(bf16[2,64,1024]{2,1,0:T(8,128)(2,1)S(1)} %get-tuple-element.205.refs_6_), channel_id=1, source_target_pairs={{0,2},{2,4},{4,6},{6,7},{7,5},{5,3},{3,1},{1,0},{8,10},{10,12},{12... | collective-permute-start | bytes 786440 | tf_op jit(solution)/shard_map/ppermute | solution.py:363
  79.0 8.5 %collective-permute-start.27 = (bf16[2,64,1024]{2,1,0:T(8,128)(2,1)S(1)}, bf16[2,64,1024]{2,1,0:T(8,128)(2,1)S(1)}, u32[]{:S(2)}, u32[]{:S(2)}) collective-permute-start(bf16[2,64,1024]{2,1,0:T(8,128)(2,1)S(1)} %get-tuple-element.208), channel_id=1, source_target_pairs={{2,0},{4,2},{6,4},{7,6},{5,7},{3,5},{1,3},{0,1},{10,8},{12,10},{14... | collective-permute-start | bytes 786440 | tf_op jit(solution)/shard_map/ppermute | solution.py:363
  81.8 10.1 %collective-permute-start.30 = (bf16[2,64,1024]{2,1,0:T(8,128)(2,1)S(1)}, bf16[2,64,1024]{2,1,0:T(8,128)(2,1)S(1)}, u32[]{:S(2)}, u32[]{:S(2)}) collective-permute-start(bf16[2,64,1024]{2,1,0:T(8,128)(2,1)S(1)} %get-tuple-element.215), channel_id=1, source_target_pairs={{0,2},{2,4},{4,6},{6,7},{7,5},{5,3},{3,1},{1,0},{8,10},{10,12},{12... | collective-permute-start | bytes 786440 | tf_op jit(solution)/shard_map/ppermute | solution.py:363
  83.3 9.8 %collective-permute-start.31 = (bf16[2,64,1024]{2,1,0:T(8,128)(2,1)S(1)}, bf16[2,64,1024]{2,1,0:T(8,128)(2,1)S(1)}, u32[]{:S(2)}, u32[]{:S(2)}) collective-permute-start(bf16[2,64,1024]{2,1,0:T(8,128)(2,1)S(1)} %get-tuple-element.216), channel_id=1, source_target_pairs={{2,0},{4,2},{6,4},{7,6},{5,7},{3,5},{1,3},{0,1},{10,8},{12,10},{14... | collective-permute-start | bytes 786440 | tf_op jit(solution)/shard_map/ppermute | solution.py:363
  87.6 10.0 %collective-permute-start.28 = (bf16[2,64,1024]{2,1,0:T(8,128)(2,1)S(1)}, bf16[2,64,1024]{2,1,0:T(8,128)(2,1)S(1)}, u32[]{:S(2)}, u32[]{:S(2)}) collective-permute-start(bf16[2,64,1024]{2,1,0:T(8,128)(2,1)S(1)} %get-tuple-element.209.refs_6_.refs_0_), channel_id=1, source_target_pairs={{0,2},{2,4},{4,6},{6,7},{7,5},{5,3},{3,1},{1,0},{8,10},{10,12},{12... | collective-permute-start | bytes 786440 | tf_op jit(solution)/shard_map/ppermute | solution.py:363
  89.2 9.5 %collective-permute-start.29 = (bf16[2,64,1024]{2,1,0:T(8,128)(2,1)S(1)}, bf16[2,64,1024]{2,1,0:T(8,128)(2,1)S(1)}, u32[]{:S(2)}, u32[]{:S(2)}) collective-permute-start(bf16[2,64,1024]{2,1,0:T(8,128)(2,1)S(1)} %get-tuple-element.212), channel_id=1, source_target_pairs={{2,0},{4,2},{6,4},{7,6},{5,7},{3,5},{1,3},{0,1},{10,8},{12,10},{14... | collective-permute-start | bytes 786440 | tf_op jit(solution)/shard_map/ppermute | solution.py:363
  93.3 10.0 %collective-permute-start.34 = (bf16[2,64,1024]{2,1,0:T(8,128)(2,1)S(1)}, bf16[2,64,1024]{2,1,0:T(8,128)(2,1)S(1)}, u32[]{:S(2)}, u32[]{:S(2)}) collective-permute-start(bf16[2,64,1024]{2,1,0:T(8,128)(2,1)S(1)} %get-tuple-element.217.refs_0_), channel_id=1, source_target_pairs={{0,2},{2,4},{4,6},{6,7},{7,5},{5,3},{3,1},{1,0},{8,10},{10,12},{12... | collective-permute-start | bytes 786440 | tf_op jit(solution)/shard_map/ppermute | solution.py:363
  94.8 9.5 %collective-permute-start.35 = (bf16[2,64,1024]{2,1,0:T(8,128)(2,1)S(1)}, bf16[2,64,1024]{2,1,0:T(8,128)(2,1)S(1)}, u32[]{:S(2)}, u32[]{:S(2)}) collective-permute-start(bf16[2,64,1024]{2,1,0:T(8,128)(2,1)S(1)} %get-tuple-element.224), channel_id=1, source_target_pairs={{2,0},{4,2},{6,4},{7,6},{5,7},{3,5},{1,3},{0,1},{10,8},{12,10},{14... | collective-permute-start | bytes 786440 | tf_op jit(solution)/shard_map/ppermute | solution.py:363
  98.9 10.0 %collective-permute-start.32 = (bf16[2,64,1024]{2,1,0:T(8,128)(2,1)S(1)}, bf16[2,64,1024]{2,1,0:T(8,128)(2,1)S(1)}, u32[]{:S(2)}, u32[]{:S(2)}) collective-permute-start(bf16[2,64,1024]{2,1,0:T(8,128)(2,1)S(1)} %get-tuple-element.218.refs_6_.refs_0_), channel_id=1, source_target_pairs={{0,2},{2,4},{4,6},{6,7},{7,5},{5,3},{3,1},{1,0},{8,10},{10,12},{12... | collective-permute-start | bytes 786440 | tf_op jit(solution)/shard_map/ppermute | solution.py:363
  100.4 9.5 %collective-permute-start.33 = (bf16[2,64,1024]{2,1,0:T(8,128)(2,1)S(1)}, bf16[2,64,1024]{2,1,0:T(8,128)(2,1)S(1)}, u32[]{:S(2)}, u32[]{:S(2)}) collective-permute-start(bf16[2,64,1024]{2,1,0:T(8,128)(2,1)S(1)} %get-tuple-element.221), channel_id=1, source_target_pairs={{2,0},{4,2},{6,4},{7,6},{5,7},{3,5},{1,3},{0,1},{10,8},{12,10},{14... | collective-permute-start | bytes 786440 | tf_op jit(solution)/shard_map/ppermute | solution.py:363
  104.5 11.1 %collective-permute-start.37 = (bf16[2,64,1024]{2,1,0:T(8,128)(2,1)S(1)}, bf16[2,64,1024]{2,1,0:T(8,128)(2,1)S(1)}, u32[]{:S(2)}, u32[]{:S(2)}) collective-permute-start(bf16[2,64,1024]{2,1,0:T(8,128)(2,1)S(1)} %get-tuple-element.229), channel_id=1, source_target_pairs={{2,0},{4,2},{6,4},{7,6},{5,7},{3,5},{1,3},{0,1},{10,8},{12,10},{14... | collective-permute-start | bytes 786440 | tf_op jit(solution)/shard_map/ppermute | solution.py:363
  105.2 10.4 %collective-permute-start.38 = (bf16[2,64,1024]{2,1,0:T(8,128)(2,1)S(1)}, bf16[2,64,1024]{2,1,0:T(8,128)(2,1)S(1)}, u32[]{:S(2)}, u32[]{:S(2)}) collective-permute-start(bf16[2,64,1024]{2,1,0:T(8,128)(2,1)S(1)} %get-tuple-element.225.refs_0_), channel_id=1, source_target_pairs={{0,2},{2,4},{4,6},{6,7},{7,5},{5,3},{3,1},{1,0},{8,10},{10,12},{12... | collective-permute-start | bytes 786440 | tf_op jit(solution)/shard_map/ppermute | solution.py:363
  110.1 8.1 %collective-permute-start.36 = (bf16[2,64,1024]{2,1,0:T(8,128)(2,1)S(1)}, bf16[2,64,1024]{2,1,0:T(8,128)(2,1)S(1)}, u32[]{:S(2)}, u32[]{:S(2)}) collective-permute-start(bf16[2,64,1024]{2,1,0:T(8,128)(2,1)S(1)} %get-tuple-element.226.refs_6_), channel_id=1, source_target_pairs={{0,2},{2,4},{4,6},{6,7},{7,5},{5,3},{3,1},{1,0},{8,10},{10,12},{12... | collective-permute-start | bytes 786440 | tf_op jit(solution)/shard_map/ppermute | solution.py:363
  111.7 7.6 %collective-permute-start.39 = (bf16[2,64,1024]{2,1,0:T(8,128)(2,1)S(1)}, bf16[2,64,1024]{2,1,0:T(8,128)(2,1)S(1)}, u32[]{:S(2)}, u32[]{:S(2)}) collective-permute-start(bf16[2,64,1024]{2,1,0:T(8,128)(2,1)S(1)} %get-tuple-element.230), channel_id=1, source_target_pairs={{2,0},{4,2},{6,4},{7,6},{5,7},{3,5},{1,3},{0,1},{10,8},{12,10},{14... | collective-permute-start | bytes 786440 | tf_op jit(solution)/shard_map/ppermute | solution.py:363
  (13 other events, 47.1 us)

commit v2 on v0

--- a/solution.py
+++ b/solution.py
@@ -289,7 +289,9 @@
     def mix_rows(m):
         return jnp.concatenate([hids[m][pl.ds(row, part), :] for row in places], axis=0)
 
-    @pl.loop(0, wide // step)
+    unroll = offsets == (replicas // 2,)
+
+    @pl.loop(0, wide // step, unroll=unroll)
     def _(j):
         columns = pl.ds(pl.multiple_of(j * step, step), step)
         conv = product(conv_rows, lambda m, at: pgs[m][:, at], columns)
@@ -299,7 +301,7 @@
                 at = (slot * 3 + k) * part
                 target[index, :, columns] = conv[at : at + part, :].astype(low.dtype)
 
-    @pl.loop(0, channels // step)
+    @pl.loop(0, channels // step, unroll=unroll)
     def _(j):
         columns = pl.ds(pl.multiple_of(j * step, step), step)
         after = pl.ds(pl.multiple_of(channels + j * step, step), step)

time: 121 us -> 120 us (level)
  no operation moved by 1% of the time
where the time goes in v2:
time: 120 us
  waiting for transfers between devices  46 us (38%)
  starting transfers between devices  42.3 us (35%)
  Pallas kernels  27.8 us (23%)
  local copies, waits for them, and re-layouts  1.32 us (1%)
    ppermute x15, starting transfers between devices, send(): lax.ppermute(to_right, 'dp', right)  24.4 us
    ppermute x15, waiting for transfers between devices, send(): lax.ppermute(to_left, 'dp', left)  21.5 us
    ppermute x15, waiting for transfers between devices, send(): lax.ppermute(to_right, 'dp', right)  15 us
    ppermute x8, waiting for transfers between devices, local(): g[m][half_at] = lax.ppermute(piece, 'pipe', [(stage, stage - 1)])  9.4 us
    pallas_call x5, Pallas kernels, term_call(): pl.pallas_call(functools.partial(term_kernel, replicas, offsets, micro),...  9.13 us
    ppermute x15, starting transfers between devices, send(): lax.ppermute(to_left, 'dp', left)  8.22 us
    ppermute x8, starting transfers between devices, local(): g[m][half_at] = lax.ppermute(piece, 'pipe', [(stage, stage - 1)])  8.1 us
    pallas_call x7, Pallas kernels, partial_call(): pl.pallas_call(functools.partial(partial_kernel, replicas, items, not hel...  6.69 us
  transfers between devices with their start and end apart: 40, of which 29 were waited for; matrix products, arithmetic and copies ran while one was open for 1% of the time, Pallas kernels for 19%

profile of v2, /device:TPU:0, one launch (start us, length us, event | category | flops | bytes accessed | tf_op | source)
XLA Modules:
  0.0 119.5 jit_solution(4550001131053655040)
XLA Ops:
  1.7 3.1 %collective-permute-start.2 = (bf16[2,64,1024]{2,1,0:T(8,128)(2,1)S(1)}, bf16[2,64,1024]{2,1,0:T(8,128)(2,1)S(1)}, u32[]{:S(2)}, u32[]{:S(2)}) collective-permute-start(bf16[2,64,1024]{2,1,0:T(8,128)(2,1)S(1)} %get-tuple-element.121.refs_0_), channel_id=1, source_target_pairs={{0,2},{2,4},{4,6},{6,7},{7,5},{5,3},{3,1},{1,0},{8,10},{10,12},{12... | collective-permute-start | bytes 786440 | tf_op jit(solution)/shard_map/ppermute | solution.py:378
  4.8 2.0 %collective-permute-start = (bf16[2,64,1024]{2,1,0:T(8,128)(2,1)S(1)}, bf16[2,64,1024]{2,1,0:T(8,128)(2,1)S(1)}, u32[]{:S(2)}, u32[]{:S(2)}) collective-permute-start(bf16[2,64,1024]{2,1,0:T(8,128)(2,1)S(1)} %get-tuple-element.120.refs_1_), channel_id=1, source_target_pairs={{0,2},{2,4},{4,6},{6,7},{7,5},{5,3},{3,1},{1,0},{8,10},{10,12},{12... | collective-permute-start | bytes 786440 | tf_op jit(solution)/shard_map/ppermute | solution.py:378
  10.2 1.7 %collective-permute-done.2.refs_0_ = bf16[2,64,1024]{2,1,0:T(8,128)(2,1)S(1)} collective-permute-done((bf16[2,64,1024]{2,1,0:T(8,128)(2,1)S(1)}, bf16[2,64,1024]{2,1,0:T(8,128)(2,1)S(1)}, u32[]{:S(2)}, u32[]{:S(2)}) %collective-permute-start.2) | collective-permute-done | bytes 262176 | tf_op jit(solution)/shard_map/ppermute | solution.py:378
  11.9 2.2 %collective-permute-done.3.refs_1_ = bf16[2,64,1024]{2,1,0:T(8,128)(2,1)S(1)} collective-permute-done((bf16[2,64,1024]{2,1,0:T(8,128)(2,1)S(1)}, bf16[2,64,1024]{2,1,0:T(8,128)(2,1)S(1)}, u32[]{:S(2)}, u32[]{:S(2)}) %collective-permute-start.3) | collective-permute-done | bytes 262176 | tf_op jit(solution)/shard_map/ppermute | solution.py:378
  15.0 1.6 %collective-permute-start.6 = (bf16[2,64,1024]{2,1,0:T(8,128)(2,1)S(1)}, bf16[2,64,1024]{2,1,0:T(8,128)(2,1)S(1)}, u32[]{:S(2)}, u32[]{:S(2)}) collective-permute-start(bf16[2,64,1024]{2,1,0:T(8,128)(2,1)S(1)} %get-tuple-element.128), channel_id=1, source_target_pairs={{0,2},{2,4},{4,6},{6,7},{7,5},{5,3},{3,1},{1,0},{8,10},{10,12},{12... | collective-permute-start | bytes 786440 | tf_op jit(solution)/shard_map/ppermute | solution.py:378
  17.5 2.2 %collective-permute-done.1.refs_1_ = bf16[2,64,1024]{2,1,0:T(8,128)(2,1)S(1)} collective-permute-done((bf16[2,64,1024]{2,1,0:T(8,128)(2,1)S(1)}, bf16[2,64,1024]{2,1,0:T(8,128)(2,1)S(1)}, u32[]{:S(2)}, u32[]{:S(2)}) %collective-permute-start.1) | collective-permute-done | bytes 262176 | tf_op jit(solution)/shard_map/ppermute | solution.py:378
  20.6 1.6 %collective-permute-start.4 = (bf16[2,64,1024]{2,1,0:T(8,128)(2,1)S(1)}, bf16[2,64,1024]{2,1,0:T(8,128)(2,1)S(1)}, u32[]{:S(2)}, u32[]{:S(2)}) collective-permute-start(bf16[2,64,1024]{2,1,0:T(8,128)(2,1)S(1)} %get-tuple-element.126), channel_id=1, source_target_pairs={{0,2},{2,4},{4,6},{6,7},{7,5},{5,3},{3,1},{1,0},{8,10},{10,12},{12... | collective-permute-start | bytes 786440 | tf_op jit(solution)/shard_map/ppermute | solution.py:378
  24.1 1.7 %collective-permute-done.7.refs_1_ = bf16[2,64,1024]{2,1,0:T(8,128)(2,1)S(1)} collective-permute-done((bf16[2,64,1024]{2,1,0:T(8,128)(2,1)S(1)}, bf16[2,64,1024]{2,1,0:T(8,128)(2,1)S(1)}, u32[]{:S(2)}, u32[]{:S(2)}) %collective-permute-start.7) | collective-permute-done | bytes 262176 | tf_op jit(solution)/shard_map/ppermute | solution.py:378
  26.8 1.6 %collective-permute-start.10 = (bf16[2,64,1024]{2,1,0:T(8,128)(2,1)S(1)}, bf16[2,64,1024]{2,1,0:T(8,128)(2,1)S(1)}, u32[]{:S(2)}, u32[]{:S(2)}) collective-permute-start(bf16[2,64,1024]{2,1,0:T(8,128)(2,1)S(1)} %get-tuple-element.136), channel_id=1, source_target_pairs={{0,2},{2,4},{4,6},{6,7},{7,5},{5,3},{3,1},{1,0},{8,10},{10,12},{12... | collective-permute-start | bytes 786440 | tf_op jit(solution)/shard_map/ppermute | solution.py:378
  29.9 1.5 %collective-permute-done.5.refs_1_ = bf16[2,64,1024]{2,1,0:T(8,128)(2,1)S(1)} collective-permute-done((bf16[2,64,1024]{2,1,0:T(8,128)(2,1)S(1)}, bf16[2,64,1024]{2,1,0:T(8,128)(2,1)S(1)}, u32[]{:S(2)}, u32[]{:S(2)}) %collective-permute-start.5) | collective-permute-done | bytes 262176 | tf_op jit(solution)/shard_map/ppermute | solution.py:378
  32.4 1.6 %collective-permute-start.8 = (bf16[2,64,1024]{2,1,0:T(8,128)(2,1)S(1)}, bf16[2,64,1024]{2,1,0:T(8,128)(2,1)S(1)}, u32[]{:S(2)}, u32[]{:S(2)}) collective-permute-start(bf16[2,64,1024]{2,1,0:T(8,128)(2,1)S(1)} %get-tuple-element.134), channel_id=1, source_target_pairs={{0,2},{2,4},{4,6},{6,7},{7,5},{5,3},{3,1},{1,0},{8,10},{10,12},{12... | collective-permute-start | bytes 786440 | tf_op jit(solution)/shard_map/ppermute | solution.py:378
  35.9 1.7 %collective-permute-done.11.refs_1_ = bf16[2,64,1024]{2,1,0:T(8,128)(2,1)S(1)} collective-permute-done((bf16[2,64,1024]{2,1,0:T(8,128)(2,1)S(1)}, bf16[2,64,1024]{2,1,0:T(8,128)(2,1)S(1)}, u32[]{:S(2)}, u32[]{:S(2)}) %collective-permute-start.11) | collective-permute-done | bytes 262176 | tf_op jit(solution)/shard_map/ppermute | solution.py:378
  40.8 2.5 %collective-permute-start.14 = (bf16[1,64,1024]{2,1,0:T(8,128)(2,1)S(1)}, bf16[1,64,1024]{2,1,0:T(8,128)(2,1)S(1)}, u32[]{:S(2)}, u32[]{:S(2)}) collective-permute-start(bf16[1,64,1024]{2,1,0:T(8,128)(2,1)S(1)} %slice.10), channel_id=1, source_target_pairs={{0,2},{2,4},{4,6},{6,7},{7,5},{5,3},{3,1},{1,0},{8,10},{10,12},{12... | collective-permute-start | bytes 393224 | tf_op jit(solution)/shard_map/ppermute | solution.py:378
  46.0 2.4 %collective-permute-done.15.refs_1_ = bf16[1,64,1024]{2,1,0:T(8,128)(2,1)S(1)} collective-permute-done((bf16[1,64,1024]{2,1,0:T(8,128)(2,1)S(1)}, bf16[1,64,1024]{2,1,0:T(8,128)(2,1)S(1)}, u32[]{:S(2)}, u32[]{:S(2)}) %collective-permute-start.15) | collective-permute-done | bytes 131104 | tf_op jit(solution)/shard_map/ppermute | solution.py:378
  57.3 1.5 %collective-permute-start.25 = (bf16[256,512]{1,0:T(8,128)(2,1)S(1)}, bf16[256,512]{1,0:T(8,128)(2,1)S(1)}, u32[]{:S(2)}, u32[]{:S(2)}) collective-permute-start(bf16[256,512]{1,0:T(8,128)(2,1)S(1)} %get-tuple-element.194), channel_id=1, source_target_pairs={{8,0},{9,1},{10,2},{11,3},{12,4},{13,5},{14,6},{15,7}} | collective-permute-start | bytes 786440 | tf_op jit(solution)/shard_map/ppermute | solution.py:429
  60.2 5.1 %collective-permute-done.20.g = bf16[256,512]{1,0:T(8,128)(2,1)S(1)} collective-permute-done((bf16[256,512]{1,0:T(8,128)(2,1)S(1)}, bf16[256,512]{1,0:T(8,128)(2,1)S(1)}, u32[]{:S(2)}, u32[]{:S(2)}) %collective-permute-start.20) | collective-permute-done | bytes 262176 | tf_op jit(solution)/shard_map/ppermute | solution.py:429
  65.3 1.5 %shard_map.91 = (bf16[512,1024]{1,0:T(8,128)(2,1)S(1)}, bf16[512,512]{1,0:T(8,128)(2,1)S(1)}, bf16[512,512]{1,0:T(8,128)(2,1)S(1)}, f32[2,16,512]{2,1,0:T(8,128)S(1)}) custom-call(bf16[256,512]{1,0:T(8,128)(2,1)S(1)} %collective-permute-done.20.g, bf16[2,512,512]{2,1,0:T(8,128)(2,1)S(1)} %bitcast.30, ...), custom_call_target="tpu_custom_call", output_to_operand_aliasing={{0}: (5, {}), {1}: (6, {}), {2}: (7, {})} | custom-call | flops 536870912 | bytes 4194304 | tf_op jit(solution)/shard_map/pallas_call | solution.py:255
  68.2 1.5 %shard_map.92 = (bf16[512,1024]{1,0:T(8,128)(2,1)S(1)}, bf16[512,512]{1,0:T(8,128)(2,1)S(1)}, bf16[512,512]{1,0:T(8,128)(2,1)S(1)}) custom-call(bf16[256,512]{1,0:T(8,128)(2,1)S(1)} %collective-permute-done.19.g, bf16[2,512,512]{2,1,0:T(8,128)(2,1)S(1)} %bitcast.31, ...), custom_call_target="tpu_custom_call", output_to_operand_aliasing={{0}: (6, {}), {1}: (7, {}), {2}: (8, {})} | custom-call | flops 536870912 | bytes 4194304 | tf_op jit(solution)/shard_map/pallas_call | solution.py:255
  71.0 1.5 %shard_map.99 = (bf16[512,1024]{1,0:T(8,128)(2,1)S(1)}, bf16[512,512]{1,0:T(8,128)(2,1)S(1)}, bf16[512,512]{1,0:T(8,128)(2,1)S(1)}, f32[2,16,512]{2,1,0:T(8,128)S(1)}) custom-call(bf16[256,512]{1,0:T(8,128)(2,1)S(1)} %collective-permute-done.25.g, bf16[2,512,512]{2,1,0:T(8,128)(2,1)S(1)} %bitcast.32, ...), custom_call_target="tpu_custom_call", output_to_operand_aliasing={{0}: (6, {}), {1}: (7, {}), {2}: (8, {})} | custom-call | flops 536870912 | bytes 4194304 | tf_op jit(solution)/shard_map/pallas_call | solution.py:255
  72.5 1.6 %collective-permute-done.24.g = bf16[256,512]{1,0:T(8,128)(2,1)S(1)} collective-permute-done((bf16[256,512]{1,0:T(8,128)(2,1)S(1)}, bf16[256,512]{1,0:T(8,128)(2,1)S(1)}, u32[]{:S(2)}, u32[]{:S(2)}) %collective-permute-start.24) | collective-permute-done | bytes 262176 | tf_op jit(solution)/shard_map/ppermute | solution.py:429
  74.1 1.5 %shard_map.100 = (bf16[512,1024]{1,0:T(8,128)(2,1)S(1)}, bf16[512,512]{1,0:T(8,128)(2,1)S(1)}, bf16[512,512]{1,0:T(8,128)(2,1)S(1)}) custom-call(bf16[256,512]{1,0:T(8,128)(2,1)S(1)} %collective-permute-done.24.g, bf16[2,512,512]{2,1,0:T(8,128)(2,1)S(1)} %bitcast.33, ...), custom_call_target="tpu_custom_call", output_to_operand_aliasing={{0}: (6, {}), {1}: (7, {}), {2}: (8, {})} | custom-call | flops 536870912 | bytes 4194304 | tf_op jit(solution)/shard_map/pallas_call | solution.py:255
  76.5 1.7 %collective-permute-start.26 = (bf16[2,64,1024]{2,1,0:T(8,128)(2,1)S(1)}, bf16[2,64,1024]{2,1,0:T(8,128)(2,1)S(1)}, u32[]{:S(2)}, u32[]{:S(2)}) collective-permute-start(bf16[2,64,1024]{2,1,0:T(8,128)(2,1)S(1)} %get-tuple-element.209.refs_6_), channel_id=1, source_target_pairs={{0,2},{2,4},{4,6},{6,7},{7,5},{5,3},{3,1},{1,0},{8,10},{10,12},{12... | collective-permute-start | bytes 786440 | tf_op jit(solution)/shard_map/ppermute | solution.py:378
  78.6 2.2 %shard_map.102 = (bf16[2,64,1024]{2,1,0:T(8,128)(2,1)S(1)}, bf16[2,64,1024]{2,1,0:T(8,128)(2,1)S(1)}, bf16[2,64,1024]{2,1,0:T(8,128)(2,1)S(1)}, bf16[2,64,1024]{2,1,0:T(8,128)(2,1)S(1)}) custom-call(bf16[1536,1024]{1,0:T(8,128)(2,1)S(1)} %shard_map.76.taps_t, bf16[2,512,512]{2,1,0:T(8,128)(2,1)S(1)} %bitcast.35, ...), custom_call_target="tpu_custom_call" | custom-call | flops 1073741824 | bytes 1048576 | tf_op jit(solution)/shard_map/pallas_call | solution.py:322
  80.8 1.7 %collective-permute-start.30 = (bf16[2,64,1024]{2,1,0:T(8,128)(2,1)S(1)}, bf16[2,64,1024]{2,1,0:T(8,128)(2,1)S(1)}, u32[]{:S(2)}, u32[]{:S(2)}) collective-permute-start(bf16[2,64,1024]{2,1,0:T(8,128)(2,1)S(1)} %get-tuple-element.219), channel_id=1, source_target_pairs={{0,2},{2,4},{4,6},{6,7},{7,5},{5,3},{3,1},{1,0},{8,10},{10,12},{12... | collective-permute-start | bytes 786440 | tf_op jit(solution)/shard_map/ppermute | solution.py:378
  82.9 2.4 %collective-permute-done.26.got_r = bf16[2,64,1024]{2,1,0:T(8,128)(2,1)S(1)} collective-permute-done((bf16[2,64,1024]{2,1,0:T(8,128)(2,1)S(1)}, bf16[2,64,1024]{2,1,0:T(8,128)(2,1)S(1)}, u32[]{:S(2)}, u32[]{:S(2)}) %collective-permute-start.26) | collective-permute-done | bytes 262176 | tf_op jit(solution)/shard_map/ppermute | solution.py:378
  88.9 2.2 %shard_map.104 = (bf16[2,64,1024]{2,1,0:T(8,128)(2,1)S(1)}, bf16[2,64,1024]{2,1,0:T(8,128)(2,1)S(1)}, bf16[2,64,1024]{2,1,0:T(8,128)(2,1)S(1)}, bf16[2,64,1024]{2,1,0:T(8,128)(2,1)S(1)}) custom-call(bf16[1536,1024]{1,0:T(8,128)(2,1)S(1)} %shard_map.76.taps_t, bf16[2,512,512]{2,1,0:T(8,128)(2,1)S(1)} %bitcast.36, ...), custom_call_target="tpu_custom_call" | custom-call | flops 1073741824 | bytes 1048576 | tf_op jit(solution)/shard_map/pallas_call | solution.py:322
  94.5 2.0 %collective-permute-done.28.got_r = bf16[2,64,1024]{2,1,0:T(8,128)(2,1)S(1)} collective-permute-done((bf16[2,64,1024]{2,1,0:T(8,128)(2,1)S(1)}, bf16[2,64,1024]{2,1,0:T(8,128)(2,1)S(1)}, u32[]{:S(2)}, u32[]{:S(2)}) %collective-permute-start.28) | collective-permute-done | bytes 262176 | tf_op jit(solution)/shard_map/ppermute | solution.py:378
  100.1 2.2 %shard_map.107 = (bf16[2,64,1024]{2,1,0:T(8,128)(2,1)S(1)}, bf16[2,64,1024]{2,1,0:T(8,128)(2,1)S(1)}, bf16[2,64,1024]{2,1,0:T(8,128)(2,1)S(1)}, bf16[2,64,1024]{2,1,0:T(8,128)(2,1)S(1)}) custom-call(bf16[1536,1024]{1,0:T(8,128)(2,1)S(1)} %shard_map.76.taps_t, bf16[2,512,512]{2,1,0:T(8,128)(2,1)S(1)} %bitcast.37, ...), custom_call_target="tpu_custom_call" | custom-call | flops 1073741824 | bytes 1048576 | tf_op jit(solution)/shard_map/pallas_call | solution.py:322
  104.1 1.6 %collective-permute-start.38 = (bf16[2,64,1024]{2,1,0:T(8,128)(2,1)S(1)}, bf16[2,64,1024]{2,1,0:T(8,128)(2,1)S(1)}, u32[]{:S(2)}, u32[]{:S(2)}) collective-permute-start(bf16[2,64,1024]{2,1,0:T(8,128)(2,1)S(1)} %get-tuple-element.229.refs_0_), channel_id=1, source_target_pairs={{0,2},{2,4},{4,6},{6,7},{7,5},{5,3},{3,1},{1,0},{8,10},{10,12},{12... | collective-permute-start | bytes 786440 | tf_op jit(solution)/shard_map/ppermute | solution.py:378
  105.8 2.0 %collective-permute-done.32.got_r = bf16[2,64,1024]{2,1,0:T(8,128)(2,1)S(1)} collective-permute-done((bf16[2,64,1024]{2,1,0:T(8,128)(2,1)S(1)}, bf16[2,64,1024]{2,1,0:T(8,128)(2,1)S(1)}, u32[]{:S(2)}, u32[]{:S(2)}) %collective-permute-start.32) | collective-permute-done | bytes 262176 | tf_op jit(solution)/shard_map/ppermute | solution.py:378
  112.4 1.7 %shard_map.110 = (f32[2,64,1024]{2,1,0:T(8,128)S(1)}, f32[2,64,1024]{2,1,0:T(8,128)S(1)}) custom-call(bf16[1536,1024]{1,0:T(8,128)(2,1)S(1)} %shard_map.76.taps_t, bf16[2,512,512]{2,1,0:T(8,128)(2,1)S(1)} %bitcast.38, bf16[512,512]{1,0:T(8,128)(2,1)S(1)} %get-tuple-element.203.refs_0_, bf16[512,512]{1,0:T(8,128)(2,1)S(1)} %get-tuple-element.204.refs_1_, ...), custom_call_target="tpu_custom_call" | custom-call | flops 536870912 | bytes 1048576 | tf_op jit(solution)/shard_map/pallas_call | solution.py:322
  114.8 2.3 %collective-permute-done.36.low_r = bf16[2,64,1024]{2,1,0:T(8,128)(2,1)S(1)} collective-permute-done((bf16[2,64,1024]{2,1,0:T(8,128)(2,1)S(1)}, bf16[2,64,1024]{2,1,0:T(8,128)(2,1)S(1)}, u32[]{:S(2)}, u32[]{:S(2)}) %collective-permute-start.36) | collective-permute-done | bytes 262176 | tf_op jit(solution)/shard_map/ppermute | solution.py:378
  (94 shorter events, 54.7 us)
Async XLA Ops:
  1.7 10.2 %collective-permute-start.2 = (bf16[2,64,1024]{2,1,0:T(8,128)(2,1)S(1)}, bf16[2,64,1024]{2,1,0:T(8,128)(2,1)S(1)}, u32[]{:S(2)}, u32[]{:S(2)}) collective-permute-start(bf16[2,64,1024]{2,1,0:T(8,128)(2,1)S(1)} %get-tuple-element.121.refs_0_), channel_id=1, source_target_pairs={{0,2},{2,4},{4,6},{6,7},{7,5},{5,3},{3,1},{1,0},{8,10},{10,12},{12... | collective-permute-start | bytes 786440 | tf_op jit(solution)/shard_map/ppermute | solution.py:378
  4.8 9.2 %collective-permute-start.3 = (bf16[2,64,1024]{2,1,0:T(8,128)(2,1)S(1)}, bf16[2,64,1024]{2,1,0:T(8,128)(2,1)S(1)}, u32[]{:S(2)}, u32[]{:S(2)}) collective-permute-start(bf16[2,64,1024]{2,1,0:T(8,128)(2,1)S(1)} %get-tuple-element.121.refs_0_), channel_id=1, source_target_pairs={{2,0},{4,2},{6,4},{7,6},{5,7},{3,5},{1,3},{0,1},{10,8},{12,10},{14... | collective-permute-start | bytes 786440 | tf_op jit(solution)/shard_map/ppermute | solution.py:378
  4.8 12.7 %collective-permute-start = (bf16[2,64,1024]{2,1,0:T(8,128)(2,1)S(1)}, bf16[2,64,1024]{2,1,0:T(8,128)(2,1)S(1)}, u32[]{:S(2)}, u32[]{:S(2)}) collective-permute-start(bf16[2,64,1024]{2,1,0:T(8,128)(2,1)S(1)} %get-tuple-element.120.refs_1_), channel_id=1, source_target_pairs={{0,2},{2,4},{4,6},{6,7},{7,5},{5,3},{3,1},{1,0},{8,10},{10,12},{12... | collective-permute-start | bytes 786440 | tf_op jit(solution)/shard_map/ppermute | solution.py:378
  6.8 12.8 %collective-permute-start.1 = (bf16[2,64,1024]{2,1,0:T(8,128)(2,1)S(1)}, bf16[2,64,1024]{2,1,0:T(8,128)(2,1)S(1)}, u32[]{:S(2)}, u32[]{:S(2)}) collective-permute-start(bf16[2,64,1024]{2,1,0:T(8,128)(2,1)S(1)} %get-tuple-element.120.refs_1_), channel_id=1, source_target_pairs={{2,0},{4,2},{6,4},{7,6},{5,7},{3,5},{1,3},{0,1},{10,8},{12,10},{14... | collective-permute-start | bytes 786440 | tf_op jit(solution)/shard_map/ppermute | solution.py:378
  15.0 9.0 %collective-permute-start.6 = (bf16[2,64,1024]{2,1,0:T(8,128)(2,1)S(1)}, bf16[2,64,1024]{2,1,0:T(8,128)(2,1)S(1)}, u32[]{:S(2)}, u32[]{:S(2)}) collective-permute-start(bf16[2,64,1024]{2,1,0:T(8,128)(2,1)S(1)} %get-tuple-element.128), channel_id=1, source_target_pairs={{0,2},{2,4},{4,6},{6,7},{7,5},{5,3},{3,1},{1,0},{8,10},{10,12},{12... | collective-permute-start | bytes 786440 | tf_op jit(solution)/shard_map/ppermute | solution.py:378
  16.6 9.2 %collective-permute-start.7 = (bf16[2,64,1024]{2,1,0:T(8,128)(2,1)S(1)}, bf16[2,64,1024]{2,1,0:T(8,128)(2,1)S(1)}, u32[]{:S(2)}, u32[]{:S(2)}) collective-permute-start(bf16[2,64,1024]{2,1,0:T(8,128)(2,1)S(1)} %get-tuple-element.129), channel_id=1, source_target_pairs={{2,0},{4,2},{6,4},{7,6},{5,7},{3,5},{1,3},{0,1},{10,8},{12,10},{14... | collective-permute-start | bytes 786440 | tf_op jit(solution)/shard_map/ppermute | solution.py:378
  20.6 9.3 %collective-permute-start.4 = (bf16[2,64,1024]{2,1,0:T(8,128)(2,1)S(1)}, bf16[2,64,1024]{2,1,0:T(8,128)(2,1)S(1)}, u32[]{:S(2)}, u32[]{:S(2)}) collective-permute-start(bf16[2,64,1024]{2,1,0:T(8,128)(2,1)S(1)} %get-tuple-element.126), channel_id=1, source_target_pairs={{0,2},{2,4},{4,6},{6,7},{7,5},{5,3},{3,1},{1,0},{8,10},{10,12},{12... | collective-permute-start | bytes 786440 | tf_op jit(solution)/shard_map/ppermute | solution.py:378
  22.2 9.2 %collective-permute-start.5 = (bf16[2,64,1024]{2,1,0:T(8,128)(2,1)S(1)}, bf16[2,64,1024]{2,1,0:T(8,128)(2,1)S(1)}, u32[]{:S(2)}, u32[]{:S(2)}) collective-permute-start(bf16[2,64,1024]{2,1,0:T(8,128)(2,1)S(1)} %get-tuple-element.127), channel_id=1, source_target_pairs={{2,0},{4,2},{6,4},{7,6},{5,7},{3,5},{1,3},{0,1},{10,8},{12,10},{14... | collective-permute-start | bytes 786440 | tf_op jit(solution)/shard_map/ppermute | solution.py:378
  26.8 9.1 %collective-permute-start.10 = (bf16[2,64,1024]{2,1,0:T(8,128)(2,1)S(1)}, bf16[2,64,1024]{2,1,0:T(8,128)(2,1)S(1)}, u32[]{:S(2)}, u32[]{:S(2)}) collective-permute-start(bf16[2,64,1024]{2,1,0:T(8,128)(2,1)S(1)} %get-tuple-element.136), channel_id=1, source_target_pairs={{0,2},{2,4},{4,6},{6,7},{7,5},{5,3},{3,1},{1,0},{8,10},{10,12},{12... | collective-permute-start | bytes 786440 | tf_op jit(solution)/shard_map/ppermute | solution.py:378
  28.4 9.2 %collective-permute-start.11 = (bf16[2,64,1024]{2,1,0:T(8,128)(2,1)S(1)}, bf16[2,64,1024]{2,1,0:T(8,128)(2,1)S(1)}, u32[]{:S(2)}, u32[]{:S(2)}) collective-permute-start(bf16[2,64,1024]{2,1,0:T(8,128)(2,1)S(1)} %get-tuple-element.137), channel_id=1, source_target_pairs={{2,0},{4,2},{6,4},{7,6},{5,7},{3,5},{1,3},{0,1},{10,8},{12,10},{14... | collective-permute-start | bytes 786440 | tf_op jit(solution)/shard_map/ppermute | solution.py:378
  32.4 8.4 %collective-permute-start.8 = (bf16[2,64,1024]{2,1,0:T(8,128)(2,1)S(1)}, bf16[2,64,1024]{2,1,0:T(8,128)(2,1)S(1)}, u32[]{:S(2)}, u32[]{:S(2)}) collective-permute-start(bf16[2,64,1024]{2,1,0:T(8,128)(2,1)S(1)} %get-tuple-element.134), channel_id=1, source_target_pairs={{0,2},{2,4},{4,6},{6,7},{7,5},{5,3},{3,1},{1,0},{8,10},{10,12},{12... | collective-permute-start | bytes 786440 | tf_op jit(solution)/shard_map/ppermute | solution.py:378
  34.0 9.4 %collective-permute-start.9 = (bf16[2,64,1024]{2,1,0:T(8,128)(2,1)S(1)}, bf16[2,64,1024]{2,1,0:T(8,128)(2,1)S(1)}, u32[]{:S(2)}, u32[]{:S(2)}) collective-permute-start(bf16[2,64,1024]{2,1,0:T(8,128)(2,1)S(1)} %get-tuple-element.135), channel_id=1, source_target_pairs={{2,0},{4,2},{6,4},{7,6},{5,7},{3,5},{1,3},{0,1},{10,8},{12,10},{14... | collective-permute-start | bytes 786440 | tf_op jit(solution)/shard_map/ppermute | solution.py:378
  38.6 5.0 %collective-permute-start.12 = (bf16[1,64,1024]{2,1,0:T(8,128)(2,1)S(1)}, bf16[1,64,1024]{2,1,0:T(8,128)(2,1)S(1)}, u32[]{:S(2)}, u32[]{:S(2)}) collective-permute-start(bf16[1,64,1024]{2,1,0:T(8,128)(2,1)S(1)} %get-tuple-element.140), channel_id=1, source_target_pairs={{0,2},{2,4},{4,6},{6,7},{7,5},{5,3},{3,1},{1,0},{8,10},{10,12},{12... | collective-permute-start | bytes 393224 | tf_op jit(solution)/shard_map/ppermute | solution.py:378
  40.8 5.2 %collective-permute-start.14 = (bf16[1,64,1024]{2,1,0:T(8,128)(2,1)S(1)}, bf16[1,64,1024]{2,1,0:T(8,128)(2,1)S(1)}, u32[]{:S(2)}, u32[]{:S(2)}) collective-permute-start(bf16[1,64,1024]{2,1,0:T(8,128)(2,1)S(1)} %slice.10), channel_id=1, source_target_pairs={{0,2},{2,4},{4,6},{6,7},{7,5},{5,3},{3,1},{1,0},{8,10},{10,12},{12... | collective-permute-start | bytes 393224 | tf_op jit(solution)/shard_map/ppermute | solution.py:378
  54.6 10.7 %collective-permute-start.20 = (bf16[256,512]{1,0:T(8,128)(2,1)S(1)}, bf16[256,512]{1,0:T(8,128)(2,1)S(1)}, u32[]{:S(2)}, u32[]{:S(2)}) collective-permute-start(bf16[256,512]{1,0:T(8,128)(2,1)S(1)} %get-tuple-element.166), channel_id=1, source_target_pairs={{8,0},{9,1},{10,2},{11,3},{12,4},{13,5},{14,6},{15,7}} | collective-permute-start | bytes 786440 | tf_op jit(solution)/shard_map/ppermute | solution.py:429
  56.0 12.2 %collective-permute-start.19 = (bf16[256,512]{1,0:T(8,128)(2,1)S(1)}, bf16[256,512]{1,0:T(8,128)(2,1)S(1)}, u32[]{:S(2)}, u32[]{:S(2)}) collective-permute-start(bf16[256,512]{1,0:T(8,128)(2,1)S(1)} %get-tuple-element.165.refs_0_), channel_id=1, source_target_pairs={{8,0},{9,1},{10,2},{11,3},{12,4},{13,5},{14,6},{15,7}} | collective-permute-start | bytes 786440 | tf_op jit(solution)/shard_map/ppermute | solution.py:429
  57.3 13.7 %collective-permute-start.25 = (bf16[256,512]{1,0:T(8,128)(2,1)S(1)}, bf16[256,512]{1,0:T(8,128)(2,1)S(1)}, u32[]{:S(2)}, u32[]{:S(2)}) collective-permute-start(bf16[256,512]{1,0:T(8,128)(2,1)S(1)} %get-tuple-element.194), channel_id=1, source_target_pairs={{8,0},{9,1},{10,2},{11,3},{12,4},{13,5},{14,6},{15,7}} | collective-permute-start | bytes 786440 | tf_op jit(solution)/shard_map/ppermute | solution.py:429
  58.9 15.2 %collective-permute-start.24 = (bf16[256,512]{1,0:T(8,128)(2,1)S(1)}, bf16[256,512]{1,0:T(8,128)(2,1)S(1)}, u32[]{:S(2)}, u32[]{:S(2)}) collective-permute-start(bf16[256,512]{1,0:T(8,128)(2,1)S(1)} %get-tuple-element.193), channel_id=1, source_target_pairs={{8,0},{9,1},{10,2},{11,3},{12,4},{13,5},{14,6},{15,7}} | collective-permute-start | bytes 786440 | tf_op jit(solution)/shard_map/ppermute | solution.py:429
  76.5 8.8 %collective-permute-start.26 = (bf16[2,64,1024]{2,1,0:T(8,128)(2,1)S(1)}, bf16[2,64,1024]{2,1,0:T(8,128)(2,1)S(1)}, u32[]{:S(2)}, u32[]{:S(2)}) collective-permute-start(bf16[2,64,1024]{2,1,0:T(8,128)(2,1)S(1)} %get-tuple-element.209.refs_6_), channel_id=1, source_target_pairs={{0,2},{2,4},{4,6},{6,7},{7,5},{5,3},{3,1},{1,0},{8,10},{10,12},{12... | collective-permute-start | bytes 786440 | tf_op jit(solution)/shard_map/ppermute | solution.py:378
  78.2 8.5 %collective-permute-start.27 = (bf16[2,64,1024]{2,1,0:T(8,128)(2,1)S(1)}, bf16[2,64,1024]{2,1,0:T(8,128)(2,1)S(1)}, u32[]{:S(2)}, u32[]{:S(2)}) collective-permute-start(bf16[2,64,1024]{2,1,0:T(8,128)(2,1)S(1)} %get-tuple-element.212), channel_id=1, source_target_pairs={{2,0},{4,2},{6,4},{7,6},{5,7},{3,5},{1,3},{0,1},{10,8},{12,10},{14... | collective-permute-start | bytes 786440 | tf_op jit(solution)/shard_map/ppermute | solution.py:378
  80.8 10.3 %collective-permute-start.30 = (bf16[2,64,1024]{2,1,0:T(8,128)(2,1)S(1)}, bf16[2,64,1024]{2,1,0:T(8,128)(2,1)S(1)}, u32[]{:S(2)}, u32[]{:S(2)}) collective-permute-start(bf16[2,64,1024]{2,1,0:T(8,128)(2,1)S(1)} %get-tuple-element.219), channel_id=1, source_target_pairs={{0,2},{2,4},{4,6},{6,7},{7,5},{5,3},{3,1},{1,0},{8,10},{10,12},{12... | collective-permute-start | bytes 786440 | tf_op jit(solution)/shard_map/ppermute | solution.py:378
  82.5 9.8 %collective-permute-start.31 = (bf16[2,64,1024]{2,1,0:T(8,128)(2,1)S(1)}, bf16[2,64,1024]{2,1,0:T(8,128)(2,1)S(1)}, u32[]{:S(2)}, u32[]{:S(2)}) collective-permute-start(bf16[2,64,1024]{2,1,0:T(8,128)(2,1)S(1)} %get-tuple-element.220), channel_id=1, source_target_pairs={{2,0},{4,2},{6,4},{7,6},{5,7},{3,5},{1,3},{0,1},{10,8},{12,10},{14... | collective-permute-start | bytes 786440 | tf_op jit(solution)/shard_map/ppermute | solution.py:378
  86.8 9.7 %collective-permute-start.28 = (bf16[2,64,1024]{2,1,0:T(8,128)(2,1)S(1)}, bf16[2,64,1024]{2,1,0:T(8,128)(2,1)S(1)}, u32[]{:S(2)}, u32[]{:S(2)}) collective-permute-start(bf16[2,64,1024]{2,1,0:T(8,128)(2,1)S(1)} %get-tuple-element.213.refs_6_.refs_0_), channel_id=1, source_target_pairs={{0,2},{2,4},{4,6},{6,7},{7,5},{5,3},{3,1},{1,0},{8,10},{10,12},{12... | collective-permute-start | bytes 786440 | tf_op jit(solution)/shard_map/ppermute | solution.py:378
  87.8 10.1 %collective-permute-start.29 = (bf16[2,64,1024]{2,1,0:T(8,128)(2,1)S(1)}, bf16[2,64,1024]{2,1,0:T(8,128)(2,1)S(1)}, u32[]{:S(2)}, u32[]{:S(2)}) collective-permute-start(bf16[2,64,1024]{2,1,0:T(8,128)(2,1)S(1)} %get-tuple-element.216), channel_id=1, source_target_pairs={{2,0},{4,2},{6,4},{7,6},{5,7},{3,5},{1,3},{0,1},{10,8},{12,10},{14... | collective-permute-start | bytes 786440 | tf_op jit(solution)/shard_map/ppermute | solution.py:378
  92.4 9.9 %collective-permute-start.34 = (bf16[2,64,1024]{2,1,0:T(8,128)(2,1)S(1)}, bf16[2,64,1024]{2,1,0:T(8,128)(2,1)S(1)}, u32[]{:S(2)}, u32[]{:S(2)}) collective-permute-start(bf16[2,64,1024]{2,1,0:T(8,128)(2,1)S(1)} %get-tuple-element.221.refs_0_), channel_id=1, source_target_pairs={{0,2},{2,4},{4,6},{6,7},{7,5},{5,3},{3,1},{1,0},{8,10},{10,12},{12... | collective-permute-start | bytes 786440 | tf_op jit(solution)/shard_map/ppermute | solution.py:378
  93.4 10.1 %collective-permute-start.35 = (bf16[2,64,1024]{2,1,0:T(8,128)(2,1)S(1)}, bf16[2,64,1024]{2,1,0:T(8,128)(2,1)S(1)}, u32[]{:S(2)}, u32[]{:S(2)}) collective-permute-start(bf16[2,64,1024]{2,1,0:T(8,128)(2,1)S(1)} %get-tuple-element.228), channel_id=1, source_target_pairs={{2,0},{4,2},{6,4},{7,6},{5,7},{3,5},{1,3},{0,1},{10,8},{12,10},{14... | collective-permute-start | bytes 786440 | tf_op jit(solution)/shard_map/ppermute | solution.py:378
  98.1 9.7 %collective-permute-start.32 = (bf16[2,64,1024]{2,1,0:T(8,128)(2,1)S(1)}, bf16[2,64,1024]{2,1,0:T(8,128)(2,1)S(1)}, u32[]{:S(2)}, u32[]{:S(2)}) collective-permute-start(bf16[2,64,1024]{2,1,0:T(8,128)(2,1)S(1)} %get-tuple-element.222.refs_6_.refs_0_), channel_id=1, source_target_pairs={{0,2},{2,4},{4,6},{6,7},{7,5},{5,3},{3,1},{1,0},{8,10},{10,12},{12... | collective-permute-start | bytes 786440 | tf_op jit(solution)/shard_map/ppermute | solution.py:378
  99.0 10.1 %collective-permute-start.33 = (bf16[2,64,1024]{2,1,0:T(8,128)(2,1)S(1)}, bf16[2,64,1024]{2,1,0:T(8,128)(2,1)S(1)}, u32[]{:S(2)}, u32[]{:S(2)}) collective-permute-start(bf16[2,64,1024]{2,1,0:T(8,128)(2,1)S(1)} %get-tuple-element.225), channel_id=1, source_target_pairs={{2,0},{4,2},{6,4},{7,6},{5,7},{3,5},{1,3},{0,1},{10,8},{12,10},{14... | collective-permute-start | bytes 786440 | tf_op jit(solution)/shard_map/ppermute | solution.py:378
  103.7 11.1 %collective-permute-start.37 = (bf16[2,64,1024]{2,1,0:T(8,128)(2,1)S(1)}, bf16[2,64,1024]{2,1,0:T(8,128)(2,1)S(1)}, u32[]{:S(2)}, u32[]{:S(2)}) collective-permute-start(bf16[2,64,1024]{2,1,0:T(8,128)(2,1)S(1)} %get-tuple-element.233), channel_id=1, source_target_pairs={{2,0},{4,2},{6,4},{7,6},{5,7},{3,5},{1,3},{0,1},{10,8},{12,10},{14... | collective-permute-start | bytes 786440 | tf_op jit(solution)/shard_map/ppermute | solution.py:378
  104.1 10.7 %collective-permute-start.38 = (bf16[2,64,1024]{2,1,0:T(8,128)(2,1)S(1)}, bf16[2,64,1024]{2,1,0:T(8,128)(2,1)S(1)}, u32[]{:S(2)}, u32[]{:S(2)}) collective-permute-start(bf16[2,64,1024]{2,1,0:T(8,128)(2,1)S(1)} %get-tuple-element.229.refs_0_), channel_id=1, source_target_pairs={{0,2},{2,4},{4,6},{6,7},{7,5},{5,3},{3,1},{1,0},{8,10},{10,12},{12... | collective-permute-start | bytes 786440 | tf_op jit(solution)/shard_map/ppermute | solution.py:378
  109.3 7.8 %collective-permute-start.36 = (bf16[2,64,1024]{2,1,0:T(8,128)(2,1)S(1)}, bf16[2,64,1024]{2,1,0:T(8,128)(2,1)S(1)}, u32[]{:S(2)}, u32[]{:S(2)}) collective-permute-start(bf16[2,64,1024]{2,1,0:T(8,128)(2,1)S(1)} %get-tuple-element.230.refs_6_), channel_id=1, source_target_pairs={{0,2},{2,4},{4,6},{6,7},{7,5},{5,3},{3,1},{1,0},{8,10},{10,12},{12... | collective-permute-start | bytes 786440 | tf_op jit(solution)/shard_map/ppermute | solution.py:378
  110.3 8.2 %collective-permute-start.39 = (bf16[2,64,1024]{2,1,0:T(8,128)(2,1)S(1)}, bf16[2,64,1024]{2,1,0:T(8,128)(2,1)S(1)}, u32[]{:S(2)}, u32[]{:S(2)}) collective-permute-start(bf16[2,64,1024]{2,1,0:T(8,128)(2,1)S(1)} %get-tuple-element.234), channel_id=1, source_target_pairs={{2,0},{4,2},{6,4},{7,6},{5,7},{3,5},{1,3},{0,1},{10,8},{12,10},{14... | collective-permute-start | bytes 786440 | tf_op jit(solution)/shard_map/ppermute | solution.py:378
  (11 other events, 44.3 us)

commit v3 on v2

--- a/solution.py
+++ b/solution.py
@@ -38,7 +38,7 @@
     return pl.multiple_of(owner * part, part)
 
 
-def split_kernel(conv, mix, low, high, sems):
+def split_kernel(conv, mix, _taps, low, high, sems):
     copies = [
         pltpu.make_async_copy(conv.at[0:2], low, sems.at[0]),
         pltpu.make_async_copy(conv.at[2], high.at[0], sems.at[1]),
@@ -50,44 +50,57 @@
         copy.wait()
 
 
-def split_call(conv, mix):
+def split_call(conv, mix, taps_t):
     anywhere = pl.BlockSpec(memory_space=pl.ANY)
     return pl.pallas_call(
         split_kernel,
         out_shape=[pltpu.VMEM((2, *conv.shape[1:]), BF16)] * 2,
-        in_specs=[anywhere] * 2,
+        in_specs=[anywhere] * 2 + [VMEM],
         out_specs=[VMEM] * 2,
         scratch_shapes=[pltpu.SemaphoreType.DMA((3,))],
         compiler_params=PARAMS,
         cost_estimate=cost(0, 2**20),
-    )(*[pltpu.with_memory_space_constraint(array, pltpu.HBM) for array in (conv, mix)])
-
-
-def prepare_kernel(x, taps_t):
+    )(*[pltpu.with_memory_space_constraint(array, pltpu.HBM) for array in (conv, mix)], *in_vmem(taps_t))
+
+
+def prepare_kernel(parity, x_hbm, *refs):
+    taps_t, x, sem = refs[-3:]
     seqs, samples, channels = x.shape
-    dilation = jnp.left_shift(jnp.int32(1), lax.axis_index("pipe"))
+    section = lax.axis_index("pipe")
     wide = 128
-    for s in range(seqs):
-        columns = slice(s * samples, (s + 1) * samples)
-        for at in range(0, channels, wide):
-            turned = x[s, :, at : at + wide].astype(F32).T
-            position = lax.broadcasted_iota(jnp.int32, turned.shape, 1)
-            taps_t[at : at + wide, columns] = turned.astype(BF16)
-            for k in (1, 2):
-                delayed = jnp.where(position >= k * dilation, pltpu.roll(turned, k * dilation, 1), 0.0)
-                taps_t[k * channels + at : k * channels + at + wide, columns] = delayed.astype(BF16)
-
-
-def prepare_call(x):
+
+    @pl.when(lax.rem(section, 2) == parity)
+    def _():
+        copy = pltpu.make_async_copy(x_hbm, x, sem)
+        copy.start()
+        copy.wait()
+        dilation = jnp.left_shift(jnp.int32(1), section)
+        for s in range(seqs):
+            columns = slice(s * samples, (s + 1) * samples)
+
+            @pl.loop(0, channels // wide)
+            def _(j):
+                at = pl.multiple_of(j * wide, wide)
+                turned = x[s, :, pl.ds(at, wide)].astype(F32).T
+                position = lax.broadcasted_iota(jnp.int32, turned.shape, 1)
+                taps_t[pl.ds(at, wide), columns] = turned.astype(BF16)
+                for k in (1, 2):
+                    delayed = jnp.where(position >= k * dilation, pltpu.roll(turned, k * dilation, 1), 0.0)
+                    taps_t[pl.ds(k * channels + at, wide), columns] = delayed.astype(BF16)
+
+
+def prepare_call(parity, x, held):
     seqs, samples, channels = x.shape
     return pl.pallas_call(
-        prepare_kernel,
+        functools.partial(prepare_kernel, parity),
         out_shape=pltpu.VMEM((3 * channels, seqs * samples), BF16),
-        in_specs=[VMEM],
+        in_specs=[pl.BlockSpec(memory_space=pl.ANY)] + [VMEM] * len(held),
         out_specs=VMEM,
+        scratch_shapes=[pltpu.VMEM(x.shape, BF16), pltpu.SemaphoreType.DMA],
+        input_output_aliases={1: 0} if held else {},
         compiler_params=PARAMS,
         cost_estimate=cost(2**20, 2**22),
-    )(x)
+    )(pltpu.with_memory_space_constraint(x, pltpu.HBM), *in_vmem(*held))
 
 
 def tap_rows(taps_t, row, part, columns):
@@ -377,8 +390,10 @@
     def send(to_right, to_left):
         return lax.ppermute(to_right, "dp", right), lax.ppermute(to_left, "dp", left)
 
-    taps_t = prepare_call(x_ckpt[0].reshape(micro * seqs, samples, channels))
-    low, high = split_call(w_conv[0].transpose(1, 0, 2), w_mix)
+    x_rows = x_ckpt[0].reshape(micro * seqs, samples, channels)
+    taps_t = prepare_call(1, x_rows, [])
+    low, high = split_call(w_conv[0].transpose(1, 0, 2), w_mix, taps_t)
+    taps_t = prepare_call(0, x_rows, [taps_t])
     streams = {0: (low, low), 2: (high, high)}
     held = partial_call(replicas, ((0, 0), (0, 2)), taps_t, [low, high], [])
     skip = skip_cot.reshape(micro, block, channels)

time: 120 us -> 120 us (level)
  Pallas kernels: 27.8 us -> 29.9 us
  local copies, waits for them, and re-layouts: 1.32 us -> 0.09 us
    ppermute x15, waiting for transfers between devices: 15 us -> 11.9 us  [send(): lax.ppermute(to_right, 'dp', right)]
    pallas_call x1 -> x2, Pallas kernels: 1.34 us -> 3.28 us  [prepare_call(): pl.pallas_call(functools.partial(prepare_kernel, parity), out_shape=pltpu...]
    ppermute x15, starting transfers between devices: 8.22 us -> 6.52 us  [send(): lax.ppermute(to_left, 'dp', left)]
    ppermute x15, starting transfers between devices: 24.4 us -> 26 us  [send(): lax.ppermute(to_right, 'dp', right)]
    ppermute x15, waiting for transfers between devices: 21.5 us -> 23.1 us  [send(): lax.ppermute(to_left, 'dp', left)]
    ppermute x8, waiting for transfers between devices: 9.4 us -> 11 us  [local(): g[m][half_at] = lax.ppermute(piece, 'pipe', [(stage, stage - 1)])]
    unnamed x6 -> x4, local copies, waits for them, and re-layouts: 1.23 us -> 0.01 us
  transfers between devices with their start and end apart: 40 -> 40, of which waited for: 29 -> 29; matrix products, arithmetic and copies ran while one was open for 1% -> 1% of each run, Pallas kernels for 19% -> 20%
where the time goes in v3:
time: 120 us
  waiting for transfers between devices  46 us (38%)
  starting transfers between devices  42 us (35%)
  Pallas kernels  29.9 us (25%)
    ppermute x15, starting transfers between devices, send(): lax.ppermute(to_right, 'dp', right)  26 us
    ppermute x15, waiting for transfers between devices, send(): lax.ppermute(to_left, 'dp', left)  23.1 us
    ppermute x15, waiting for transfers between devices, send(): lax.ppermute(to_right, 'dp', right)  11.9 us
    ppermute x8, waiting for transfers between devices, local(): g[m][half_at] = lax.ppermute(piece, 'pipe', [(stage, stage - 1)])  11 us
    pallas_call x5, Pallas kernels, term_call(): pl.pallas_call(functools.partial(term_kernel, replicas, offsets, micro),...  9.1 us
    ppermute x8, starting transfers between devices, local(): g[m][half_at] = lax.ppermute(piece, 'pipe', [(stage, stage - 1)])  7.88 us
    pallas_call x7, Pallas kernels, partial_call(): pl.pallas_call(functools.partial(partial_kernel, replicas, items, not hel...  6.67 us
    ppermute x15, starting transfers between devices, send(): lax.ppermute(to_left, 'dp', left)  6.52 us
  transfers between devices with their start and end apart: 40, of which 29 were waited for; matrix products, arithmetic and copies ran while one was open for 1% of the time, Pallas kernels for 20%

profile of v3, /device:TPU:0, one launch (start us, length us, event | category | flops | bytes accessed | tf_op | source)
XLA Modules:
  0.0 120.1 jit_solution(4759453228345778671)
XLA Ops:
  1.7 3.1 %collective-permute-start.2 = (bf16[2,64,1024]{2,1,0:T(8,128)(2,1)S(1)}, bf16[2,64,1024]{2,1,0:T(8,128)(2,1)S(1)}, u32[]{:S(2)}, u32[]{:S(2)}) collective-permute-start(bf16[2,64,1024]{2,1,0:T(8,128)(2,1)S(1)} %get-tuple-element.121.refs_0_), channel_id=1, source_target_pairs={{0,2},{2,4},{4,6},{6,7},{7,5},{5,3},{3,1},{1,0},{8,10},{10,12},{12... | collective-permute-start | bytes 786440 | tf_op jit(solution)/shard_map/ppermute | solution.py:391
  4.8 2.0 %collective-permute-start = (bf16[2,64,1024]{2,1,0:T(8,128)(2,1)S(1)}, bf16[2,64,1024]{2,1,0:T(8,128)(2,1)S(1)}, u32[]{:S(2)}, u32[]{:S(2)}) collective-permute-start(bf16[2,64,1024]{2,1,0:T(8,128)(2,1)S(1)} %get-tuple-element.120.refs_1_), channel_id=1, source_target_pairs={{0,2},{2,4},{4,6},{6,7},{7,5},{5,3},{3,1},{1,0},{8,10},{10,12},{12... | collective-permute-start | bytes 786440 | tf_op jit(solution)/shard_map/ppermute | solution.py:391
  6.9 3.3 %shard_map.77.taps_t = bf16[1536,1024]{1,0:T(8,128)(2,1)S(1)} custom-call(bf16[2,512,512]{2,1,0:T(8,128)(2,1)} %bitcast.42, bf16[1536,1024]{1,0:T(8,128)(2,1)S(1)} %shard_map.76.refs_0_._taps), custom_call_target="tpu_custom_call", output_to_operand_aliasing={{}: (1, {})} | custom-call | flops 1048576 | bytes 4194304 | tf_op jit(solution)/shard_map/pallas_call | solution.py:94
  13.1 1.6 %collective-permute-start.6 = (bf16[2,64,1024]{2,1,0:T(8,128)(2,1)S(1)}, bf16[2,64,1024]{2,1,0:T(8,128)(2,1)S(1)}, u32[]{:S(2)}, u32[]{:S(2)}) collective-permute-start(bf16[2,64,1024]{2,1,0:T(8,128)(2,1)S(1)} %get-tuple-element.128), channel_id=1, source_target_pairs={{0,2},{2,4},{4,6},{6,7},{7,5},{5,3},{3,1},{1,0},{8,10},{10,12},{12... | collective-permute-start | bytes 786440 | tf_op jit(solution)/shard_map/ppermute | solution.py:391
  15.2 2.5 %collective-permute-done.1.refs_1_ = bf16[2,64,1024]{2,1,0:T(8,128)(2,1)S(1)} collective-permute-done((bf16[2,64,1024]{2,1,0:T(8,128)(2,1)S(1)}, bf16[2,64,1024]{2,1,0:T(8,128)(2,1)S(1)}, u32[]{:S(2)}, u32[]{:S(2)}) %collective-permute-start.1) | collective-permute-done | bytes 262176 | tf_op jit(solution)/shard_map/ppermute | solution.py:391
  18.7 1.6 %collective-permute-start.4 = (bf16[2,64,1024]{2,1,0:T(8,128)(2,1)S(1)}, bf16[2,64,1024]{2,1,0:T(8,128)(2,1)S(1)}, u32[]{:S(2)}, u32[]{:S(2)}) collective-permute-start(bf16[2,64,1024]{2,1,0:T(8,128)(2,1)S(1)} %get-tuple-element.126), channel_id=1, source_target_pairs={{0,2},{2,4},{4,6},{6,7},{7,5},{5,3},{3,1},{1,0},{8,10},{10,12},{12... | collective-permute-start | bytes 786440 | tf_op jit(solution)/shard_map/ppermute | solution.py:391
  21.1 2.8 %collective-permute-done.7.refs_1_ = bf16[2,64,1024]{2,1,0:T(8,128)(2,1)S(1)} collective-permute-done((bf16[2,64,1024]{2,1,0:T(8,128)(2,1)S(1)}, bf16[2,64,1024]{2,1,0:T(8,128)(2,1)S(1)}, u32[]{:S(2)}, u32[]{:S(2)}) %collective-permute-start.7) | collective-permute-done | bytes 262176 | tf_op jit(solution)/shard_map/ppermute | solution.py:391
  24.8 1.6 %collective-permute-start.10 = (bf16[2,64,1024]{2,1,0:T(8,128)(2,1)S(1)}, bf16[2,64,1024]{2,1,0:T(8,128)(2,1)S(1)}, u32[]{:S(2)}, u32[]{:S(2)}) collective-permute-start(bf16[2,64,1024]{2,1,0:T(8,128)(2,1)S(1)} %get-tuple-element.136), channel_id=1, source_target_pairs={{0,2},{2,4},{4,6},{6,7},{7,5},{5,3},{3,1},{1,0},{8,10},{10,12},{12... | collective-permute-start | bytes 786440 | tf_op jit(solution)/shard_map/ppermute | solution.py:391
  27.3 2.3 %collective-permute-done.5.refs_1_ = bf16[2,64,1024]{2,1,0:T(8,128)(2,1)S(1)} collective-permute-done((bf16[2,64,1024]{2,1,0:T(8,128)(2,1)S(1)}, bf16[2,64,1024]{2,1,0:T(8,128)(2,1)S(1)}, u32[]{:S(2)}, u32[]{:S(2)}) %collective-permute-start.5) | collective-permute-done | bytes 262176 | tf_op jit(solution)/shard_map/ppermute | solution.py:391
  30.5 1.6 %collective-permute-start.8 = (bf16[2,64,1024]{2,1,0:T(8,128)(2,1)S(1)}, bf16[2,64,1024]{2,1,0:T(8,128)(2,1)S(1)}, u32[]{:S(2)}, u32[]{:S(2)}) collective-permute-start(bf16[2,64,1024]{2,1,0:T(8,128)(2,1)S(1)} %get-tuple-element.134), channel_id=1, source_target_pairs={{0,2},{2,4},{4,6},{6,7},{7,5},{5,3},{3,1},{1,0},{8,10},{10,12},{12... | collective-permute-start | bytes 786440 | tf_op jit(solution)/shard_map/ppermute | solution.py:391
  32.9 2.8 %collective-permute-done.11.refs_1_ = bf16[2,64,1024]{2,1,0:T(8,128)(2,1)S(1)} collective-permute-done((bf16[2,64,1024]{2,1,0:T(8,128)(2,1)S(1)}, bf16[2,64,1024]{2,1,0:T(8,128)(2,1)S(1)}, u32[]{:S(2)}, u32[]{:S(2)}) %collective-permute-start.11) | collective-permute-done | bytes 262176 | tf_op jit(solution)/shard_map/ppermute | solution.py:391
  39.1 2.4 %collective-permute-start.14 = (bf16[1,64,1024]{2,1,0:T(8,128)(2,1)S(1)}, bf16[1,64,1024]{2,1,0:T(8,128)(2,1)S(1)}, u32[]{:S(2)}, u32[]{:S(2)}) collective-permute-start(bf16[1,64,1024]{2,1,0:T(8,128)(2,1)S(1)} %slice.10), channel_id=1, source_target_pairs={{0,2},{2,4},{4,6},{6,7},{7,5},{5,3},{3,1},{1,0},{8,10},{10,12},{12... | collective-permute-start | bytes 393224 | tf_op jit(solution)/shard_map/ppermute | solution.py:391
  42.5 1.8 %collective-permute-done.13.refs_3_ = bf16[1,64,1024]{2,1,0:T(8,128)(2,1)S(1)} collective-permute-done((bf16[1,64,1024]{2,1,0:T(8,128)(2,1)S(1)}, bf16[1,64,1024]{2,1,0:T(8,128)(2,1)S(1)}, u32[]{:S(2)}, u32[]{:S(2)}) %collective-permute-start.13) | collective-permute-done | bytes 131104 | tf_op jit(solution)/shard_map/ppermute | solution.py:391
  45.3 2.3 %collective-permute-done.15.refs_1_ = bf16[1,64,1024]{2,1,0:T(8,128)(2,1)S(1)} collective-permute-done((bf16[1,64,1024]{2,1,0:T(8,128)(2,1)S(1)}, bf16[1,64,1024]{2,1,0:T(8,128)(2,1)S(1)}, u32[]{:S(2)}, u32[]{:S(2)}) %collective-permute-start.15) | collective-permute-done | bytes 131104 | tf_op jit(solution)/shard_map/ppermute | solution.py:391
  59.4 6.7 %collective-permute-done.20.g = bf16[256,512]{1,0:T(8,128)(2,1)S(1)} collective-permute-done((bf16[256,512]{1,0:T(8,128)(2,1)S(1)}, bf16[256,512]{1,0:T(8,128)(2,1)S(1)}, u32[]{:S(2)}, u32[]{:S(2)}) %collective-permute-start.20) | collective-permute-done | bytes 262176 | tf_op jit(solution)/shard_map/ppermute | solution.py:444
  66.1 1.5 %shard_map.92 = (bf16[512,1024]{1,0:T(8,128)(2,1)S(1)}, bf16[512,512]{1,0:T(8,128)(2,1)S(1)}, bf16[512,512]{1,0:T(8,128)(2,1)S(1)}, f32[2,16,512]{2,1,0:T(8,128)S(1)}) custom-call(bf16[256,512]{1,0:T(8,128)(2,1)S(1)} %collective-permute-done.20.g, bf16[2,512,512]{2,1,0:T(8,128)(2,1)S(1)} %bitcast.30, ...), custom_call_target="tpu_custom_call", output_to_operand_aliasing={{0}: (5, {}), {1}: (6, {}), {2}: (7, {})} | custom-call | flops 536870912 | bytes 4194304 | tf_op jit(solution)/shard_map/pallas_call | solution.py:268
  69.0 1.5 %shard_map.93 = (bf16[512,1024]{1,0:T(8,128)(2,1)S(1)}, bf16[512,512]{1,0:T(8,128)(2,1)S(1)}, bf16[512,512]{1,0:T(8,128)(2,1)S(1)}) custom-call(bf16[256,512]{1,0:T(8,128)(2,1)S(1)} %collective-permute-done.19.g, bf16[2,512,512]{2,1,0:T(8,128)(2,1)S(1)} %bitcast.31, ...), custom_call_target="tpu_custom_call", output_to_operand_aliasing={{0}: (6, {}), {1}: (7, {}), {2}: (8, {})} | custom-call | flops 536870912 | bytes 4194304 | tf_op jit(solution)/shard_map/pallas_call | solution.py:268
  71.8 1.5 %shard_map.100 = (bf16[512,1024]{1,0:T(8,128)(2,1)S(1)}, bf16[512,512]{1,0:T(8,128)(2,1)S(1)}, bf16[512,512]{1,0:T(8,128)(2,1)S(1)}, f32[2,16,512]{2,1,0:T(8,128)S(1)}) custom-call(bf16[256,512]{1,0:T(8,128)(2,1)S(1)} %collective-permute-done.25.g, bf16[2,512,512]{2,1,0:T(8,128)(2,1)S(1)} %bitcast.32, ...), custom_call_target="tpu_custom_call", output_to_operand_aliasing={{0}: (6, {}), {1}: (7, {}), {2}: (8, {})} | custom-call | flops 536870912 | bytes 4194304 | tf_op jit(solution)/shard_map/pallas_call | solution.py:268
  73.3 1.6 %collective-permute-done.24.g = bf16[256,512]{1,0:T(8,128)(2,1)S(1)} collective-permute-done((bf16[256,512]{1,0:T(8,128)(2,1)S(1)}, bf16[256,512]{1,0:T(8,128)(2,1)S(1)}, u32[]{:S(2)}, u32[]{:S(2)}) %collective-permute-start.24) | collective-permute-done | bytes 262176 | tf_op jit(solution)/shard_map/ppermute | solution.py:444
  74.9 1.5 %shard_map.101 = (bf16[512,1024]{1,0:T(8,128)(2,1)S(1)}, bf16[512,512]{1,0:T(8,128)(2,1)S(1)}, bf16[512,512]{1,0:T(8,128)(2,1)S(1)}) custom-call(bf16[256,512]{1,0:T(8,128)(2,1)S(1)} %collective-permute-done.24.g, bf16[2,512,512]{2,1,0:T(8,128)(2,1)S(1)} %bitcast.33, ...), custom_call_target="tpu_custom_call", output_to_operand_aliasing={{0}: (6, {}), {1}: (7, {}), {2}: (8, {})} | custom-call | flops 536870912 | bytes 4194304 | tf_op jit(solution)/shard_map/pallas_call | solution.py:268
  79.4 2.2 %shard_map.103 = (bf16[2,64,1024]{2,1,0:T(8,128)(2,1)S(1)}, bf16[2,64,1024]{2,1,0:T(8,128)(2,1)S(1)}, bf16[2,64,1024]{2,1,0:T(8,128)(2,1)S(1)}, bf16[2,64,1024]{2,1,0:T(8,128)(2,1)S(1)}) custom-call(bf16[1536,1024]{1,0:T(8,128)(2,1)S(1)} %shard_map.77.taps_t, bf16[2,512,512]{2,1,0:T(8,128)(2,1)S(1)} %bitcast.35, ...), custom_call_target="tpu_custom_call" | custom-call | flops 1073741824 | bytes 1048576 | tf_op jit(solution)/shard_map/pallas_call | solution.py:335
  83.7 2.4 %collective-permute-done.26.got_r = bf16[2,64,1024]{2,1,0:T(8,128)(2,1)S(1)} collective-permute-done((bf16[2,64,1024]{2,1,0:T(8,128)(2,1)S(1)}, bf16[2,64,1024]{2,1,0:T(8,128)(2,1)S(1)}, u32[]{:S(2)}, u32[]{:S(2)}) %collective-permute-start.26) | collective-permute-done | bytes 262176 | tf_op jit(solution)/shard_map/ppermute | solution.py:391
  87.4 1.6 %collective-permute-start.28 = (bf16[2,64,1024]{2,1,0:T(8,128)(2,1)S(1)}, bf16[2,64,1024]{2,1,0:T(8,128)(2,1)S(1)}, u32[]{:S(2)}, u32[]{:S(2)}) collective-permute-start(bf16[2,64,1024]{2,1,0:T(8,128)(2,1)S(1)} %get-tuple-element.213.refs_6_.refs_0_), channel_id=1, source_target_pairs={{0,2},{2,4},{4,6},{6,7},{7,5},{5,3},{3,1},{1,0},{8,10},{10,12},{12... | collective-permute-start | bytes 786440 | tf_op jit(solution)/shard_map/ppermute | solution.py:391
  89.5 2.2 %shard_map.105 = (bf16[2,64,1024]{2,1,0:T(8,128)(2,1)S(1)}, bf16[2,64,1024]{2,1,0:T(8,128)(2,1)S(1)}, bf16[2,64,1024]{2,1,0:T(8,128)(2,1)S(1)}, bf16[2,64,1024]{2,1,0:T(8,128)(2,1)S(1)}) custom-call(bf16[1536,1024]{1,0:T(8,128)(2,1)S(1)} %shard_map.77.taps_t, bf16[2,512,512]{2,1,0:T(8,128)(2,1)S(1)} %bitcast.36, ...), custom_call_target="tpu_custom_call" | custom-call | flops 1073741824 | bytes 1048576 | tf_op jit(solution)/shard_map/pallas_call | solution.py:335
  93.0 1.6 %collective-permute-start.34 = (bf16[2,64,1024]{2,1,0:T(8,128)(2,1)S(1)}, bf16[2,64,1024]{2,1,0:T(8,128)(2,1)S(1)}, u32[]{:S(2)}, u32[]{:S(2)}) collective-permute-start(bf16[2,64,1024]{2,1,0:T(8,128)(2,1)S(1)} %get-tuple-element.221.refs_0_), channel_id=1, source_target_pairs={{0,2},{2,4},{4,6},{6,7},{7,5},{5,3},{3,1},{1,0},{8,10},{10,12},{12... | collective-permute-start | bytes 786440 | tf_op jit(solution)/shard_map/ppermute | solution.py:391
  95.1 2.3 %collective-permute-done.28.got_r = bf16[2,64,1024]{2,1,0:T(8,128)(2,1)S(1)} collective-permute-done((bf16[2,64,1024]{2,1,0:T(8,128)(2,1)S(1)}, bf16[2,64,1024]{2,1,0:T(8,128)(2,1)S(1)}, u32[]{:S(2)}, u32[]{:S(2)}) %collective-permute-start.28) | collective-permute-done | bytes 262176 | tf_op jit(solution)/shard_map/ppermute | solution.py:391
  98.6 1.6 %collective-permute-start.32 = (bf16[2,64,1024]{2,1,0:T(8,128)(2,1)S(1)}, bf16[2,64,1024]{2,1,0:T(8,128)(2,1)S(1)}, u32[]{:S(2)}, u32[]{:S(2)}) collective-permute-start(bf16[2,64,1024]{2,1,0:T(8,128)(2,1)S(1)} %get-tuple-element.222.refs_6_.refs_0_), channel_id=1, source_target_pairs={{0,2},{2,4},{4,6},{6,7},{7,5},{5,3},{3,1},{1,0},{8,10},{10,12},{12... | collective-permute-start | bytes 786440 | tf_op jit(solution)/shard_map/ppermute | solution.py:391
  100.7 2.1 %shard_map.108 = (bf16[2,64,1024]{2,1,0:T(8,128)(2,1)S(1)}, bf16[2,64,1024]{2,1,0:T(8,128)(2,1)S(1)}, bf16[2,64,1024]{2,1,0:T(8,128)(2,1)S(1)}, bf16[2,64,1024]{2,1,0:T(8,128)(2,1)S(1)}) custom-call(bf16[1536,1024]{1,0:T(8,128)(2,1)S(1)} %shard_map.77.taps_t, bf16[2,512,512]{2,1,0:T(8,128)(2,1)S(1)} %bitcast.37, ...), custom_call_target="tpu_custom_call" | custom-call | flops 1073741824 | bytes 1048576 | tf_op jit(solution)/shard_map/pallas_call | solution.py:335
  106.3 2.3 %collective-permute-done.32.got_r = bf16[2,64,1024]{2,1,0:T(8,128)(2,1)S(1)} collective-permute-done((bf16[2,64,1024]{2,1,0:T(8,128)(2,1)S(1)}, bf16[2,64,1024]{2,1,0:T(8,128)(2,1)S(1)}, u32[]{:S(2)}, u32[]{:S(2)}) %collective-permute-start.32) | collective-permute-done | bytes 262176 | tf_op jit(solution)/shard_map/ppermute | solution.py:391
  109.8 1.6 %collective-permute-start.36 = (bf16[2,64,1024]{2,1,0:T(8,128)(2,1)S(1)}, bf16[2,64,1024]{2,1,0:T(8,128)(2,1)S(1)}, u32[]{:S(2)}, u32[]{:S(2)}) collective-permute-start(bf16[2,64,1024]{2,1,0:T(8,128)(2,1)S(1)} %get-tuple-element.230.refs_6_), channel_id=1, source_target_pairs={{0,2},{2,4},{4,6},{6,7},{7,5},{5,3},{3,1},{1,0},{8,10},{10,12},{12... | collective-permute-start | bytes 786440 | tf_op jit(solution)/shard_map/ppermute | solution.py:391
  113.0 1.7 %shard_map.111 = (f32[2,64,1024]{2,1,0:T(8,128)S(1)}, f32[2,64,1024]{2,1,0:T(8,128)S(1)}) custom-call(bf16[1536,1024]{1,0:T(8,128)(2,1)S(1)} %shard_map.77.taps_t, bf16[2,512,512]{2,1,0:T(8,128)(2,1)S(1)} %bitcast.38, bf16[512,512]{1,0:T(8,128)(2,1)S(1)} %get-tuple-element.203.refs_0_, bf16[512,512]{1,0:T(8,128)(2,1)S(1)} %get-tuple-element.204.refs_1_, ...), custom_call_target="tpu_custom_call" | custom-call | flops 536870912 | bytes 1048576 | tf_op jit(solution)/shard_map/pallas_call | solution.py:335
  115.3 2.6 %collective-permute-done.36.low_r = bf16[2,64,1024]{2,1,0:T(8,128)(2,1)S(1)} collective-permute-done((bf16[2,64,1024]{2,1,0:T(8,128)(2,1)S(1)}, bf16[2,64,1024]{2,1,0:T(8,128)(2,1)S(1)}, u32[]{:S(2)}, u32[]{:S(2)}) %collective-permute-start.36) | collective-permute-done | bytes 262176 | tf_op jit(solution)/shard_map/ppermute | solution.py:391
  (93 shorter events, 48.8 us)
Async XLA Ops:
  1.7 9.2 %collective-permute-start.2 = (bf16[2,64,1024]{2,1,0:T(8,128)(2,1)S(1)}, bf16[2,64,1024]{2,1,0:T(8,128)(2,1)S(1)}, u32[]{:S(2)}, u32[]{:S(2)}) collective-permute-start(bf16[2,64,1024]{2,1,0:T(8,128)(2,1)S(1)} %get-tuple-element.121.refs_0_), channel_id=1, source_target_pairs={{0,2},{2,4},{4,6},{6,7},{7,5},{5,3},{3,1},{1,0},{8,10},{10,12},{12... | collective-permute-start | bytes 786440 | tf_op jit(solution)/shard_map/ppermute | solution.py:391
  4.8 7.3 %collective-permute-start.3 = (bf16[2,64,1024]{2,1,0:T(8,128)(2,1)S(1)}, bf16[2,64,1024]{2,1,0:T(8,128)(2,1)S(1)}, u32[]{:S(2)}, u32[]{:S(2)}) collective-permute-start(bf16[2,64,1024]{2,1,0:T(8,128)(2,1)S(1)} %get-tuple-element.121.refs_0_), channel_id=1, source_target_pairs={{2,0},{4,2},{6,4},{7,6},{5,7},{3,5},{1,3},{0,1},{10,8},{12,10},{14... | collective-permute-start | bytes 786440 | tf_op jit(solution)/shard_map/ppermute | solution.py:391
  4.8 10.4 %collective-permute-start = (bf16[2,64,1024]{2,1,0:T(8,128)(2,1)S(1)}, bf16[2,64,1024]{2,1,0:T(8,128)(2,1)S(1)}, u32[]{:S(2)}, u32[]{:S(2)}) collective-permute-start(bf16[2,64,1024]{2,1,0:T(8,128)(2,1)S(1)} %get-tuple-element.120.refs_1_), channel_id=1, source_target_pairs={{0,2},{2,4},{4,6},{6,7},{7,5},{5,3},{3,1},{1,0},{8,10},{10,12},{12... | collective-permute-start | bytes 786440 | tf_op jit(solution)/shard_map/ppermute | solution.py:391
  6.9 10.9 %collective-permute-start.1 = (bf16[2,64,1024]{2,1,0:T(8,128)(2,1)S(1)}, bf16[2,64,1024]{2,1,0:T(8,128)(2,1)S(1)}, u32[]{:S(2)}, u32[]{:S(2)}) collective-permute-start(bf16[2,64,1024]{2,1,0:T(8,128)(2,1)S(1)} %get-tuple-element.120.refs_1_), channel_id=1, source_target_pairs={{2,0},{4,2},{6,4},{7,6},{5,7},{3,5},{1,3},{0,1},{10,8},{12,10},{14... | collective-permute-start | bytes 786440 | tf_op jit(solution)/shard_map/ppermute | solution.py:391
  13.1 8.0 %collective-permute-start.6 = (bf16[2,64,1024]{2,1,0:T(8,128)(2,1)S(1)}, bf16[2,64,1024]{2,1,0:T(8,128)(2,1)S(1)}, u32[]{:S(2)}, u32[]{:S(2)}) collective-permute-start(bf16[2,64,1024]{2,1,0:T(8,128)(2,1)S(1)} %get-tuple-element.128), channel_id=1, source_target_pairs={{0,2},{2,4},{4,6},{6,7},{7,5},{5,3},{3,1},{1,0},{8,10},{10,12},{12... | collective-permute-start | bytes 786440 | tf_op jit(solution)/shard_map/ppermute | solution.py:391
  14.7 9.1 %collective-permute-start.7 = (bf16[2,64,1024]{2,1,0:T(8,128)(2,1)S(1)}, bf16[2,64,1024]{2,1,0:T(8,128)(2,1)S(1)}, u32[]{:S(2)}, u32[]{:S(2)}) collective-permute-start(bf16[2,64,1024]{2,1,0:T(8,128)(2,1)S(1)} %get-tuple-element.129), channel_id=1, source_target_pairs={{2,0},{4,2},{6,4},{7,6},{5,7},{3,5},{1,3},{0,1},{10,8},{12,10},{14... | collective-permute-start | bytes 786440 | tf_op jit(solution)/shard_map/ppermute | solution.py:391
  18.7 8.6 %collective-permute-start.4 = (bf16[2,64,1024]{2,1,0:T(8,128)(2,1)S(1)}, bf16[2,64,1024]{2,1,0:T(8,128)(2,1)S(1)}, u32[]{:S(2)}, u32[]{:S(2)}) collective-permute-start(bf16[2,64,1024]{2,1,0:T(8,128)(2,1)S(1)} %get-tuple-element.126), channel_id=1, source_target_pairs={{0,2},{2,4},{4,6},{6,7},{7,5},{5,3},{3,1},{1,0},{8,10},{10,12},{12... | collective-permute-start | bytes 786440 | tf_op jit(solution)/shard_map/ppermute | solution.py:391
  20.3 9.2 %collective-permute-start.5 = (bf16[2,64,1024]{2,1,0:T(8,128)(2,1)S(1)}, bf16[2,64,1024]{2,1,0:T(8,128)(2,1)S(1)}, u32[]{:S(2)}, u32[]{:S(2)}) collective-permute-start(bf16[2,64,1024]{2,1,0:T(8,128)(2,1)S(1)} %get-tuple-element.127), channel_id=1, source_target_pairs={{2,0},{4,2},{6,4},{7,6},{5,7},{3,5},{1,3},{0,1},{10,8},{12,10},{14... | collective-permute-start | bytes 786440 | tf_op jit(solution)/shard_map/ppermute | solution.py:391
  24.8 8.1 %collective-permute-start.10 = (bf16[2,64,1024]{2,1,0:T(8,128)(2,1)S(1)}, bf16[2,64,1024]{2,1,0:T(8,128)(2,1)S(1)}, u32[]{:S(2)}, u32[]{:S(2)}) collective-permute-start(bf16[2,64,1024]{2,1,0:T(8,128)(2,1)S(1)} %get-tuple-element.136), channel_id=1, source_target_pairs={{0,2},{2,4},{4,6},{6,7},{7,5},{5,3},{3,1},{1,0},{8,10},{10,12},{12... | collective-permute-start | bytes 786440 | tf_op jit(solution)/shard_map/ppermute | solution.py:391
  26.5 9.2 %collective-permute-start.11 = (bf16[2,64,1024]{2,1,0:T(8,128)(2,1)S(1)}, bf16[2,64,1024]{2,1,0:T(8,128)(2,1)S(1)}, u32[]{:S(2)}, u32[]{:S(2)}) collective-permute-start(bf16[2,64,1024]{2,1,0:T(8,128)(2,1)S(1)} %get-tuple-element.137), channel_id=1, source_target_pairs={{2,0},{4,2},{6,4},{7,6},{5,7},{3,5},{1,3},{0,1},{10,8},{12,10},{14... | collective-permute-start | bytes 786440 | tf_op jit(solution)/shard_map/ppermute | solution.py:391
  30.5 8.5 %collective-permute-start.8 = (bf16[2,64,1024]{2,1,0:T(8,128)(2,1)S(1)}, bf16[2,64,1024]{2,1,0:T(8,128)(2,1)S(1)}, u32[]{:S(2)}, u32[]{:S(2)}) collective-permute-start(bf16[2,64,1024]{2,1,0:T(8,128)(2,1)S(1)} %get-tuple-element.134), channel_id=1, source_target_pairs={{0,2},{2,4},{4,6},{6,7},{7,5},{5,3},{3,1},{1,0},{8,10},{10,12},{12... | collective-permute-start | bytes 786440 | tf_op jit(solution)/shard_map/ppermute | solution.py:391
  32.1 9.3 %collective-permute-start.9 = (bf16[2,64,1024]{2,1,0:T(8,128)(2,1)S(1)}, bf16[2,64,1024]{2,1,0:T(8,128)(2,1)S(1)}, u32[]{:S(2)}, u32[]{:S(2)}) collective-permute-start(bf16[2,64,1024]{2,1,0:T(8,128)(2,1)S(1)} %get-tuple-element.135), channel_id=1, source_target_pairs={{2,0},{4,2},{6,4},{7,6},{5,7},{3,5},{1,3},{0,1},{10,8},{12,10},{14... | collective-permute-start | bytes 786440 | tf_op jit(solution)/shard_map/ppermute | solution.py:391
  38.0 6.3 %collective-permute-start.13 = (bf16[1,64,1024]{2,1,0:T(8,128)(2,1)S(1)}, bf16[1,64,1024]{2,1,0:T(8,128)(2,1)S(1)}, u32[]{:S(2)}, u32[]{:S(2)}) collective-permute-start(bf16[1,64,1024]{2,1,0:T(8,128)(2,1)S(1)} %get-tuple-element.141), channel_id=1, source_target_pairs={{2,0},{4,2},{6,4},{7,6},{5,7},{3,5},{1,3},{0,1},{10,8},{12,10},{14... | collective-permute-start | bytes 393224 | tf_op jit(solution)/shard_map/ppermute | solution.py:391
  39.1 6.2 %collective-permute-start.14 = (bf16[1,64,1024]{2,1,0:T(8,128)(2,1)S(1)}, bf16[1,64,1024]{2,1,0:T(8,128)(2,1)S(1)}, u32[]{:S(2)}, u32[]{:S(2)}) collective-permute-start(bf16[1,64,1024]{2,1,0:T(8,128)(2,1)S(1)} %slice.10), channel_id=1, source_target_pairs={{0,2},{2,4},{4,6},{6,7},{7,5},{5,3},{3,1},{1,0},{8,10},{10,12},{12... | collective-permute-start | bytes 393224 | tf_op jit(solution)/shard_map/ppermute | solution.py:391
  53.9 12.2 %collective-permute-start.20 = (bf16[256,512]{1,0:T(8,128)(2,1)S(1)}, bf16[256,512]{1,0:T(8,128)(2,1)S(1)}, u32[]{:S(2)}, u32[]{:S(2)}) collective-permute-start(bf16[256,512]{1,0:T(8,128)(2,1)S(1)} %get-tuple-element.166), channel_id=1, source_target_pairs={{8,0},{9,1},{10,2},{11,3},{12,4},{13,5},{14,6},{15,7}} | collective-permute-start | bytes 786440 | tf_op jit(solution)/shard_map/ppermute | solution.py:444
  55.2 13.8 %collective-permute-start.19 = (bf16[256,512]{1,0:T(8,128)(2,1)S(1)}, bf16[256,512]{1,0:T(8,128)(2,1)S(1)}, u32[]{:S(2)}, u32[]{:S(2)}) collective-permute-start(bf16[256,512]{1,0:T(8,128)(2,1)S(1)} %get-tuple-element.165.refs_0_), channel_id=1, source_target_pairs={{8,0},{9,1},{10,2},{11,3},{12,4},{13,5},{14,6},{15,7}} | collective-permute-start | bytes 786440 | tf_op jit(solution)/shard_map/ppermute | solution.py:444
  56.5 15.3 %collective-permute-start.25 = (bf16[256,512]{1,0:T(8,128)(2,1)S(1)}, bf16[256,512]{1,0:T(8,128)(2,1)S(1)}, u32[]{:S(2)}, u32[]{:S(2)}) collective-permute-start(bf16[256,512]{1,0:T(8,128)(2,1)S(1)} %get-tuple-element.194), channel_id=1, source_target_pairs={{8,0},{9,1},{10,2},{11,3},{12,4},{13,5},{14,6},{15,7}} | collective-permute-start | bytes 786440 | tf_op jit(solution)/shard_map/ppermute | solution.py:444
  58.1 16.8 %collective-permute-start.24 = (bf16[256,512]{1,0:T(8,128)(2,1)S(1)}, bf16[256,512]{1,0:T(8,128)(2,1)S(1)}, u32[]{:S(2)}, u32[]{:S(2)}) collective-permute-start(bf16[256,512]{1,0:T(8,128)(2,1)S(1)} %get-tuple-element.193), channel_id=1, source_target_pairs={{8,0},{9,1},{10,2},{11,3},{12,4},{13,5},{14,6},{15,7}} | collective-permute-start | bytes 786440 | tf_op jit(solution)/shard_map/ppermute | solution.py:444
  77.3 8.8 %collective-permute-start.26 = (bf16[2,64,1024]{2,1,0:T(8,128)(2,1)S(1)}, bf16[2,64,1024]{2,1,0:T(8,128)(2,1)S(1)}, u32[]{:S(2)}, u32[]{:S(2)}) collective-permute-start(bf16[2,64,1024]{2,1,0:T(8,128)(2,1)S(1)} %get-tuple-element.209.refs_6_), channel_id=1, source_target_pairs={{0,2},{2,4},{4,6},{6,7},{7,5},{5,3},{3,1},{1,0},{8,10},{10,12},{12... | collective-permute-start | bytes 786440 | tf_op jit(solution)/shard_map/ppermute | solution.py:391
  78.8 8.5 %collective-permute-start.27 = (bf16[2,64,1024]{2,1,0:T(8,128)(2,1)S(1)}, bf16[2,64,1024]{2,1,0:T(8,128)(2,1)S(1)}, u32[]{:S(2)}, u32[]{:S(2)}) collective-permute-start(bf16[2,64,1024]{2,1,0:T(8,128)(2,1)S(1)} %get-tuple-element.212), channel_id=1, source_target_pairs={{2,0},{4,2},{6,4},{7,6},{5,7},{3,5},{1,3},{0,1},{10,8},{12,10},{14... | collective-permute-start | bytes 786440 | tf_op jit(solution)/shard_map/ppermute | solution.py:391
  81.6 10.1 %collective-permute-start.30 = (bf16[2,64,1024]{2,1,0:T(8,128)(2,1)S(1)}, bf16[2,64,1024]{2,1,0:T(8,128)(2,1)S(1)}, u32[]{:S(2)}, u32[]{:S(2)}) collective-permute-start(bf16[2,64,1024]{2,1,0:T(8,128)(2,1)S(1)} %get-tuple-element.219), channel_id=1, source_target_pairs={{0,2},{2,4},{4,6},{6,7},{7,5},{5,3},{3,1},{1,0},{8,10},{10,12},{12... | collective-permute-start | bytes 786440 | tf_op jit(solution)/shard_map/ppermute | solution.py:391
  83.0 9.9 %collective-permute-start.31 = (bf16[2,64,1024]{2,1,0:T(8,128)(2,1)S(1)}, bf16[2,64,1024]{2,1,0:T(8,128)(2,1)S(1)}, u32[]{:S(2)}, u32[]{:S(2)}) collective-permute-start(bf16[2,64,1024]{2,1,0:T(8,128)(2,1)S(1)} %get-tuple-element.220), channel_id=1, source_target_pairs={{2,0},{4,2},{6,4},{7,6},{5,7},{3,5},{1,3},{0,1},{10,8},{12,10},{14... | collective-permute-start | bytes 786440 | tf_op jit(solution)/shard_map/ppermute | solution.py:391
  87.4 10.0 %collective-permute-start.28 = (bf16[2,64,1024]{2,1,0:T(8,128)(2,1)S(1)}, bf16[2,64,1024]{2,1,0:T(8,128)(2,1)S(1)}, u32[]{:S(2)}, u32[]{:S(2)}) collective-permute-start(bf16[2,64,1024]{2,1,0:T(8,128)(2,1)S(1)} %get-tuple-element.213.refs_6_.refs_0_), channel_id=1, source_target_pairs={{0,2},{2,4},{4,6},{6,7},{7,5},{5,3},{3,1},{1,0},{8,10},{10,12},{12... | collective-permute-start | bytes 786440 | tf_op jit(solution)/shard_map/ppermute | solution.py:391
  89.0 9.5 %collective-permute-start.29 = (bf16[2,64,1024]{2,1,0:T(8,128)(2,1)S(1)}, bf16[2,64,1024]{2,1,0:T(8,128)(2,1)S(1)}, u32[]{:S(2)}, u32[]{:S(2)}) collective-permute-start(bf16[2,64,1024]{2,1,0:T(8,128)(2,1)S(1)} %get-tuple-element.216), channel_id=1, source_target_pairs={{2,0},{4,2},{6,4},{7,6},{5,7},{3,5},{1,3},{0,1},{10,8},{12,10},{14... | collective-permute-start | bytes 786440 | tf_op jit(solution)/shard_map/ppermute | solution.py:391
  93.0 10.0 %collective-permute-start.34 = (bf16[2,64,1024]{2,1,0:T(8,128)(2,1)S(1)}, bf16[2,64,1024]{2,1,0:T(8,128)(2,1)S(1)}, u32[]{:S(2)}, u32[]{:S(2)}) collective-permute-start(bf16[2,64,1024]{2,1,0:T(8,128)(2,1)S(1)} %get-tuple-element.221.refs_0_), channel_id=1, source_target_pairs={{0,2},{2,4},{4,6},{6,7},{7,5},{5,3},{3,1},{1,0},{8,10},{10,12},{12... | collective-permute-start | bytes 786440 | tf_op jit(solution)/shard_map/ppermute | solution.py:391
  94.6 9.5 %collective-permute-start.35 = (bf16[2,64,1024]{2,1,0:T(8,128)(2,1)S(1)}, bf16[2,64,1024]{2,1,0:T(8,128)(2,1)S(1)}, u32[]{:S(2)}, u32[]{:S(2)}) collective-permute-start(bf16[2,64,1024]{2,1,0:T(8,128)(2,1)S(1)} %get-tuple-element.228), channel_id=1, source_target_pairs={{2,0},{4,2},{6,4},{7,6},{5,7},{3,5},{1,3},{0,1},{10,8},{12,10},{14... | collective-permute-start | bytes 786440 | tf_op jit(solution)/shard_map/ppermute | solution.py:391
  98.6 10.0 %collective-permute-start.32 = (bf16[2,64,1024]{2,1,0:T(8,128)(2,1)S(1)}, bf16[2,64,1024]{2,1,0:T(8,128)(2,1)S(1)}, u32[]{:S(2)}, u32[]{:S(2)}) collective-permute-start(bf16[2,64,1024]{2,1,0:T(8,128)(2,1)S(1)} %get-tuple-element.222.refs_6_.refs_0_), channel_id=1, source_target_pairs={{0,2},{2,4},{4,6},{6,7},{7,5},{5,3},{3,1},{1,0},{8,10},{10,12},{12... | collective-permute-start | bytes 786440 | tf_op jit(solution)/shard_map/ppermute | solution.py:391
  100.2 9.5 %collective-permute-start.33 = (bf16[2,64,1024]{2,1,0:T(8,128)(2,1)S(1)}, bf16[2,64,1024]{2,1,0:T(8,128)(2,1)S(1)}, u32[]{:S(2)}, u32[]{:S(2)}) collective-permute-start(bf16[2,64,1024]{2,1,0:T(8,128)(2,1)S(1)} %get-tuple-element.225), channel_id=1, source_target_pairs={{2,0},{4,2},{6,4},{7,6},{5,7},{3,5},{1,3},{0,1},{10,8},{12,10},{14... | collective-permute-start | bytes 786440 | tf_op jit(solution)/shard_map/ppermute | solution.py:391
  104.2 11.1 %collective-permute-start.37 = (bf16[2,64,1024]{2,1,0:T(8,128)(2,1)S(1)}, bf16[2,64,1024]{2,1,0:T(8,128)(2,1)S(1)}, u32[]{:S(2)}, u32[]{:S(2)}) collective-permute-start(bf16[2,64,1024]{2,1,0:T(8,128)(2,1)S(1)} %get-tuple-element.233), channel_id=1, source_target_pairs={{2,0},{4,2},{6,4},{7,6},{5,7},{3,5},{1,3},{0,1},{10,8},{12,10},{14... | collective-permute-start | bytes 786440 | tf_op jit(solution)/shard_map/ppermute | solution.py:391
  104.9 10.4 %collective-permute-start.38 = (bf16[2,64,1024]{2,1,0:T(8,128)(2,1)S(1)}, bf16[2,64,1024]{2,1,0:T(8,128)(2,1)S(1)}, u32[]{:S(2)}, u32[]{:S(2)}) collective-permute-start(bf16[2,64,1024]{2,1,0:T(8,128)(2,1)S(1)} %get-tuple-element.229.refs_0_), channel_id=1, source_target_pairs={{0,2},{2,4},{4,6},{6,7},{7,5},{5,3},{3,1},{1,0},{8,10},{10,12},{12... | collective-permute-start | bytes 786440 | tf_op jit(solution)/shard_map/ppermute | solution.py:391
  109.8 8.1 %collective-permute-start.36 = (bf16[2,64,1024]{2,1,0:T(8,128)(2,1)S(1)}, bf16[2,64,1024]{2,1,0:T(8,128)(2,1)S(1)}, u32[]{:S(2)}, u32[]{:S(2)}) collective-permute-start(bf16[2,64,1024]{2,1,0:T(8,128)(2,1)S(1)} %get-tuple-element.230.refs_6_), channel_id=1, source_target_pairs={{0,2},{2,4},{4,6},{6,7},{7,5},{5,3},{3,1},{1,0},{8,10},{10,12},{12... | collective-permute-start | bytes 786440 | tf_op jit(solution)/shard_map/ppermute | solution.py:391
  111.5 7.6 %collective-permute-start.39 = (bf16[2,64,1024]{2,1,0:T(8,128)(2,1)S(1)}, bf16[2,64,1024]{2,1,0:T(8,128)(2,1)S(1)}, u32[]{:S(2)}, u32[]{:S(2)}) collective-permute-start(bf16[2,64,1024]{2,1,0:T(8,128)(2,1)S(1)} %get-tuple-element.234), channel_id=1, source_target_pairs={{2,0},{4,2},{6,4},{7,6},{5,7},{3,5},{1,3},{0,1},{10,8},{12,10},{14... | collective-permute-start | bytes 786440 | tf_op jit(solution)/shard_map/ppermute | solution.py:391
  (10 other events, 46.0 us)

commit v4 on v2

--- a/solution.py
+++ b/solution.py
@@ -347,23 +347,49 @@
     )(*inputs)
 
 
-def final_kernel(low, high, low_r, low_l, high_r, high_l, conv, mix):
-    conv[0:2] = low[...] + (low_r[...].astype(F32) + low_l[...].astype(F32))
-    total = high[...] + (high_r[...].astype(F32) + high_l[...].astype(F32))
-    conv[2] = total[0]
-    mix[...] = total[1]
-
-
-def final_call(*blocks):
-    part, wide = blocks[0].shape[1:]
-    return pl.pallas_call(
-        final_kernel,
-        out_shape=[jax.ShapeDtypeStruct((3, part, wide), F32), jax.ShapeDtypeStruct((part, wide), F32)],
-        in_specs=[VMEM] * 6,
-        out_specs=[VMEM] * 2,
-        compiler_params=PARAMS,
-        cost_estimate=cost(2**19, 2**20),
-    )(*in_vmem(*blocks))
+def final_low_kernel(mine, right, left, conv, total, sem):
+    total[...] = mine[...] + (right[...].astype(F32) + left[...].astype(F32))
+    copy = pltpu.make_async_copy(total, conv.at[0:2], sem)
+    copy.start()
+    copy.wait()
+
+
+def final_high_kernel(mine, right, left, _conv, conv, mix, total, sems):
+    total[...] = mine[...] + (right[...].astype(F32) + left[...].astype(F32))
+    copies = [
+        pltpu.make_async_copy(total.at[0], conv.at[2], sems.at[0]),
+        pltpu.make_async_copy(total.at[1], mix, sems.at[1]),
+    ]
+    for copy in copies:
+        copy.start()
+    for copy in copies:
+        copy.wait()
+
+
+def final_call(low, high, low_r, low_l, high_r, high_l):
+    part, wide = low.shape[1:]
+    anywhere = pl.BlockSpec(memory_space=pl.ANY)
+    conv_shape = jax.ShapeDtypeStruct((3, part, wide), F32)
+    estimate = cost(2**18, 2**19)
+    conv = pl.pallas_call(
+        final_low_kernel,
+        out_shape=conv_shape,
+        in_specs=[VMEM] * 3,
+        out_specs=anywhere,
+        scratch_shapes=[pltpu.VMEM(low.shape, F32), pltpu.SemaphoreType.DMA],
+        compiler_params=PARAMS,
+        cost_estimate=estimate,
+    )(*in_vmem(low, low_r, low_l))
+    return pl.pallas_call(
+        final_high_kernel,
+        out_shape=[conv_shape, jax.ShapeDtypeStruct((part, wide), F32)],
+        in_specs=[VMEM] * 3 + [anywhere],
+        out_specs=[anywhere] * 2,
+        scratch_shapes=[pltpu.VMEM(high.shape, F32), pltpu.SemaphoreType.DMA((2,))],
+        input_output_aliases={3: 0},
+        compiler_params=PARAMS,
+        cost_estimate=estimate,
+    )(*in_vmem(high, high_r, high_l), conv)
 
 
 def local(x_ckpt, top_cot, skip_cot, w_conv, w_mix):

time: 120 us -> 121 us (level)
  transfers between devices with their start and end apart: 40 -> 40, of which waited for: 29 -> 28; matrix products, arithmetic and copies ran while one was open for 1% -> 1% of each run, Pallas kernels for 19% -> 19%
where the time goes in v4:
time: 121 us; the launch traced here: 120 us
  waiting for transfers between devices  46.7 us (39%)
  starting transfers between devices  41.6 us (34%)
  Pallas kernels  28.5 us (24%)
  local copies, waits for them, and re-layouts  1.32 us (1%)
  between operations  1.28 us (1%)
    ppermute x15, starting transfers between devices, send(): lax.ppermute(to_right, 'dp', right)  23.7 us
    ppermute x15, waiting for transfers between devices, send(): lax.ppermute(to_left, 'dp', left)  21.5 us
    ppermute x15, waiting for transfers between devices, send(): lax.ppermute(to_right, 'dp', right)  15.9 us
    ppermute x8, waiting for transfers between devices, local(): g[m][half_at] = lax.ppermute(piece, 'pipe', [(stage, stage - 1)])  9.4 us
    pallas_call x5, Pallas kernels, term_call(): pl.pallas_call(functools.partial(term_kernel, replicas, offsets, micro),...  9.13 us
    ppermute x15, starting transfers between devices, send(): lax.ppermute(to_left, 'dp', left)  8.25 us
    ppermute x8, starting transfers between devices, local(): g[m][half_at] = lax.ppermute(piece, 'pipe', [(stage, stage - 1)])  8.1 us
    pallas_call x7, Pallas kernels, partial_call(): pl.pallas_call(functools.partial(partial_kernel, replicas, items, not hel...  6.69 us
  transfers between devices with their start and end apart: 40, of which 28 were waited for; matrix products, arithmetic and copies ran while one was open for 1% of the time, Pallas kernels for 19%

profile of v4, /device:TPU:0, one launch (start us, length us, event | category | flops | bytes accessed | tf_op | source)
XLA Modules:
  0.0 120.5 jit_solution(11403909704267201166)
XLA Ops:
  1.7 3.1 %collective-permute-start.2 = (bf16[2,64,1024]{2,1,0:T(8,128)(2,1)S(1)}, bf16[2,64,1024]{2,1,0:T(8,128)(2,1)S(1)}, u32[]{:S(2)}, u32[]{:S(2)}) collective-permute-start(bf16[2,64,1024]{2,1,0:T(8,128)(2,1)S(1)} %get-tuple-element.121.refs_0_), channel_id=1, source_target_pairs={{0,2},{2,4},{4,6},{6,7},{7,5},{5,3},{3,1},{1,0},{8,10},{10,12},{12... | collective-permute-start | bytes 786440 | tf_op jit(solution)/shard_map/ppermute | solution.py:404
  4.8 2.0 %collective-permute-start = (bf16[2,64,1024]{2,1,0:T(8,128)(2,1)S(1)}, bf16[2,64,1024]{2,1,0:T(8,128)(2,1)S(1)}, u32[]{:S(2)}, u32[]{:S(2)}) collective-permute-start(bf16[2,64,1024]{2,1,0:T(8,128)(2,1)S(1)} %get-tuple-element.120.refs_1_), channel_id=1, source_target_pairs={{0,2},{2,4},{4,6},{6,7},{7,5},{5,3},{3,1},{1,0},{8,10},{10,12},{12... | collective-permute-start | bytes 786440 | tf_op jit(solution)/shard_map/ppermute | solution.py:404
  10.2 1.7 %collective-permute-done.2.refs_0_ = bf16[2,64,1024]{2,1,0:T(8,128)(2,1)S(1)} collective-permute-done((bf16[2,64,1024]{2,1,0:T(8,128)(2,1)S(1)}, bf16[2,64,1024]{2,1,0:T(8,128)(2,1)S(1)}, u32[]{:S(2)}, u32[]{:S(2)}) %collective-permute-start.2) | collective-permute-done | bytes 262176 | tf_op jit(solution)/shard_map/ppermute | solution.py:404
  11.9 2.2 %collective-permute-done.3.refs_1_ = bf16[2,64,1024]{2,1,0:T(8,128)(2,1)S(1)} collective-permute-done((bf16[2,64,1024]{2,1,0:T(8,128)(2,1)S(1)}, bf16[2,64,1024]{2,1,0:T(8,128)(2,1)S(1)}, u32[]{:S(2)}, u32[]{:S(2)}) %collective-permute-start.3) | collective-permute-done | bytes 262176 | tf_op jit(solution)/shard_map/ppermute | solution.py:404
  15.0 1.6 %collective-permute-start.6 = (bf16[2,64,1024]{2,1,0:T(8,128)(2,1)S(1)}, bf16[2,64,1024]{2,1,0:T(8,128)(2,1)S(1)}, u32[]{:S(2)}, u32[]{:S(2)}) collective-permute-start(bf16[2,64,1024]{2,1,0:T(8,128)(2,1)S(1)} %get-tuple-element.128), channel_id=1, source_target_pairs={{0,2},{2,4},{4,6},{6,7},{7,5},{5,3},{3,1},{1,0},{8,10},{10,12},{12... | collective-permute-start | bytes 786440 | tf_op jit(solution)/shard_map/ppermute | solution.py:404
  17.5 2.2 %collective-permute-done.1.refs_1_ = bf16[2,64,1024]{2,1,0:T(8,128)(2,1)S(1)} collective-permute-done((bf16[2,64,1024]{2,1,0:T(8,128)(2,1)S(1)}, bf16[2,64,1024]{2,1,0:T(8,128)(2,1)S(1)}, u32[]{:S(2)}, u32[]{:S(2)}) %collective-permute-start.1) | collective-permute-done | bytes 262176 | tf_op jit(solution)/shard_map/ppermute | solution.py:404
  20.6 1.6 %collective-permute-start.4 = (bf16[2,64,1024]{2,1,0:T(8,128)(2,1)S(1)}, bf16[2,64,1024]{2,1,0:T(8,128)(2,1)S(1)}, u32[]{:S(2)}, u32[]{:S(2)}) collective-permute-start(bf16[2,64,1024]{2,1,0:T(8,128)(2,1)S(1)} %get-tuple-element.126), channel_id=1, source_target_pairs={{0,2},{2,4},{4,6},{6,7},{7,5},{5,3},{3,1},{1,0},{8,10},{10,12},{12... | collective-permute-start | bytes 786440 | tf_op jit(solution)/shard_map/ppermute | solution.py:404
  24.1 1.7 %collective-permute-done.7.refs_1_ = bf16[2,64,1024]{2,1,0:T(8,128)(2,1)S(1)} collective-permute-done((bf16[2,64,1024]{2,1,0:T(8,128)(2,1)S(1)}, bf16[2,64,1024]{2,1,0:T(8,128)(2,1)S(1)}, u32[]{:S(2)}, u32[]{:S(2)}) %collective-permute-start.7) | collective-permute-done | bytes 262176 | tf_op jit(solution)/shard_map/ppermute | solution.py:404
  26.8 1.6 %collective-permute-start.10 = (bf16[2,64,1024]{2,1,0:T(8,128)(2,1)S(1)}, bf16[2,64,1024]{2,1,0:T(8,128)(2,1)S(1)}, u32[]{:S(2)}, u32[]{:S(2)}) collective-permute-start(bf16[2,64,1024]{2,1,0:T(8,128)(2,1)S(1)} %get-tuple-element.136), channel_id=1, source_target_pairs={{0,2},{2,4},{4,6},{6,7},{7,5},{5,3},{3,1},{1,0},{8,10},{10,12},{12... | collective-permute-start | bytes 786440 | tf_op jit(solution)/shard_map/ppermute | solution.py:404
  29.9 1.5 %collective-permute-done.5.refs_1_ = bf16[2,64,1024]{2,1,0:T(8,128)(2,1)S(1)} collective-permute-done((bf16[2,64,1024]{2,1,0:T(8,128)(2,1)S(1)}, bf16[2,64,1024]{2,1,0:T(8,128)(2,1)S(1)}, u32[]{:S(2)}, u32[]{:S(2)}) %collective-permute-start.5) | collective-permute-done | bytes 262176 | tf_op jit(solution)/shard_map/ppermute | solution.py:404
  32.4 1.6 %collective-permute-start.8 = (bf16[2,64,1024]{2,1,0:T(8,128)(2,1)S(1)}, bf16[2,64,1024]{2,1,0:T(8,128)(2,1)S(1)}, u32[]{:S(2)}, u32[]{:S(2)}) collective-permute-start(bf16[2,64,1024]{2,1,0:T(8,128)(2,1)S(1)} %get-tuple-element.134), channel_id=1, source_target_pairs={{0,2},{2,4},{4,6},{6,7},{7,5},{5,3},{3,1},{1,0},{8,10},{10,12},{12... | collective-permute-start | bytes 786440 | tf_op jit(solution)/shard_map/ppermute | solution.py:404
  35.9 1.7 %collective-permute-done.11.refs_1_ = bf16[2,64,1024]{2,1,0:T(8,128)(2,1)S(1)} collective-permute-done((bf16[2,64,1024]{2,1,0:T(8,128)(2,1)S(1)}, bf16[2,64,1024]{2,1,0:T(8,128)(2,1)S(1)}, u32[]{:S(2)}, u32[]{:S(2)}) %collective-permute-start.11) | collective-permute-done | bytes 262176 | tf_op jit(solution)/shard_map/ppermute | solution.py:404
  40.8 2.5 %collective-permute-start.14 = (bf16[1,64,1024]{2,1,0:T(8,128)(2,1)S(1)}, bf16[1,64,1024]{2,1,0:T(8,128)(2,1)S(1)}, u32[]{:S(2)}, u32[]{:S(2)}) collective-permute-start(bf16[1,64,1024]{2,1,0:T(8,128)(2,1)S(1)} %slice.10), channel_id=1, source_target_pairs={{0,2},{2,4},{4,6},{6,7},{7,5},{5,3},{3,1},{1,0},{8,10},{10,12},{12... | collective-permute-start | bytes 393224 | tf_op jit(solution)/shard_map/ppermute | solution.py:404
  46.0 2.4 %collective-permute-done.15.refs_1_ = bf16[1,64,1024]{2,1,0:T(8,128)(2,1)S(1)} collective-permute-done((bf16[1,64,1024]{2,1,0:T(8,128)(2,1)S(1)}, bf16[1,64,1024]{2,1,0:T(8,128)(2,1)S(1)}, u32[]{:S(2)}, u32[]{:S(2)}) %collective-permute-start.15) | collective-permute-done | bytes 131104 | tf_op jit(solution)/shard_map/ppermute | solution.py:404
  57.3 1.5 %collective-permute-start.25 = (bf16[256,512]{1,0:T(8,128)(2,1)S(1)}, bf16[256,512]{1,0:T(8,128)(2,1)S(1)}, u32[]{:S(2)}, u32[]{:S(2)}) collective-permute-start(bf16[256,512]{1,0:T(8,128)(2,1)S(1)} %get-tuple-element.194), channel_id=1, source_target_pairs={{8,0},{9,1},{10,2},{11,3},{12,4},{13,5},{14,6},{15,7}} | collective-permute-start | bytes 786440 | tf_op jit(solution)/shard_map/ppermute | solution.py:455
  60.2 5.1 %collective-permute-done.20.g = bf16[256,512]{1,0:T(8,128)(2,1)S(1)} collective-permute-done((bf16[256,512]{1,0:T(8,128)(2,1)S(1)}, bf16[256,512]{1,0:T(8,128)(2,1)S(1)}, u32[]{:S(2)}, u32[]{:S(2)}) %collective-permute-start.20) | collective-permute-done | bytes 262176 | tf_op jit(solution)/shard_map/ppermute | solution.py:455
  65.3 1.5 %shard_map.91 = (bf16[512,1024]{1,0:T(8,128)(2,1)S(1)}, bf16[512,512]{1,0:T(8,128)(2,1)S(1)}, bf16[512,512]{1,0:T(8,128)(2,1)S(1)}, f32[2,16,512]{2,1,0:T(8,128)S(1)}) custom-call(bf16[256,512]{1,0:T(8,128)(2,1)S(1)} %collective-permute-done.20.g, bf16[2,512,512]{2,1,0:T(8,128)(2,1)S(1)} %bitcast.30, ...), custom_call_target="tpu_custom_call", output_to_operand_aliasing={{0}: (5, {}), {1}: (6, {}), {2}: (7, {})} | custom-call | flops 536870912 | bytes 4194304 | tf_op jit(solution)/shard_map/pallas_call | solution.py:255
  68.2 1.5 %shard_map.92 = (bf16[512,1024]{1,0:T(8,128)(2,1)S(1)}, bf16[512,512]{1,0:T(8,128)(2,1)S(1)}, bf16[512,512]{1,0:T(8,128)(2,1)S(1)}) custom-call(bf16[256,512]{1,0:T(8,128)(2,1)S(1)} %collective-permute-done.19.g, bf16[2,512,512]{2,1,0:T(8,128)(2,1)S(1)} %bitcast.31, ...), custom_call_target="tpu_custom_call", output_to_operand_aliasing={{0}: (6, {}), {1}: (7, {}), {2}: (8, {})} | custom-call | flops 536870912 | bytes 4194304 | tf_op jit(solution)/shard_map/pallas_call | solution.py:255
  72.5 1.6 %collective-permute-done.24.g = bf16[256,512]{1,0:T(8,128)(2,1)S(1)} collective-permute-done((bf16[256,512]{1,0:T(8,128)(2,1)S(1)}, bf16[256,512]{1,0:T(8,128)(2,1)S(1)}, u32[]{:S(2)}, u32[]{:S(2)}) %collective-permute-start.24) | collective-permute-done | bytes 262176 | tf_op jit(solution)/shard_map/ppermute | solution.py:455
  74.1 1.5 %shard_map.100 = (bf16[512,1024]{1,0:T(8,128)(2,1)S(1)}, bf16[512,512]{1,0:T(8,128)(2,1)S(1)}, bf16[512,512]{1,0:T(8,128)(2,1)S(1)}) custom-call(bf16[256,512]{1,0:T(8,128)(2,1)S(1)} %collective-permute-done.24.g, bf16[2,512,512]{2,1,0:T(8,128)(2,1)S(1)} %bitcast.33, ...), custom_call_target="tpu_custom_call", output_to_operand_aliasing={{0}: (6, {}), {1}: (7, {}), {2}: (8, {})} | custom-call | flops 536870912 | bytes 4194304 | tf_op jit(solution)/shard_map/pallas_call | solution.py:255
  76.5 1.7 %collective-permute-start.26 = (bf16[2,64,1024]{2,1,0:T(8,128)(2,1)S(1)}, bf16[2,64,1024]{2,1,0:T(8,128)(2,1)S(1)}, u32[]{:S(2)}, u32[]{:S(2)}) collective-permute-start(bf16[2,64,1024]{2,1,0:T(8,128)(2,1)S(1)} %get-tuple-element.209.refs_6_), channel_id=1, source_target_pairs={{0,2},{2,4},{4,6},{6,7},{7,5},{5,3},{3,1},{1,0},{8,10},{10,12},{12... | collective-permute-start | bytes 786440 | tf_op jit(solution)/shard_map/ppermute | solution.py:404
  78.6 2.2 %shard_map.102 = (bf16[2,64,1024]{2,1,0:T(8,128)(2,1)S(1)}, bf16[2,64,1024]{2,1,0:T(8,128)(2,1)S(1)}, bf16[2,64,1024]{2,1,0:T(8,128)(2,1)S(1)}, bf16[2,64,1024]{2,1,0:T(8,128)(2,1)S(1)}) custom-call(bf16[1536,1024]{1,0:T(8,128)(2,1)S(1)} %shard_map.76.taps_t, bf16[2,512,512]{2,1,0:T(8,128)(2,1)S(1)} %bitcast.35, ...), custom_call_target="tpu_custom_call" | custom-call | flops 1073741824 | bytes 1048576 | tf_op jit(solution)/shard_map/pallas_call | solution.py:322
  80.8 1.7 %collective-permute-start.30 = (bf16[2,64,1024]{2,1,0:T(8,128)(2,1)S(1)}, bf16[2,64,1024]{2,1,0:T(8,128)(2,1)S(1)}, u32[]{:S(2)}, u32[]{:S(2)}) collective-permute-start(bf16[2,64,1024]{2,1,0:T(8,128)(2,1)S(1)} %get-tuple-element.219), channel_id=1, source_target_pairs={{0,2},{2,4},{4,6},{6,7},{7,5},{5,3},{3,1},{1,0},{8,10},{10,12},{12... | collective-permute-start | bytes 786440 | tf_op jit(solution)/shard_map/ppermute | solution.py:404
  82.9 2.4 %collective-permute-done.26.got_r = bf16[2,64,1024]{2,1,0:T(8,128)(2,1)S(1)} collective-permute-done((bf16[2,64,1024]{2,1,0:T(8,128)(2,1)S(1)}, bf16[2,64,1024]{2,1,0:T(8,128)(2,1)S(1)}, u32[]{:S(2)}, u32[]{:S(2)}) %collective-permute-start.26) | collective-permute-done | bytes 262176 | tf_op jit(solution)/shard_map/ppermute | solution.py:404
  88.9 2.2 %shard_map.104 = (bf16[2,64,1024]{2,1,0:T(8,128)(2,1)S(1)}, bf16[2,64,1024]{2,1,0:T(8,128)(2,1)S(1)}, bf16[2,64,1024]{2,1,0:T(8,128)(2,1)S(1)}, bf16[2,64,1024]{2,1,0:T(8,128)(2,1)S(1)}) custom-call(bf16[1536,1024]{1,0:T(8,128)(2,1)S(1)} %shard_map.76.taps_t, bf16[2,512,512]{2,1,0:T(8,128)(2,1)S(1)} %bitcast.36, ...), custom_call_target="tpu_custom_call" | custom-call | flops 1073741824 | bytes 1048576 | tf_op jit(solution)/shard_map/pallas_call | solution.py:322
  94.5 2.0 %collective-permute-done.28.got_r = bf16[2,64,1024]{2,1,0:T(8,128)(2,1)S(1)} collective-permute-done((bf16[2,64,1024]{2,1,0:T(8,128)(2,1)S(1)}, bf16[2,64,1024]{2,1,0:T(8,128)(2,1)S(1)}, u32[]{:S(2)}, u32[]{:S(2)}) %collective-permute-start.28) | collective-permute-done | bytes 262176 | tf_op jit(solution)/shard_map/ppermute | solution.py:404
  100.1 2.2 %shard_map.107 = (bf16[2,64,1024]{2,1,0:T(8,128)(2,1)S(1)}, bf16[2,64,1024]{2,1,0:T(8,128)(2,1)S(1)}, bf16[2,64,1024]{2,1,0:T(8,128)(2,1)S(1)}, bf16[2,64,1024]{2,1,0:T(8,128)(2,1)S(1)}) custom-call(bf16[1536,1024]{1,0:T(8,128)(2,1)S(1)} %shard_map.76.taps_t, bf16[2,512,512]{2,1,0:T(8,128)(2,1)S(1)} %bitcast.37, ...), custom_call_target="tpu_custom_call" | custom-call | flops 1073741824 | bytes 1048576 | tf_op jit(solution)/shard_map/pallas_call | solution.py:322
  104.1 1.8 %collective-permute-done.32.got_r = bf16[2,64,1024]{2,1,0:T(8,128)(2,1)S(1)} collective-permute-done((bf16[2,64,1024]{2,1,0:T(8,128)(2,1)S(1)}, bf16[2,64,1024]{2,1,0:T(8,128)(2,1)S(1)}, u32[]{:S(2)}, u32[]{:S(2)}) %collective-permute-start.32) | collective-permute-done | bytes 262176 | tf_op jit(solution)/shard_map/ppermute | solution.py:404
  105.9 3.3 %collective-permute-done.33.got_l = bf16[2,64,1024]{2,1,0:T(8,128)(2,1)S(1)} collective-permute-done((bf16[2,64,1024]{2,1,0:T(8,128)(2,1)S(1)}, bf16[2,64,1024]{2,1,0:T(8,128)(2,1)S(1)}, u32[]{:S(2)}, u32[]{:S(2)}) %collective-permute-start.33) | collective-permute-done | bytes 262176 | tf_op jit(solution)/shard_map/ppermute | solution.py:404
  113.4 1.7 %shard_map.110 = (f32[2,64,1024]{2,1,0:T(8,128)S(1)}, f32[2,64,1024]{2,1,0:T(8,128)S(1)}) custom-call(bf16[1536,1024]{1,0:T(8,128)(2,1)S(1)} %shard_map.76.taps_t, bf16[2,512,512]{2,1,0:T(8,128)(2,1)S(1)} %bitcast.38, bf16[512,512]{1,0:T(8,128)(2,1)S(1)} %get-tuple-element.203.refs_0_, bf16[512,512]{1,0:T(8,128)(2,1)S(1)} %get-tuple-element.204.refs_1_, ...), custom_call_target="tpu_custom_call" | custom-call | flops 536870912 | bytes 1048576 | tf_op jit(solution)/shard_map/pallas_call | solution.py:322
  115.1 1.5 %collective-permute-done.38.right = bf16[2,64,1024]{2,1,0:T(8,128)(2,1)S(1)} collective-permute-done((bf16[2,64,1024]{2,1,0:T(8,128)(2,1)S(1)}, bf16[2,64,1024]{2,1,0:T(8,128)(2,1)S(1)}, u32[]{:S(2)}, u32[]{:S(2)}) %collective-permute-start.38) | collective-permute-done | bytes 262176 | tf_op jit(solution)/shard_map/ppermute | solution.py:404
  117.5 1.9 %collective-permute-done.36.right = bf16[2,64,1024]{2,1,0:T(8,128)(2,1)S(1)} collective-permute-done((bf16[2,64,1024]{2,1,0:T(8,128)(2,1)S(1)}, bf16[2,64,1024]{2,1,0:T(8,128)(2,1)S(1)}, u32[]{:S(2)}, u32[]{:S(2)}) %collective-permute-start.36) | collective-permute-done | bytes 262176 | tf_op jit(solution)/shard_map/ppermute | solution.py:404
  (95 shorter events, 54.5 us)
Async XLA Ops:
  1.7 10.2 %collective-permute-start.2 = (bf16[2,64,1024]{2,1,0:T(8,128)(2,1)S(1)}, bf16[2,64,1024]{2,1,0:T(8,128)(2,1)S(1)}, u32[]{:S(2)}, u32[]{:S(2)}) collective-permute-start(bf16[2,64,1024]{2,1,0:T(8,128)(2,1)S(1)} %get-tuple-element.121.refs_0_), channel_id=1, source_target_pairs={{0,2},{2,4},{4,6},{6,7},{7,5},{5,3},{3,1},{1,0},{8,10},{10,12},{12... | collective-permute-start | bytes 786440 | tf_op jit(solution)/shard_map/ppermute | solution.py:404
  4.8 9.2 %collective-permute-start.3 = (bf16[2,64,1024]{2,1,0:T(8,128)(2,1)S(1)}, bf16[2,64,1024]{2,1,0:T(8,128)(2,1)S(1)}, u32[]{:S(2)}, u32[]{:S(2)}) collective-permute-start(bf16[2,64,1024]{2,1,0:T(8,128)(2,1)S(1)} %get-tuple-element.121.refs_0_), channel_id=1, source_target_pairs={{2,0},{4,2},{6,4},{7,6},{5,7},{3,5},{1,3},{0,1},{10,8},{12,10},{14... | collective-permute-start | bytes 786440 | tf_op jit(solution)/shard_map/ppermute | solution.py:404
  4.8 12.7 %collective-permute-start = (bf16[2,64,1024]{2,1,0:T(8,128)(2,1)S(1)}, bf16[2,64,1024]{2,1,0:T(8,128)(2,1)S(1)}, u32[]{:S(2)}, u32[]{:S(2)}) collective-permute-start(bf16[2,64,1024]{2,1,0:T(8,128)(2,1)S(1)} %get-tuple-element.120.refs_1_), channel_id=1, source_target_pairs={{0,2},{2,4},{4,6},{6,7},{7,5},{5,3},{3,1},{1,0},{8,10},{10,12},{12... | collective-permute-start | bytes 786440 | tf_op jit(solution)/shard_map/ppermute | solution.py:404
  6.8 12.8 %collective-permute-start.1 = (bf16[2,64,1024]{2,1,0:T(8,128)(2,1)S(1)}, bf16[2,64,1024]{2,1,0:T(8,128)(2,1)S(1)}, u32[]{:S(2)}, u32[]{:S(2)}) collective-permute-start(bf16[2,64,1024]{2,1,0:T(8,128)(2,1)S(1)} %get-tuple-element.120.refs_1_), channel_id=1, source_target_pairs={{2,0},{4,2},{6,4},{7,6},{5,7},{3,5},{1,3},{0,1},{10,8},{12,10},{14... | collective-permute-start | bytes 786440 | tf_op jit(solution)/shard_map/ppermute | solution.py:404
  15.0 9.0 %collective-permute-start.6 = (bf16[2,64,1024]{2,1,0:T(8,128)(2,1)S(1)}, bf16[2,64,1024]{2,1,0:T(8,128)(2,1)S(1)}, u32[]{:S(2)}, u32[]{:S(2)}) collective-permute-start(bf16[2,64,1024]{2,1,0:T(8,128)(2,1)S(1)} %get-tuple-element.128), channel_id=1, source_target_pairs={{0,2},{2,4},{4,6},{6,7},{7,5},{5,3},{3,1},{1,0},{8,10},{10,12},{12... | collective-permute-start | bytes 786440 | tf_op jit(solution)/shard_map/ppermute | solution.py:404
  16.6 9.2 %collective-permute-start.7 = (bf16[2,64,1024]{2,1,0:T(8,128)(2,1)S(1)}, bf16[2,64,1024]{2,1,0:T(8,128)(2,1)S(1)}, u32[]{:S(2)}, u32[]{:S(2)}) collective-permute-start(bf16[2,64,1024]{2,1,0:T(8,128)(2,1)S(1)} %get-tuple-element.129), channel_id=1, source_target_pairs={{2,0},{4,2},{6,4},{7,6},{5,7},{3,5},{1,3},{0,1},{10,8},{12,10},{14... | collective-permute-start | bytes 786440 | tf_op jit(solution)/shard_map/ppermute | solution.py:404
  20.6 9.3 %collective-permute-start.4 = (bf16[2,64,1024]{2,1,0:T(8,128)(2,1)S(1)}, bf16[2,64,1024]{2,1,0:T(8,128)(2,1)S(1)}, u32[]{:S(2)}, u32[]{:S(2)}) collective-permute-start(bf16[2,64,1024]{2,1,0:T(8,128)(2,1)S(1)} %get-tuple-element.126), channel_id=1, source_target_pairs={{0,2},{2,4},{4,6},{6,7},{7,5},{5,3},{3,1},{1,0},{8,10},{10,12},{12... | collective-permute-start | bytes 786440 | tf_op jit(solution)/shard_map/ppermute | solution.py:404
  22.2 9.2 %collective-permute-start.5 = (bf16[2,64,1024]{2,1,0:T(8,128)(2,1)S(1)}, bf16[2,64,1024]{2,1,0:T(8,128)(2,1)S(1)}, u32[]{:S(2)}, u32[]{:S(2)}) collective-permute-start(bf16[2,64,1024]{2,1,0:T(8,128)(2,1)S(1)} %get-tuple-element.127), channel_id=1, source_target_pairs={{2,0},{4,2},{6,4},{7,6},{5,7},{3,5},{1,3},{0,1},{10,8},{12,10},{14... | collective-permute-start | bytes 786440 | tf_op jit(solution)/shard_map/ppermute | solution.py:404
  26.8 9.1 %collective-permute-start.10 = (bf16[2,64,1024]{2,1,0:T(8,128)(2,1)S(1)}, bf16[2,64,1024]{2,1,0:T(8,128)(2,1)S(1)}, u32[]{:S(2)}, u32[]{:S(2)}) collective-permute-start(bf16[2,64,1024]{2,1,0:T(8,128)(2,1)S(1)} %get-tuple-element.136), channel_id=1, source_target_pairs={{0,2},{2,4},{4,6},{6,7},{7,5},{5,3},{3,1},{1,0},{8,10},{10,12},{12... | collective-permute-start | bytes 786440 | tf_op jit(solution)/shard_map/ppermute | solution.py:404
  28.4 9.2 %collective-permute-start.11 = (bf16[2,64,1024]{2,1,0:T(8,128)(2,1)S(1)}, bf16[2,64,1024]{2,1,0:T(8,128)(2,1)S(1)}, u32[]{:S(2)}, u32[]{:S(2)}) collective-permute-start(bf16[2,64,1024]{2,1,0:T(8,128)(2,1)S(1)} %get-tuple-element.137), channel_id=1, source_target_pairs={{2,0},{4,2},{6,4},{7,6},{5,7},{3,5},{1,3},{0,1},{10,8},{12,10},{14... | collective-permute-start | bytes 786440 | tf_op jit(solution)/shard_map/ppermute | solution.py:404
  32.4 8.4 %collective-permute-start.8 = (bf16[2,64,1024]{2,1,0:T(8,128)(2,1)S(1)}, bf16[2,64,1024]{2,1,0:T(8,128)(2,1)S(1)}, u32[]{:S(2)}, u32[]{:S(2)}) collective-permute-start(bf16[2,64,1024]{2,1,0:T(8,128)(2,1)S(1)} %get-tuple-element.134), channel_id=1, source_target_pairs={{0,2},{2,4},{4,6},{6,7},{7,5},{5,3},{3,1},{1,0},{8,10},{10,12},{12... | collective-permute-start | bytes 786440 | tf_op jit(solution)/shard_map/ppermute | solution.py:404
  34.0 9.4 %collective-permute-start.9 = (bf16[2,64,1024]{2,1,0:T(8,128)(2,1)S(1)}, bf16[2,64,1024]{2,1,0:T(8,128)(2,1)S(1)}, u32[]{:S(2)}, u32[]{:S(2)}) collective-permute-start(bf16[2,64,1024]{2,1,0:T(8,128)(2,1)S(1)} %get-tuple-element.135), channel_id=1, source_target_pairs={{2,0},{4,2},{6,4},{7,6},{5,7},{3,5},{1,3},{0,1},{10,8},{12,10},{14... | collective-permute-start | bytes 786440 | tf_op jit(solution)/shard_map/ppermute | solution.py:404
  38.6 5.0 %collective-permute-start.12 = (bf16[1,64,1024]{2,1,0:T(8,128)(2,1)S(1)}, bf16[1,64,1024]{2,1,0:T(8,128)(2,1)S(1)}, u32[]{:S(2)}, u32[]{:S(2)}) collective-permute-start(bf16[1,64,1024]{2,1,0:T(8,128)(2,1)S(1)} %get-tuple-element.140), channel_id=1, source_target_pairs={{0,2},{2,4},{4,6},{6,7},{7,5},{5,3},{3,1},{1,0},{8,10},{10,12},{12... | collective-permute-start | bytes 393224 | tf_op jit(solution)/shard_map/ppermute | solution.py:404
  40.8 5.2 %collective-permute-start.14 = (bf16[1,64,1024]{2,1,0:T(8,128)(2,1)S(1)}, bf16[1,64,1024]{2,1,0:T(8,128)(2,1)S(1)}, u32[]{:S(2)}, u32[]{:S(2)}) collective-permute-start(bf16[1,64,1024]{2,1,0:T(8,128)(2,1)S(1)} %slice.10), channel_id=1, source_target_pairs={{0,2},{2,4},{4,6},{6,7},{7,5},{5,3},{3,1},{1,0},{8,10},{10,12},{12... | collective-permute-start | bytes 393224 | tf_op jit(solution)/shard_map/ppermute | solution.py:404
  54.6 10.7 %collective-permute-start.20 = (bf16[256,512]{1,0:T(8,128)(2,1)S(1)}, bf16[256,512]{1,0:T(8,128)(2,1)S(1)}, u32[]{:S(2)}, u32[]{:S(2)}) collective-permute-start(bf16[256,512]{1,0:T(8,128)(2,1)S(1)} %get-tuple-element.166), channel_id=1, source_target_pairs={{8,0},{9,1},{10,2},{11,3},{12,4},{13,5},{14,6},{15,7}} | collective-permute-start | bytes 786440 | tf_op jit(solution)/shard_map/ppermute | solution.py:455
  56.0 12.2 %collective-permute-start.19 = (bf16[256,512]{1,0:T(8,128)(2,1)S(1)}, bf16[256,512]{1,0:T(8,128)(2,1)S(1)}, u32[]{:S(2)}, u32[]{:S(2)}) collective-permute-start(bf16[256,512]{1,0:T(8,128)(2,1)S(1)} %get-tuple-element.165.refs_0_), channel_id=1, source_target_pairs={{8,0},{9,1},{10,2},{11,3},{12,4},{13,5},{14,6},{15,7}} | collective-permute-start | bytes 786440 | tf_op jit(solution)/shard_map/ppermute | solution.py:455
  57.3 13.7 %collective-permute-start.25 = (bf16[256,512]{1,0:T(8,128)(2,1)S(1)}, bf16[256,512]{1,0:T(8,128)(2,1)S(1)}, u32[]{:S(2)}, u32[]{:S(2)}) collective-permute-start(bf16[256,512]{1,0:T(8,128)(2,1)S(1)} %get-tuple-element.194), channel_id=1, source_target_pairs={{8,0},{9,1},{10,2},{11,3},{12,4},{13,5},{14,6},{15,7}} | collective-permute-start | bytes 786440 | tf_op jit(solution)/shard_map/ppermute | solution.py:455
  58.9 15.2 %collective-permute-start.24 = (bf16[256,512]{1,0:T(8,128)(2,1)S(1)}, bf16[256,512]{1,0:T(8,128)(2,1)S(1)}, u32[]{:S(2)}, u32[]{:S(2)}) collective-permute-start(bf16[256,512]{1,0:T(8,128)(2,1)S(1)} %get-tuple-element.193), channel_id=1, source_target_pairs={{8,0},{9,1},{10,2},{11,3},{12,4},{13,5},{14,6},{15,7}} | collective-permute-start | bytes 786440 | tf_op jit(solution)/shard_map/ppermute | solution.py:455
  76.5 8.8 %collective-permute-start.26 = (bf16[2,64,1024]{2,1,0:T(8,128)(2,1)S(1)}, bf16[2,64,1024]{2,1,0:T(8,128)(2,1)S(1)}, u32[]{:S(2)}, u32[]{:S(2)}) collective-permute-start(bf16[2,64,1024]{2,1,0:T(8,128)(2,1)S(1)} %get-tuple-element.209.refs_6_), channel_id=1, source_target_pairs={{0,2},{2,4},{4,6},{6,7},{7,5},{5,3},{3,1},{1,0},{8,10},{10,12},{12... | collective-permute-start | bytes 786440 | tf_op jit(solution)/shard_map/ppermute | solution.py:404
  78.2 8.5 %collective-permute-start.27 = (bf16[2,64,1024]{2,1,0:T(8,128)(2,1)S(1)}, bf16[2,64,1024]{2,1,0:T(8,128)(2,1)S(1)}, u32[]{:S(2)}, u32[]{:S(2)}) collective-permute-start(bf16[2,64,1024]{2,1,0:T(8,128)(2,1)S(1)} %get-tuple-element.212), channel_id=1, source_target_pairs={{2,0},{4,2},{6,4},{7,6},{5,7},{3,5},{1,3},{0,1},{10,8},{12,10},{14... | collective-permute-start | bytes 786440 | tf_op jit(solution)/shard_map/ppermute | solution.py:404
  80.8 10.3 %collective-permute-start.30 = (bf16[2,64,1024]{2,1,0:T(8,128)(2,1)S(1)}, bf16[2,64,1024]{2,1,0:T(8,128)(2,1)S(1)}, u32[]{:S(2)}, u32[]{:S(2)}) collective-permute-start(bf16[2,64,1024]{2,1,0:T(8,128)(2,1)S(1)} %get-tuple-element.219), channel_id=1, source_target_pairs={{0,2},{2,4},{4,6},{6,7},{7,5},{5,3},{3,1},{1,0},{8,10},{10,12},{12... | collective-permute-start | bytes 786440 | tf_op jit(solution)/shard_map/ppermute | solution.py:404
  82.5 9.8 %collective-permute-start.31 = (bf16[2,64,1024]{2,1,0:T(8,128)(2,1)S(1)}, bf16[2,64,1024]{2,1,0:T(8,128)(2,1)S(1)}, u32[]{:S(2)}, u32[]{:S(2)}) collective-permute-start(bf16[2,64,1024]{2,1,0:T(8,128)(2,1)S(1)} %get-tuple-element.220), channel_id=1, source_target_pairs={{2,0},{4,2},{6,4},{7,6},{5,7},{3,5},{1,3},{0,1},{10,8},{12,10},{14... | collective-permute-start | bytes 786440 | tf_op jit(solution)/shard_map/ppermute | solution.py:404
  86.8 9.7 %collective-permute-start.28 = (bf16[2,64,1024]{2,1,0:T(8,128)(2,1)S(1)}, bf16[2,64,1024]{2,1,0:T(8,128)(2,1)S(1)}, u32[]{:S(2)}, u32[]{:S(2)}) collective-permute-start(bf16[2,64,1024]{2,1,0:T(8,128)(2,1)S(1)} %get-tuple-element.213.refs_6_.refs_0_), channel_id=1, source_target_pairs={{0,2},{2,4},{4,6},{6,7},{7,5},{5,3},{3,1},{1,0},{8,10},{10,12},{12... | collective-permute-start | bytes 786440 | tf_op jit(solution)/shard_map/ppermute | solution.py:404
  87.8 10.1 %collective-permute-start.29 = (bf16[2,64,1024]{2,1,0:T(8,128)(2,1)S(1)}, bf16[2,64,1024]{2,1,0:T(8,128)(2,1)S(1)}, u32[]{:S(2)}, u32[]{:S(2)}) collective-permute-start(bf16[2,64,1024]{2,1,0:T(8,128)(2,1)S(1)} %get-tuple-element.216), channel_id=1, source_target_pairs={{2,0},{4,2},{6,4},{7,6},{5,7},{3,5},{1,3},{0,1},{10,8},{12,10},{14... | collective-permute-start | bytes 786440 | tf_op jit(solution)/shard_map/ppermute | solution.py:404
  92.4 9.9 %collective-permute-start.34 = (bf16[2,64,1024]{2,1,0:T(8,128)(2,1)S(1)}, bf16[2,64,1024]{2,1,0:T(8,128)(2,1)S(1)}, u32[]{:S(2)}, u32[]{:S(2)}) collective-permute-start(bf16[2,64,1024]{2,1,0:T(8,128)(2,1)S(1)} %get-tuple-element.221.refs_0_), channel_id=1, source_target_pairs={{0,2},{2,4},{4,6},{6,7},{7,5},{5,3},{3,1},{1,0},{8,10},{10,12},{12... | collective-permute-start | bytes 786440 | tf_op jit(solution)/shard_map/ppermute | solution.py:404
  93.4 10.1 %collective-permute-start.35 = (bf16[2,64,1024]{2,1,0:T(8,128)(2,1)S(1)}, bf16[2,64,1024]{2,1,0:T(8,128)(2,1)S(1)}, u32[]{:S(2)}, u32[]{:S(2)}) collective-permute-start(bf16[2,64,1024]{2,1,0:T(8,128)(2,1)S(1)} %get-tuple-element.228), channel_id=1, source_target_pairs={{2,0},{4,2},{6,4},{7,6},{5,7},{3,5},{1,3},{0,1},{10,8},{12,10},{14... | collective-permute-start | bytes 786440 | tf_op jit(solution)/shard_map/ppermute | solution.py:404
  98.1 7.8 %collective-permute-start.32 = (bf16[2,64,1024]{2,1,0:T(8,128)(2,1)S(1)}, bf16[2,64,1024]{2,1,0:T(8,128)(2,1)S(1)}, u32[]{:S(2)}, u32[]{:S(2)}) collective-permute-start(bf16[2,64,1024]{2,1,0:T(8,128)(2,1)S(1)} %get-tuple-element.222.refs_6_.refs_0_), channel_id=1, source_target_pairs={{0,2},{2,4},{4,6},{6,7},{7,5},{5,3},{3,1},{1,0},{8,10},{10,12},{12... | collective-permute-start | bytes 786440 | tf_op jit(solution)/shard_map/ppermute | solution.py:404
  99.0 10.1 %collective-permute-start.33 = (bf16[2,64,1024]{2,1,0:T(8,128)(2,1)S(1)}, bf16[2,64,1024]{2,1,0:T(8,128)(2,1)S(1)}, u32[]{:S(2)}, u32[]{:S(2)}) collective-permute-start(bf16[2,64,1024]{2,1,0:T(8,128)(2,1)S(1)} %get-tuple-element.225), channel_id=1, source_target_pairs={{2,0},{4,2},{6,4},{7,6},{5,7},{3,5},{1,3},{0,1},{10,8},{12,10},{14... | collective-permute-start | bytes 786440 | tf_op jit(solution)/shard_map/ppermute | solution.py:404
  103.7 11.4 %collective-permute-start.39 = (bf16[2,64,1024]{2,1,0:T(8,128)(2,1)S(1)}, bf16[2,64,1024]{2,1,0:T(8,128)(2,1)S(1)}, u32[]{:S(2)}, u32[]{:S(2)}) collective-permute-start(bf16[2,64,1024]{2,1,0:T(8,128)(2,1)S(1)} %get-tuple-element.234), channel_id=1, source_target_pairs={{2,0},{4,2},{6,4},{7,6},{5,7},{3,5},{1,3},{0,1},{10,8},{12,10},{14... | collective-permute-start | bytes 786440 | tf_op jit(solution)/shard_map/ppermute | solution.py:404
  109.3 7.3 %collective-permute-start.38 = (bf16[2,64,1024]{2,1,0:T(8,128)(2,1)S(1)}, bf16[2,64,1024]{2,1,0:T(8,128)(2,1)S(1)}, u32[]{:S(2)}, u32[]{:S(2)}) collective-permute-start(bf16[2,64,1024]{2,1,0:T(8,128)(2,1)S(1)} %get-tuple-element.230.refs_6_), channel_id=1, source_target_pairs={{0,2},{2,4},{4,6},{6,7},{7,5},{5,3},{3,1},{1,0},{8,10},{10,12},{12... | collective-permute-start | bytes 786440 | tf_op jit(solution)/shard_map/ppermute | solution.py:404
  110.3 9.2 %collective-permute-start.36 = (bf16[2,64,1024]{2,1,0:T(8,128)(2,1)S(1)}, bf16[2,64,1024]{2,1,0:T(8,128)(2,1)S(1)}, u32[]{:S(2)}, u32[]{:S(2)}) collective-permute-start(bf16[2,64,1024]{2,1,0:T(8,128)(2,1)S(1)} %get-tuple-element.229.refs_0_), channel_id=1, source_target_pairs={{0,2},{2,4},{4,6},{6,7},{7,5},{5,3},{3,1},{1,0},{8,10},{10,12},{12... | collective-permute-start | bytes 786440 | tf_op jit(solution)/shard_map/ppermute | solution.py:404
  111.2 8.3 %collective-permute-start.37 = (bf16[2,64,1024]{2,1,0:T(8,128)(2,1)S(1)}, bf16[2,64,1024]{2,1,0:T(8,128)(2,1)S(1)}, u32[]{:S(2)}, u32[]{:S(2)}) collective-permute-start(bf16[2,64,1024]{2,1,0:T(8,128)(2,1)S(1)} %get-tuple-element.232), channel_id=1, source_target_pairs={{2,0},{4,2},{6,4},{7,6},{5,7},{3,5},{1,3},{0,1},{10,8},{12,10},{14... | collective-permute-start | bytes 786440 | tf_op jit(solution)/shard_map/ppermute | solution.py:404
  (11 other events, 44.3 us)
